TPU v7x, 256 devices: a whole 4x4x8 slice. The times are simulated.
256 devices in a mesh: fsdp: 32 (over z, y), tensor: 8 (over x, core).
Axes of the slice: x: 4, y: 4, z: 8, core: 2. Of those that a mesh axis runs over, the one named last changes fastest.
Arguments:
- mom_square: float32 [2, 8192, 8192], P(None, 'fsdp', 'tensor'), may hold values from -6 to 6
- grad_square: bfloat16 [2, 8192, 8192], P(None, 'fsdp', 'tensor'), may hold values from -6 to 6
- basis_square: float32 [2, 8192, 256], P(None, 'tensor'), may hold values from -0.0625 to 0.0625
- mom_narrow: float32 [2, 8192, 1024], P(None, 'fsdp', 'tensor'), may hold values from -6 to 6
- grad_narrow: bfloat16 [2, 8192, 1024], P(None, 'fsdp', 'tensor'), may hold values from -6 to 6
- basis_narrow: float32 [2, 1024, 256], P(None, 'tensor'), may hold values from -0.1875 to 0.1875
Outputs:
- new_mom_square: float32 [2, 8192, 8192], P(None, 'fsdp', 'tensor')
- update_square: bfloat16 [2, 8192, 8192], P(None, 'fsdp', 'tensor')
- new_basis_square: float32 [2, 8192, 256], P(None, 'tensor')
- new_mom_narrow: float32 [2, 8192, 1024], P(None, 'fsdp', 'tensor')
- update_narrow: bfloat16 [2, 8192, 1024], P(None, 'fsdp', 'tensor')
- new_basis_narrow: float32 [2, 1024, 256], P(None, 'tensor')
All inputs are finite; a program needn't handle non-finite values.
Results may differ from a plain program's by a relative error of at most 0.001.
Values sent between devices are 32-bit elements; how exact they have to be, the bound alone decides.
No kernel may reach another device: no remote copies, remote signals or barrier semaphores. Data moves between devices by JAX's collectives and lax.ppermute only.
A program may use at most 64 MiB of HBM per device.

v0:
```python
import jax
import jax.numpy as jnp
from jax import lax
from jax.sharding import PartitionSpec as P

D = 8192
KVW = 1024
RANK = 256


HIGH = lax.Precision.HIGHEST


def project(buffer, basis):
    return jnp.einsum("kmc,kcr->kmr", buffer, basis, precision=HIGH)


def gram_matrix(left):
    return jnp.einsum("kmr,kms->krs", left, left, precision=HIGH)


def solve_right(gram, matrix):
    lower = jnp.linalg.cholesky(gram)
    solved = jax.scipy.linalg.solve_triangular(lower, jnp.swapaxes(matrix, 1, 2), lower=True)
    return jnp.swapaxes(solved, 1, 2)


def back_project(buffer, ortho):
    return jnp.einsum("kmc,kmr->kcr", buffer, ortho, precision=HIGH)


def column_squares(right):
    return jnp.sum(right * right, axis=1)


def finish(buffer, ortho, right, squares, columns):
    new_momentum = buffer - (1.0 - 0.95) * jnp.einsum("kmr,kcr->kmc", ortho, right, precision=HIGH)
    new_basis = right * lax.rsqrt(squares + 1e-06)[:, None, :]
    factor = (D * columns / RANK) ** 0.5
    update = (factor * jnp.einsum("kmr,kcr->kmc", ortho, new_basis, precision=HIGH)).astype(
        jnp.bfloat16
    )
    return (new_momentum, update, new_basis)


def local(mom_square, grad_square, basis_square, mom_narrow, grad_narrow, basis_narrow):
    square_buffer = mom_square + grad_square.astype(jnp.float32)
    narrow_buffer = mom_narrow + grad_narrow.astype(jnp.float32)
    square_left, narrow_left = lax.psum(
        (project(square_buffer, basis_square), project(narrow_buffer, basis_narrow)), "tensor"
    )
    square_gram, narrow_gram = lax.psum(
        (gram_matrix(square_left), gram_matrix(narrow_left)), "fsdp"
    )
    square_ortho = solve_right(square_gram, square_left)
    narrow_ortho = solve_right(narrow_gram, narrow_left)
    square_right, narrow_right = lax.psum(
        (back_project(square_buffer, square_ortho), back_project(narrow_buffer, narrow_ortho)),
        "fsdp",
    )
    square_norms, narrow_norms = lax.psum(
        (column_squares(square_right), column_squares(narrow_right)), "tensor"
    )
    square_mom, square_update, square_basis = finish(
        square_buffer, square_ortho, square_right, square_norms, D
    )
    narrow_mom, narrow_update, narrow_basis = finish(
        narrow_buffer, narrow_ortho, narrow_right, narrow_norms, KVW
    )
    return (square_mom, square_update, square_basis, narrow_mom, narrow_update, narrow_basis)


def solution(mesh):
    in_specs = (
        P(None, "fsdp", "tensor"),
        P(None, "fsdp", "tensor"),
        P(None, "tensor", None),
        P(None, "fsdp", "tensor"),
        P(None, "fsdp", "tensor"),
        P(None, "tensor", None),
    )
    out_specs = (
        P(None, "fsdp", "tensor"),
        P(None, "fsdp", "tensor"),
        P(None, "tensor", None),
        P(None, "fsdp", "tensor"),
        P(None, "fsdp", "tensor"),
        P(None, "tensor", None),
    )
    return jax.shard_map(local, mesh=mesh, in_specs=in_specs, out_specs=out_specs, check_vma=False)
```

profile of v0, /device:TPU:1, one launch (start us, length us, event | category | flops | bytes accessed | tf_op | source)
XLA Modules:
  0.0 695.3 jit_solution(3549332517630886562)
XLA Ops:
  7.3 1.5 copy-done
  8.8 4.9 fusion.3
  13.6 1.4 fusion.21
  15.1 69.6 %all-reduce.13.cloned.1.call-done = (f32[2,256,256]{2,1,0:T(8,128)}, f32[2,256,256]{2,1,0:T(8,128)}) async-done(((f32[2,256,256]{2,1,0:T(8,128)}, f32[2,256,256]{2,1,0:T(8,128)}), (f32[2,256,256]{2,1,0:T(8,128)}, f32[2,256,256]{2,1,0:T(8,128)})) %all-reduce.13.cloned.1.call-update) | async-done | bytes 1048592 | tf_op jit(solution)/shard_map/psum | solution.py:49
  84.7 3.1 fusion.30
  87.8 1.9 fusion.31
  89.7 0.6 iota_multiply_fusion
  90.3 0.6 iota_compare_fusion.1
  90.9 0.7 iota_compare_fusion
  91.6 144.6 %all-reduce.11.cloned.1.call-done = (f32[2,256,256]{1,2,0:T(8,128)}, f32[2,256,256]{1,2,0:T(8,128)}) async-done(((f32[2,256,256]{1,2,0:T(8,128)}, f32[2,256,256]{1,2,0:T(8,128)}), (f32[2,256,256]{1,2,0:T(8,128)}, f32[2,256,256]{1,2,0:T(8,128)})) %all-reduce.11.cloned.1.call-update) | async-done | bytes 1048592 | tf_op jit(solution)/shard_map/psum | solution.py:52
  236.2 2.1 copy.40
  238.3 2.0 copy.53
  240.4 2.1 fusion.4
  242.5 0.8 copy-done.18
  243.3 23.6 %custom-call.21 = f32[2,128,128]{2,1,0:T(8,128)S(1)} custom-call(f32[2,128,128]{2,1,0:T(8,128)S(1)} %cholesky.201), custom_call_target="Cholesky" | custom-call | tf_op jit(solution)/shard_map/jit(cholesky)/cholesky | solution.py:23
  266.9 0.9 cholesky.198
  267.9 23.5 %custom-call.17 = f32[2,128,128]{2,1,0:T(8,128)S(1)} custom-call(f32[2,128,128]{2,1,0:T(8,128)S(1)} %cholesky.198), custom_call_target="Cholesky" | custom-call | tf_op jit(solution)/shard_map/jit(cholesky)/cholesky | solution.py:23
  291.3 0.7 select_bitcast_fusion
  292.1 20.3 %custom-call.22 = f32[2,1,128,128]{2,3,1,0:T(8,128)} custom-call(f32[2,1,128,128]{3,2,1,0:T(8,128)S(1)} %get-tuple-element.60), custom_call_target="InvertDiagBlocksLowerTriangular" | custom-call | tf_op jit(solution)/shard_map/jit(cholesky)/cholesky | solution.py:23
  312.4 20.1 %custom-call.18 = f32[2,1,128,128]{2,3,1,0:T(8,128)S(1)} custom-call(f32[2,1,128,128]{3,2,1,0:T(8,128)S(1)} %get-tuple-element.61), custom_call_target="InvertDiagBlocksLowerTriangular" | custom-call | tf_op jit(solution)/shard_map/jit(cholesky)/cholesky | solution.py:23
  332.5 1.2 constant_dynamic-update-slice_fusion.3
  333.7 1.3 convolution_subtract_fusion.3
  335.0 24.1 %custom-call.19 = f32[2,128,128]{2,1,0:T(8,128)} custom-call(f32[2,128,128]{2,1,0:T(8,128)S(1)} %convolution_subtract_fusion.3), custom_call_target="Cholesky" | custom-call | tf_op jit(solution)/shard_map/jit(cholesky)/cholesky | solution.py:23
  359.1 1.2 constant_dynamic-update-slice_fusion.1
  360.3 2.0 convolution_subtract_fusion.2
  362.3 24.9 %custom-call.23 = f32[2,128,128]{2,1,0:T(8,128)} custom-call(f32[2,128,128]{2,1,0:T(8,128)} %convolution_subtract_fusion.2), custom_call_target="Cholesky" | custom-call | tf_op jit(solution)/shard_map/jit(cholesky)/cholesky | solution.py:23
  387.2 1.0 select_reduce_fusion
  388.2 0.1 compare_reduce_fusion
  388.4 0.1 compare_reduce_fusion.2
  388.5 0.1 compare_reduce_fusion.1
  388.6 0.1 compare_reduce_fusion.3
  388.7 0.3 copy-done.17
  389.0 2.0 select_select_fusion
  391.1 4.0 while.5
  391.2 0.6 fusion.53
  391.8 1.4 bitcast_dynamic-update-slice_fusion.5
  393.2 0.6 fusion.53
  393.8 1.4 bitcast_dynamic-update-slice_fusion.5
  395.2 40.0 %custom-call.24 = f32[2,2,128,128]{2,3,1,0:T(8,128)} custom-call(f32[2,2,128,128]{3,2,1,0:T(8,128)S(1)} %bitcast.89), custom_call_target="InvertDiagBlocksLowerTriangular" | custom-call | tf_op jit(solution)/shard_map/jit(_solve_triangular)/vmap()/triangular_solve | solution.py:24
  435.2 5.9 while.4
  435.2 0.6 fusion.52
  435.8 2.4 bitcast_dynamic-update-slice_fusion.4
  438.2 0.6 fusion.52
  438.8 2.3 bitcast_dynamic-update-slice_fusion.4
  441.1 40.1 %custom-call.20 = f32[2,2,128,128]{2,3,1,0:T(8,128)} custom-call(f32[2,2,128,128]{3,2,1,0:T(8,128)S(1)} %bitcast.88), custom_call_target="InvertDiagBlocksLowerTriangular" | custom-call | tf_op jit(solution)/shard_map/jit(_solve_triangular)/vmap()/triangular_solve | solution.py:24
  481.2 1.4 fusion.9
  482.6 1.5 convolution_subtract_fusion.1
  484.2 1.5 fusion.16
  485.7 1.5 fusion.7
  487.2 1.7 convolution_subtract_fusion
  488.9 0.4 fusion.12
  489.4 0.7 copy-done.11
  490.0 1.4 fusion.6
  491.5 4.8 fusion.2
  496.3 153.8 %all-reduce.9.cloned.1.call-done = (f32[2,1024,256]{2,1,0:T(8,128)}, f32[2,128,256]{2,1,0:T(8,128)}) async-done(((f32[2,1024,256]{2,1,0:T(8,128)}, f32[2,128,256]{2,1,0:T(8,128)}), (f32[2,1024,256]{2,1,0:T(8,128)}, f32[2,128,256]{2,1,0:T(8,128)})) %all-reduce.9.cloned.1.call-update) | async-done | bytes 2359312 | tf_op jit(solution)/shard_map/psum | solution.py:57
  650.1 1.1 multiply_reduce_fusion.1
  651.2 2.9 fusion
  654.2 1.8 multiply_reduce_fusion
  656.0 6.5 multiply_subtract_fusion
  662.4 15.9 %all-reduce.3 = (f32[2,256]{1,0:T(2,128)S(1)}, f32[2,256]{1,0:T(2,128)S(1)}) all-reduce(f32[2,256]{1,0:T(2,128)S(1)} %multiply_reduce_fusion, f32[2,256]{1,0:T(2,128)S(1)} %multiply_reduce_fusion.1), channel_id=1, replica_groups=mesh['fsdp'=32,'tensor'=8] {'tensor'}, use_global_device_ids=true, to_apply=%region_8.0 | all-reduce | flops 1024 | bytes 8192 | tf_op jit(solution)/shard_map/psum | solution.py:61
  678.4 1.0 broadcast_multiply_fusion.1
  679.4 2.8 fusion.1
  682.2 1.8 broadcast_multiply_fusion
  684.0 4.5 multiply_convert_fusion
  (65 shorter events, 0.5 us)
Async XLA Ops:
  7.2 1.6 copy-start
  7.2 6.4 copy-start.19
  7.2 6.4 copy-start.13
  7.2 6.4 copy-start.22
  7.2 77.5 %all-reduce.13.cloned.1.call-start = ((), (), s32[]{:S(2)}) async-start(), calls=%async_computation.2 | async-start | bytes 2097152 | tf_op jit(solution)/shard_map/psum | solution.py:49
  15.0 221.2 %all-reduce.11.cloned.1.call-start = ((), (), s32[]{:S(2)}) async-start(), calls=%async_computation.1 | async-start | bytes 2097152 | tf_op jit(solution)/shard_map/psum | solution.py:52
  84.7 3.1 copy-start.6
  89.7 560.4 %all-reduce.9.cloned.1.call-start = ((), (), s32[]{:S(2)}) async-start(), calls=%async_computation | async-start | bytes 4718592 | tf_op jit(solution)/shard_map/psum | solution.py:57
  236.2 4.2 copy-start.15
  236.2 4.2 copy-start.16
  242.5 0.8 copy-start.18
  387.2 3.9 copy-start.23
  388.2 0.8 copy-start.17
  391.1 90.2 %copy-start.7 = (f32[2,256,256]{2,1,0:T(8,128)S(1)}, f32[2,256,256]{2,1,0:T(8,128)}, u32[]{:S(2)}) copy-start(f32[2,256,256]{2,1,0:T(8,128)} %get-tuple-element.50) | copy-start | bytes 1572868
  395.2 87.4 %copy-start.12 = (f32[2,256,256]{2,1,0:T(8,128)}, f32[2,256,256]{2,1,0:T(8,128)S(1)}, u32[]{:S(2)}) copy-start(f32[2,256,256]{2,1,0:T(8,128)S(1)} %get-tuple-element.175) | copy-start | bytes 1572868
  481.2 4.5 copy-start.21
  481.2 8.8 %copy-start.14 = (f32[2,256,128]{2,1,0:T(8,128)S(1)}, f32[2,256,128]{2,1,0:T(8,128)}, u32[]{:S(2)}) copy-start(f32[2,256,128]{2,1,0:T(8,128)} %param.12) | copy-start | bytes 786436
  484.2 7.3 %copy-start.2 = (f32[2,256,1024]{2,1,0:T(8,128)S(1)}, f32[2,256,1024]{2,1,0:T(8,128)}, u32[]{:S(2)}) copy-start(f32[2,256,1024]{2,1,0:T(8,128)} %param.9) | copy-start | bytes 6291460
  484.2 7.3 %copy-start.3 = (bf16[2,256,1024]{2,1,0:T(8,128)(2,1)S(1)}, bf16[2,256,1024]{2,1,0:T(8,128)(2,1)}, u32[]{:S(2)}) copy-start(bf16[2,256,1024]{2,1,0:T(8,128)(2,1)} %param.10) | copy-start | bytes 3145732
  485.7 5.8 copy-start.8
  487.2 2.2 copy-start.5
  489.3 0.7 copy-start.11
  650.1 5.9 copy-start.1
  650.1 5.9 copy-start.9
  679.4 4.6 copy-start.20
  682.2 1.8 copy-start.10
  684.0 4.5 copy-start.4
Sparse Core Ops, SparseCore 0:
  15.2 69.4 all-reduce.12
  89.8 146.3 all-reduce.10
  496.4 153.6 all-reduce.8
where the time goes:
time: 701 us; the launch traced here: 695 us
  waiting for transfers between devices  368 us (52%)
  other arithmetic  230 us (33%)
  matrix products  47.8 us (7%)
  local copies, waits for them, and re-layouts  18.5 us (3%)
  blocking collectives  15.9 us (2%)
  between operations  14.3 us (2%)
    psum x1, waiting for transfers between devices, local(): lax.psum((back_project(square_buffer, square_ortho), back_project(narrow_...  154 us
    psum x1, waiting for transfers between devices, local(): lax.psum((gram_matrix(square_left), gram_matrix(narrow_left)), 'fsdp')  145 us
    another operation x16, other arithmetic, solve_right(): lower = jnp.linalg.cholesky(gram)  139 us
    another operation x5, other arithmetic, solve_right(): jax.scipy.linalg.solve_triangular(lower, jnp.swapaxes(matrix, 1, 2), lowe...  83.3 us
    psum x1, waiting for transfers between devices, local(): lax.psum((project(square_buffer, basis_square), project(narrow_buffer, ba...  69.6 us
    psum x1, blocking collectives, local(): lax.psum((column_squares(square_right), column_squares(narrow_right)), 't...  15.9 us
  transfers between devices with their start and end apart: 3, of which 3 were waited for; matrix products, arithmetic and copies ran while one was open for 0% of the time, Pallas kernels for 0%

commit v1 on v0

v1 whole, which is shorter than its diff:
```python
import functools

import jax
import jax.numpy as jnp
from jax import lax
from jax.experimental import pallas as pl
from jax.experimental.pallas import tpu as pltpu
from jax.sharding import Mesh, PartitionSpec as P

D = 8192
KVW = 1024
RANK = 256

F32 = jnp.float32
BF16 = jnp.bfloat16
AXES = ("zh", "zl", "yh", "yl", "x", "core")
ROWS = ("zh", "zl", "yh", "yl")
COLS = ("x", "core")
FAR = ("zh", "yh")
NN = (((1,), (0,)), ((), ()))
NT = (((1,), (1,)), ((), ()))
TN = (((0,), (0,)), ((), ()))
SQ, NA, GR = 32, 8, 8
CHUNK = 2 * SQ + NA


def split(value):
    high = value.astype(BF16)
    return high, (value - high.astype(F32)).astype(BF16)


def dot3(left, right, dims):
    (lh, ll), (rh, rl) = left, right
    dot = functools.partial(lax.dot_general, dimension_numbers=dims, preferred_element_type=F32)
    return dot(lh, rh) + (dot(lh, rl) + dot(ll, rh))


def call(kernel, outs, operands, scratch=(), name=None):
    vmem = pl.BlockSpec(memory_space=pltpu.VMEM)
    return pl.pallas_call(
        kernel,
        out_shape=[jax.ShapeDtypeStruct(s, d) for s, d in outs],
        in_specs=[pl.BlockSpec(memory_space=pltpu.SMEM)] + [vmem] * (len(operands) - 1),
        out_specs=[vmem] * len(outs),
        scratch_shapes=list(scratch),
        compiler_params=pltpu.CompilerParams(vmem_limit_bytes=50 * 2**20),
        name=name,
    )(*operands)


def project_kernel(place, ms, gs, qs, mn, gn, qn, mine, theirs, left):
    core = place[0]
    for k in range(4):
        m, g, q = (ms, gs, qs) if k < 2 else (mn, gn, qn)
        buffer = split(m[k % 2] + g[k % 2].astype(F32))
        left[k] = dot3(buffer, split(q[k % 2]), NN)
    for x in range(4):
        for k in range(4):
            mine[x, k] = left[k, pl.ds(pl.multiple_of(core * 128 + x * 32, 32), 32), :]
            theirs[x, k] = left[k, pl.ds(pl.multiple_of((1 - core) * 128 + x * 32, 32), 32), :]


def back_kernel(place, ms, gs, mn, gn, own_half, other_half, left, own, to_y, to_z, to_d, w):
    core, x, q = place[0], place[1], place[2]
    for i in range(4):
        for k in range(4):
            left[k, pl.ds(pl.multiple_of(core * 128 + i * 32, 32), 32), :] = own_half[i, k]
            left[k, pl.ds(pl.multiple_of((1 - core) * 128 + i * 32, 32), 32), :] = other_half[i, k]
    for k in range(2):
        buffer = split(ms[k] + gs[k].astype(F32))
        w[:, k * SQ:(k + 1) * SQ, :] = dot3(buffer, split(left[k]), TN).reshape(32, SQ, RANK)
    for k in range(2):
        buffer = split(mn[k] + gn[k].astype(F32))
        w[k * 16:(k + 1) * 16, 2 * SQ:CHUNK, :] = dot3(buffer, split(left[2 + k]), TN).reshape(16, NA, RANK)
    one = split(left[x])
    w[:, CHUNK:, :] = dot3(one, one, TN).reshape(32, GR, RANK)
    for j, out in enumerate((own, to_y, to_z, to_d)):
        out[...] = w[pl.ds((q ^ j) * 8, 8)]


def factor_kernel(place, g0, g1, g2, g3, out, w):
    q = place[2]
    n, nb = RANK, 64
    for j, g in enumerate((g0, g1, g2, g3)):
        w[pl.ds(pl.multiple_of((q ^ j) * 64, 64), 64), :n] = g[...].reshape(64, n)
    row = lax.broadcasted_iota(jnp.int32, (n, n), 0)
    col = lax.broadcasted_iota(jnp.int32, (n, n), 1)
    w[:, n:] = jnp.where(row == col, 1.0, 0.0)
    sub = lax.broadcasted_iota(jnp.int32, (nb, 1), 0)
    for o in range(0, n, nb):
        lo, hi = o // 128 * 128, n + (o + nb + 127) // 128 * 128
        r = w[o:o + nb, lo:hi]
        d = jnp.ones((nb, 1), F32)
        for i in range(nb):
            c = o + i - lo
            pivot = r[i:i + 1, c:c + 1]
            f = jnp.where(sub > i, r[:, c:c + 1] * (1.0 / pivot), 0.0)
            d = jnp.where(sub == i, pivot, d)
            r = r - f * r[i:i + 1, :]
        s = r * lax.rsqrt(d)
        out[o:o + nb, :hi - n] = s[:, n - lo:]
        if hi < 2 * n:
            out[o:o + nb, hi - n:] = jnp.zeros((nb, 2 * n - hi), F32)
        if o + nb < n:
            change = lax.dot_general(
                s[:, :n - lo], s, TN, precision=lax.Precision.HIGHEST, preferred_element_type=F32
            )
            w[o + nb:, lo:hi] = w[o + nb:, lo:hi] - change[o + nb - lo:]


def right_kernel(place, w0, w1, w2, w3, l0, l1, l2, l3, left, ms, gs, mn, gn,
                 right_s, right_n, ortho, squares, mom_s, mom_n, inv):
    x, q = place[1], place[2]
    for d, linv in enumerate((l0, l1, l2, l3)):
        inv[(x - d) & 3] = linv[...]
    for j, w in enumerate((w0, w1, w2, w3)):
        p = q ^ j
        for k in range(2):
            rows = split(w[:, k * SQ:(k + 1) * SQ, :].reshape(8 * SQ, RANK))
            right_s[k, pl.ds(pl.multiple_of(p * 8 * SQ, 8 * SQ), 8 * SQ), :] = dot3(rows, split(inv[k]), NT)
        rows = split(w[:, 2 * SQ:, :].reshape(8 * NA, RANK))
        right_n[p >> 1, pl.ds(pl.multiple_of((p & 1) * 8 * NA, 8 * NA), 8 * NA), :] = dot3(
            rows, split(inv[2 + (p >> 1)]), NT
        )
    squares[...] = jnp.zeros_like(squares)
    for k in range(4):
        m, g, right, mom = (ms, gs, right_s, mom_s) if k < 2 else (mn, gn, right_n, mom_n)
        r = right[k % 2]
        squares[k:k + 1, :] = jnp.sum(r * r, axis=0, keepdims=True)
        o = dot3(split(left[k]), split(inv[k]), NT)
        ortho[k] = o
        low_rank = lax.dot_general(o.astype(BF16), r.astype(BF16), NT, preferred_element_type=F32)
        mom[k % 2] = (m[k % 2] + g[k % 2].astype(F32)) - (1.0 - 0.95) * low_rank


def update_kernel(place, squares, right_s, right_n, ortho, up_s, basis_s, up_n, basis_n):
    scale = lax.rsqrt(jnp.sum(squares[...], axis=0) + 1e-06)
    for k in range(4):
        right, up, basis, columns = (right_s, up_s, basis_s, D) if k < 2 else (right_n, up_n, basis_n, KVW)
        s = scale[k:k + 1, :]
        r = right[k % 2]
        basis[k % 2] = r * s
        o = ortho[k] * (s * (D * columns / RANK) ** 0.5)
        up[k % 2] = dot3(split(o), split(r), NT).astype(BF16)


def partners():
    def pair(i, core, n):
        return i ^ 1 if core == 0 else (((i - 1) ^ 1) + 1) % n

    y_pairs, z_pairs, d_pairs = [], [], []
    for i in range(256):
        z, y, x, core = i // 32, i // 8 % 4, i // 2 % 4, i % 2
        z2, y2 = pair(z, core, 8), pair((y - core) % 4, 0, 4)
        y2 = (y2 + core) % 4
        at = lambda a, b: a * 32 + b * 8 + x * 2 + core
        y_pairs.append((i, at(z, y2)))
        z_pairs.append((i, at(z2, y)))
        d_pairs.append((i, at(z2, y2)))
    return y_pairs, z_pairs, d_pairs


def around_x(value):
    got = {0: value}
    for d in (2, 1, 3):
        got[d] = lax.ppermute(value, "x", [(i, (i + d) % 4) for i in range(4)])
    return [got[d] for d in range(4)]


def swap_core(value):
    return lax.ppermute(value, "core", [(0, 1), (1, 0)])


def local(mom_square, grad_square, basis_square, mom_narrow, grad_narrow, basis_narrow):
    q = lax.axis_index("zl") * 2 + lax.axis_index("yl")
    place = jnp.stack([lax.axis_index("core"), lax.axis_index("x"), q]).astype(jnp.int32)
    in_block = partners()

    mine, theirs = call(
        project_kernel,
        [((4, 4, 32, RANK), F32)] * 2,
        (place, mom_square, grad_square, basis_square, mom_narrow, grad_narrow, basis_narrow),
        [pltpu.VMEM((4, 256, RANK), F32)],
        name="project",
    )
    half = mine + swap_core(theirs)
    part = jnp.sum(lax.all_to_all(half, "x", 0, 0), axis=0)
    own_half = lax.all_to_all(jnp.broadcast_to(part[None], (4,) + part.shape), "x", 0, 0)
    other_half = swap_core(own_half)

    left, own, *send = call(
        back_kernel,
        [((4, 256, RANK), F32)] + [((8, CHUNK + GR, RANK), F32)] * 4,
        (place, mom_square, grad_square, mom_narrow, grad_narrow, own_half, other_half),
        [pltpu.VMEM((32, CHUNK + GR, RANK), F32)],
        name="back",
    )
    for value, pairs in zip(send, in_block):
        own = own + lax.ppermute(value, AXES, pairs)
    part = jnp.sum(lax.all_to_all(own, FAR, 0, 0), axis=0)
    own = lax.all_to_all(jnp.broadcast_to(part[None], (8,) + part.shape), FAR, 0, 0)
    gram = own[:, CHUNK:, :]
    grams = [gram] + [lax.ppermute(gram, AXES, pairs) for pairs in in_block]
    w = own[:, :CHUNK, :]
    ws = [w] + [lax.ppermute(w, AXES, pairs) for pairs in in_block]
    (inverse,) = call(
        factor_kernel,
        [((RANK, RANK), F32)],
        (place, *grams),
        [pltpu.VMEM((RANK, 2 * RANK), F32)],
        name="factor",
    )
    inverses = around_x(inverse)
    right_s, right_n, ortho, squares, new_mom_s, new_mom_n = call(
        right_kernel,
        [((2, 1024, RANK), F32), ((2, 128, RANK), F32), ((4, 256, RANK), F32), ((8, RANK), F32),
         (mom_square.shape, F32), (mom_narrow.shape, F32)],
        (place, *ws, *inverses, left, mom_square, grad_square, mom_narrow, grad_narrow),
        [pltpu.VMEM((4, RANK, RANK), F32)],
        name="right",
    )
    squares = lax.all_to_all(jnp.broadcast_to(squares[None], (8,) + squares.shape), COLS, 0, 0)
    up_s, basis_s, up_n, basis_n = call(
        update_kernel,
        [(mom_square.shape, BF16), (basis_square.shape, F32), (mom_narrow.shape, BF16), (basis_narrow.shape, F32)],
        (place, squares, right_s, right_n, ortho),
        name="update",
    )
    return new_mom_s, up_s, basis_s, new_mom_n, up_n, basis_n


def solution(mesh):
    fine = Mesh(mesh.devices.reshape(4, 2, 2, 2, 4, 2), AXES)
    matrix, factor = P(None, ROWS, COLS), P(None, COLS, None)
    return jax.shard_map(
        local,
        mesh=fine,
        in_specs=(matrix, matrix, factor) * 2,
        out_specs=(matrix, matrix, factor) * 2,
        check_vma=False,
    )
```

time: 701 us -> 190 us (0.27)
  waiting for transfers between devices: 368 us -> 31.5 us
  other arithmetic: 230 us -> 0.4 us
  blocking collectives: 15.9 us -> 80.6 us
  matrix products: 47.8 us -> 0 us
  Pallas kernels: 0 us -> 43.6 us
  starting transfers between devices: 0.12 us -> 26.1 us
  between operations: 14.3 us -> 0.76 us
  local copies, waits for them, and re-layouts: 18.5 us -> 7 us
    psum x3 -> x0, waiting for transfers between devices: 368 us -> none  [the longest x1 154 us: local(): lax.psum((back_project(square_buffer, square_ortho), back_project(narrow_...]
    another operation x21 -> x1, other arithmetic: 223 us -> 0.08 us  [local(): jnp.stack([lax.axis_index('core'), lax.axis_index('x'), q])]
    all_to_all x0 -> x5, blocking collectives: none -> 80.6 us  [the longest x1 26.2 us: local(): part = jnp.sum(lax.all_to_all(own, FAR, 0, 0), axis=0)]
    pallas_call x0 -> x5, Pallas kernels: none -> 43.6 us  [call(): pl.pallas_call(kernel, out_shape=[jax.ShapeDtypeStruct(s, d) for s, d in...]
    dot_general x10 -> x0, matrix products: 34.2 us -> none  [the longest x2 9.41 us: finish(): jnp.einsum('kmr,kcr->kmc', ortho, right, precision=HIGH)]
    ppermute x0 -> x14, waiting for transfers between devices: none -> 31.5 us  [the longest x3 14.7 us: local(): own = own + lax.ppermute(value, AXES, pairs)]
    ppermute x0 -> x14, starting transfers between devices: none -> 26.1 us  [the longest x3 7.38 us: local(): own = own + lax.ppermute(value, AXES, pairs)]
    psum x1 -> x0, blocking collectives: 15.9 us -> none  [local(): lax.psum((column_squares(square_right), column_squares(narrow_right)), 't...]
  transfers between devices with their start and end apart: 3 -> 14, of which waited for: 3 -> 8; matrix products, arithmetic and copies ran while one was open for 0% -> 0% of each run, Pallas kernels for 0% -> 13%
where the time goes in v1:
time: 190 us
  blocking collectives  80.6 us (42%)
  Pallas kernels  43.6 us (23%)
  waiting for transfers between devices  31.5 us (17%)
  starting transfers between devices  26.1 us (14%)
  local copies, waits for them, and re-layouts  7 us (4%)
    pallas_call x5, Pallas kernels, call(): pl.pallas_call(kernel, out_shape=[jax.ShapeDtypeStruct(s, d) for s, d in...  43.6 us
    all_to_all x1, blocking collectives, local(): part = jnp.sum(lax.all_to_all(own, FAR, 0, 0), axis=0)  26.2 us
    all_to_all x1, blocking collectives, local(): lax.all_to_all(jnp.broadcast_to(part[None], (8,) + part.shape), FAR, 0, 0)  21 us
    ppermute x3, waiting for transfers between devices, local(): own = own + lax.ppermute(value, AXES, pairs)  14.7 us
    ppermute x3, waiting for transfers between devices, around_x(): got[d] = lax.ppermute(value, 'x', [(i, (i + d) % 4) for i in range(4)])  13.7 us
    all_to_all x1, blocking collectives, local(): part = jnp.sum(lax.all_to_all(half, 'x', 0, 0), axis=0)  11.8 us
    all_to_all x1, blocking collectives, local(): lax.all_to_all(jnp.broadcast_to(squares[None], (8,) + squares.shape), COL...  11 us
    all_to_all x1, blocking collectives, local(): lax.all_to_all(jnp.broadcast_to(part[None], (4,) + part.shape), 'x', 0, 0)  10.7 us
  transfers between devices with their start and end apart: 14, of which 8 were waited for; matrix products, arithmetic and copies ran while one was open for 0% of the time, Pallas kernels for 13%

profile of v1, /device:TPU:1, one launch (start us, length us, event | category | flops | bytes accessed | tf_op | source)
XLA Modules:
  0.0 190.0 jit_solution(6809740503966412351)
XLA Ops:
  0.6 0.1 pad_add_fusion.place
  0.7 0.0 copy-start
  0.7 1.2 copy-done
  1.9 0.0 copy-start.1
  1.9 0.9 copy-done.1
  2.9 0.0 copy-start.4
  2.9 0.9 copy-done.4
  3.8 0.0 copy-start.7
  3.8 0.9 copy-done.7
  4.7 3.7 %project.1 = (f32[4,4,32,256]{3,2,1,0:T(8,128)S(1)}, f32[4,4,32,256]{3,2,1,0:T(8,128)S(1)}) custom-call(s32[3]{0:T(128)S(1)} %pad_add_fusion.place, f32[2,256,1024]{2,1,0:T(8,128)} %ms.5, bf16[2,256,1024]{2,1,0:T(8,128)(2,1)S(1)} %copy-done, f32[2,1024,256]{2,1,0:T(8,128)} %qs.1, f32[2,256,128]{2,1,0:T(8,128)S(1)} %copy-done.1, ...), custom_call_target="tpu_custom_call" | custom-call | tf_op jit(solution)/shard_map/project/pallas_call | solution.py:40
  8.4 3.3 %collective-permute-start = (f32[4,4,32,256]{3,2,1,0:T(8,128)S(1)}, f32[4,4,32,256]{3,2,1,0:T(8,128)S(1)}, u32[]{:S(2)}, u32[]{:S(2)}) collective-permute-start(f32[4,4,32,256]{3,2,1,0:T(8,128)S(1)} %get-tuple-element.24), channel_id=1, source_target_pairs={{0,1},{1,0},{2,3},{3,2},{4,5},{5,4},{6,7},{7,6},{8,9},{9,8},{10,11... | collective-permute-start | bytes 1572872 | tf_op jit(solution)/shard_map/ppermute | solution.py:171
  11.7 1.5 collective-permute-done
  13.3 0.1 add.16
  13.4 0.0 copy-start.2
  13.4 0.0 copy-start.5
  13.4 11.8 %all_to_all.25 = f32[4,4,32,256]{3,2,1,0:T(8,128)S(1)} all-to-all(f32[4,4,32,256]{3,2,1,0:T(8,128)S(1)} %add.16), channel_id=1, replica_groups=mesh['zh'=4,'zl'=2,'yh'=2,'yl'=2,'x'=4,'core'=2] {'x'}, dimensions={0} | all-to-all | bytes 1048576 | tf_op jit(solution)/shard_map/all_to_all | solution.py:187
  25.2 10.7 %all_to_all.26.own_half = f32[4,4,32,256]{3,2,1,0:T(8,128)S(1)} all-to-all(f32[4,4,32,256]{3,2,1,0:T(8,128)S(1)} %broadcast_in_dim.6), channel_id=1, replica_groups=mesh['zh'=4,'zl'=2,'yh'=2,'yl'=2,'x'=4,'core'=2] {'x'}, dimensions={0} | all-to-all | bytes 1048576 | tf_op jit(solution)/shard_map/all_to_all | solution.py:188
  36.0 2.1 %collective-permute-start.1 = (f32[4,4,32,256]{3,2,1,0:T(8,128)S(1)}, f32[4,4,32,256]{3,2,1,0:T(8,128)S(1)}, u32[]{:S(2)}, u32[]{:S(2)}) collective-permute-start(f32[4,4,32,256]{3,2,1,0:T(8,128)S(1)} %all_to_all.26.own_half), channel_id=1, source_target_pairs={{0,1},{1,0},{2,3},{3,2},{4,5},{5,4},{6,7},{7,6},{8,9},{9,8},{10,11... | collective-permute-start | bytes 1572872 | tf_op jit(solution)/shard_map/ppermute | solution.py:171
  38.1 1.5 collective-permute-done.1.other_half
  39.6 0.0 copy-done.2
  39.6 0.0 copy-done.5
  39.6 4.4 %back.1 = (f32[4,256,256]{2,1,0:T(8,128)}, f32[8,80,256]{2,1,0:T(8,128)S(1)}, f32[8,80,256]{2,1,0:T(8,128)S(1)}, f32[8,80,256]{2,1,0:T(8,128)S(1)}, f32[8,80,256]{2,1,0:T(8,128)S(1)}) custom-call(s32[3]{0:T(128)S(1)} %pad_add_fusion.place, f32[2,256,1024]{2,1,0:T(8,128)} %ms.5, bf16[2,256,1024]{2,1,0:T(8,128)(2,1)} %gs.5, f32[2,256,128]{2,1,0:T(8,128)S(1)} %copy-done.2, ...), custom_call_target="tpu_custom_call" | custom-call | tf_op jit(solution)/shard_map/back/pallas_call | solution.py:40
  44.0 1.8 collective-permute-start.2
  45.8 5.6 %collective-permute-start.3 = (f32[8,80,256]{2,1,0:T(8,128)S(1)}, f32[8,80,256]{2,1,0:T(8,128)S(1)}, u32[]{:S(2)}, u32[]{:S(2)}) collective-permute-start(f32[8,80,256]{2,1,0:T(8,128)S(1)} %get-tuple-element.27), channel_id=1, source_target_pairs={{0,32},{1,225},{2,34},{3,227},{4,36},{5,229},{6,38},{7,231},{8,40}... | collective-permute-start | bytes 1966088 | tf_op jit(solution)/shard_map/ppermute | solution.py:199
  51.4 0.0 collective-permute-start.4
  51.4 3.3 %collective-permute-done.2 = f32[8,80,256]{2,1,0:T(8,128)S(1)} collective-permute-done((f32[8,80,256]{2,1,0:T(8,128)S(1)}, f32[8,80,256]{2,1,0:T(8,128)S(1)}, u32[]{:S(2)}, u32[]{:S(2)}) %collective-permute-start.2) | collective-permute-done | bytes 655392 | tf_op jit(solution)/shard_map/ppermute | solution.py:199
  54.7 4.8 %collective-permute-done.3 = f32[8,80,256]{2,1,0:T(8,128)S(1)} collective-permute-done((f32[8,80,256]{2,1,0:T(8,128)S(1)}, f32[8,80,256]{2,1,0:T(8,128)S(1)}, u32[]{:S(2)}, u32[]{:S(2)}) %collective-permute-start.3) | collective-permute-done | bytes 655392 | tf_op jit(solution)/shard_map/ppermute | solution.py:199
  59.5 6.6 %collective-permute-done.4 = f32[8,80,256]{2,1,0:T(8,128)S(1)} collective-permute-done((f32[8,80,256]{2,1,0:T(8,128)S(1)}, f32[8,80,256]{2,1,0:T(8,128)S(1)}, u32[]{:S(2)}, u32[]{:S(2)}) %collective-permute-start.4) | collective-permute-done | bytes 655392 | tf_op jit(solution)/shard_map/ppermute | solution.py:199
  66.1 0.2 add_add_fusion
  66.3 26.2 %all_to_all.27 = f32[8,80,256]{2,1,0:T(8,128)S(1)} all-to-all(f32[8,80,256]{2,1,0:T(8,128)S(1)} %add_add_fusion), channel_id=1, replica_groups=mesh['zh'=4,'zl'=2,'yh'=2,'yl'=2,'x'=4,'core'=2] {'zh','yh'}, dimensions={0} | all-to-all | bytes 1310720 | tf_op jit(solution)/shard_map/all_to_all | solution.py:200
  92.6 21.0 %all_to_all.28 = f32[8,80,256]{2,1,0:T(8,128)S(1)} all-to-all(f32[8,80,256]{2,1,0:T(8,128)S(1)} %broadcast_in_dim.7), channel_id=1, replica_groups=mesh['zh'=4,'zl'=2,'yh'=2,'yl'=2,'x'=4,'core'=2] {'zh','yh'}, dimensions={0} | all-to-all | bytes 1310720 | tf_op jit(solution)/shard_map/all_to_all | solution.py:201
  113.6 0.0 collective-permute-start.10
  113.6 5.5 %collective-permute-start.9 = (f32[8,8,256]{2,1,0:T(8,128)S(1)}, f32[8,8,256]{2,1,0:T(8,128)S(1)}, u32[]{:S(2)}, u32[]{:S(2)}) collective-permute-start(f32[8,8,256]{2,1,0:T(8,128)S(1)} %slice.9.g0), channel_id=1, source_target_pairs={{0,32},{1,225},{2,34},{3,227},{4,36},{5,229},{6,38},{7,231},{8,40}... | collective-permute-start | bytes 196616 | tf_op jit(solution)/shard_map/ppermute | solution.py:203
  119.0 0.0 collective-permute-start.8
  119.1 2.5 %collective-permute-start.7 = (f32[8,72,256]{2,1,0:T(8,128)S(1)}, f32[8,72,256]{2,1,0:T(8,128)S(1)}, u32[]{:S(2)}, u32[]{:S(2)}) collective-permute-start(f32[8,72,256]{2,1,0:T(8,128)S(1)} %slice.8.w0), channel_id=1, source_target_pairs={{0,40},{1,249},{2,42},{3,251},{4,44},{5,253},{6,46},{7,255},{8,32}... | collective-permute-start | bytes 1769480 | tf_op jit(solution)/shard_map/ppermute | solution.py:205
  121.6 2.7 %collective-permute-start.6 = (f32[8,72,256]{2,1,0:T(8,128)S(1)}, f32[8,72,256]{2,1,0:T(8,128)S(1)}, u32[]{:S(2)}, u32[]{:S(2)}) collective-permute-start(f32[8,72,256]{2,1,0:T(8,128)S(1)} %slice.8.w0), channel_id=1, source_target_pairs={{0,32},{1,225},{2,34},{3,227},{4,36},{5,229},{6,38},{7,231},{8,40}... | collective-permute-start | bytes 1769480 | tf_op jit(solution)/shard_map/ppermute | solution.py:205
  124.3 0.0 collective-permute-done.10.g3
  124.3 0.0 collective-permute-start.5
  124.3 0.0 collective-permute-done.9.g2
  124.3 0.0 collective-permute-done.8.g1
  124.3 25.0 %factor.1.l0 = f32[256,256]{1,0:T(8,128)S(1)} custom-call(s32[3]{0:T(128)S(1)} %pad_add_fusion.place, f32[8,8,256]{2,1,0:T(8,128)S(1)} %slice.9.g0, f32[8,8,256]{2,1,0:T(8,128)S(1)} %collective-permute-done.8.g1, f32[8,8,256]{2,1,0:T(8,128)S(1)} %collective-permute-done.9.g2, f32[8,8,256]{2,1,0:T(8,128)S(1)} %collective-permute-done.10.g3), custom_call_target="tpu_custom_call" | custom-call | tf_op jit(solution)/shard_map/factor/pallas_call | solution.py:40
  149.3 1.0 collective-permute-start.13
  150.2 1.2 collective-permute-start.12
  151.4 6.0 %collective-permute-done.13.l3 = f32[256,256]{1,0:T(8,128)S(1)} collective-permute-done((f32[256,256]{1,0:T(8,128)S(1)}, f32[256,256]{1,0:T(8,128)S(1)}, u32[]{:S(2)}, u32[]{:S(2)}) %collective-permute-start.13) | collective-permute-done | bytes 262176 | tf_op jit(solution)/shard_map/ppermute | solution.py:166
  157.4 0.5 collective-permute-start.11
  157.9 1.7 collective-permute-done.12.l2
  159.6 6.0 %collective-permute-done.11.l1 = f32[256,256]{1,0:T(8,128)S(1)} collective-permute-done((f32[256,256]{1,0:T(8,128)S(1)}, f32[256,256]{1,0:T(8,128)S(1)}, u32[]{:S(2)}, u32[]{:S(2)}) %collective-permute-start.11) | collective-permute-done | bytes 262176 | tf_op jit(solution)/shard_map/ppermute | solution.py:166
  165.6 0.0 collective-permute-done.7.w3
  165.6 0.0 collective-permute-done.6.w2
  165.6 0.0 collective-permute-done.5.w1
  165.6 7.1 %right.1 = (f32[2,1024,256]{2,1,0:T(8,128)}, f32[2,128,256]{2,1,0:T(8,128)S(1)}, f32[4,256,256]{2,1,0:T(8,128)}, f32[8,256]{1,0:T(8,128)S(1)}, f32[2,256,1024]{2,1,0:T(8,128)}, /*index=5*/f32[2,256,128]{2,1,0:T(8,128)}) custom-call(s32[3]{0:T(128)S(1)} %pad_add_fusion.place, f32[8,72,256]{2,1,0:T(8,128)S(1)} %slice.8.w0, ...), custom_call_target="tpu_custom_call" | custom-call | tf_op jit(solution)/shard_map/right/pallas_call | solution.py:40
  172.7 11.0 %all_to_all.29.squares = f32[8,8,256]{2,1,0:T(8,128)S(1)} all-to-all(f32[8,8,256]{2,1,0:T(8,128)S(1)} %broadcast_in_dim.8), channel_id=1, replica_groups=mesh['zh'=4,'zl'=2,'yh'=2,'yl'=2,'x'=4,'core'=2] {'x','core'}, dimensions={0} | all-to-all | bytes 131072 | tf_op jit(solution)/shard_map/all_to_all | solution.py:222
  183.7 0.0 copy-start.3
  183.8 1.6 copy-done.3
  185.3 0.0 copy-start.6
  185.3 1.2 copy-done.6
  186.6 3.4 %update.1 = (bf16[2,256,1024]{2,1,0:T(8,128)(2,1)}, f32[2,1024,256]{2,1,0:T(8,128)}, bf16[2,256,128]{2,1,0:T(8,128)(2,1)}, f32[2,128,256]{2,1,0:T(8,128)}) custom-call(s32[3]{0:T(128)S(1)} %pad_add_fusion.place, f32[8,8,256]{2,1,0:T(8,128)S(1)} %all_to_all.29.squares, f32[2,1024,256]{2,1,0:T(8,128)S(1)} %copy-done.3, ...), custom_call_target="tpu_custom_call" | custom-call | tf_op jit(solution)/shard_map/update/pallas_call | solution.py:40
  (7 shorter events, 0.2 us)
Async XLA Ops:
  0.7 1.2 copy-start
  1.9 0.9 copy-start.1
  2.9 0.9 copy-start.4
  3.8 0.9 copy-start.7
  8.4 4.9 %collective-permute-start = (f32[4,4,32,256]{3,2,1,0:T(8,128)S(1)}, f32[4,4,32,256]{3,2,1,0:T(8,128)S(1)}, u32[]{:S(2)}, u32[]{:S(2)}) collective-permute-start(f32[4,4,32,256]{3,2,1,0:T(8,128)S(1)} %get-tuple-element.24), channel_id=1, source_target_pairs={{0,1},{1,0},{2,3},{3,2},{4,5},{5,4},{6,7},{7,6},{8,9},{9,8},{10,11... | collective-permute-start | bytes 1572872 | tf_op jit(solution)/shard_map/ppermute | solution.py:171
  13.4 26.2 %copy-start.2 = (f32[2,256,128]{2,1,0:T(8,128)S(1)}, f32[2,256,128]{2,1,0:T(8,128)}, u32[]{:S(2)}) copy-start(f32[2,256,128]{2,1,0:T(8,128)} %mn.5) | copy-start | bytes 786436
  13.4 26.2 %copy-start.5 = (bf16[2,256,128]{2,1,0:T(8,128)(2,1)S(1)}, bf16[2,256,128]{2,1,0:T(8,128)(2,1)}, u32[]{:S(2)}) copy-start(bf16[2,256,128]{2,1,0:T(8,128)(2,1)} %gn.5) | copy-start | bytes 393220
  36.0 3.7 %collective-permute-start.1 = (f32[4,4,32,256]{3,2,1,0:T(8,128)S(1)}, f32[4,4,32,256]{3,2,1,0:T(8,128)S(1)}, u32[]{:S(2)}, u32[]{:S(2)}) collective-permute-start(f32[4,4,32,256]{3,2,1,0:T(8,128)S(1)} %all_to_all.26.own_half), channel_id=1, source_target_pairs={{0,1},{1,0},{2,3},{3,2},{4,5},{5,4},{6,7},{7,6},{8,9},{9,8},{10,11... | collective-permute-start | bytes 1572872 | tf_op jit(solution)/shard_map/ppermute | solution.py:171
  44.0 10.6 %collective-permute-start.2 = (f32[8,80,256]{2,1,0:T(8,128)S(1)}, f32[8,80,256]{2,1,0:T(8,128)S(1)}, u32[]{:S(2)}, u32[]{:S(2)}) collective-permute-start(f32[8,80,256]{2,1,0:T(8,128)S(1)} %get-tuple-element.26), channel_id=1, source_target_pairs={{0,8},{1,25},{2,10},{3,27},{4,12},{5,29},{6,14},{7,31},{8,0},{9,17... | collective-permute-start | bytes 1966088 | tf_op jit(solution)/shard_map/ppermute | solution.py:199
  45.8 13.7 %collective-permute-start.3 = (f32[8,80,256]{2,1,0:T(8,128)S(1)}, f32[8,80,256]{2,1,0:T(8,128)S(1)}, u32[]{:S(2)}, u32[]{:S(2)}) collective-permute-start(f32[8,80,256]{2,1,0:T(8,128)S(1)} %get-tuple-element.27), channel_id=1, source_target_pairs={{0,32},{1,225},{2,34},{3,227},{4,36},{5,229},{6,38},{7,231},{8,40}... | collective-permute-start | bytes 1966088 | tf_op jit(solution)/shard_map/ppermute | solution.py:199
  51.4 14.7 %collective-permute-start.4 = (f32[8,80,256]{2,1,0:T(8,128)S(1)}, f32[8,80,256]{2,1,0:T(8,128)S(1)}, u32[]{:S(2)}, u32[]{:S(2)}) collective-permute-start(f32[8,80,256]{2,1,0:T(8,128)S(1)} %get-tuple-element.28), channel_id=1, source_target_pairs={{0,40},{1,249},{2,42},{3,251},{4,44},{5,253},{6,46},{7,255},{8,32}... | collective-permute-start | bytes 1966088 | tf_op jit(solution)/shard_map/ppermute | solution.py:199
  113.6 10.7 %collective-permute-start.10 = (f32[8,8,256]{2,1,0:T(8,128)S(1)}, f32[8,8,256]{2,1,0:T(8,128)S(1)}, u32[]{:S(2)}, u32[]{:S(2)}) collective-permute-start(f32[8,8,256]{2,1,0:T(8,128)S(1)} %slice.9.g0), channel_id=1, source_target_pairs={{0,40},{1,249},{2,42},{3,251},{4,44},{5,253},{6,46},{7,255},{8,32}... | collective-permute-start | bytes 196616 | tf_op jit(solution)/shard_map/ppermute | solution.py:203
  113.6 10.7 %collective-permute-start.9 = (f32[8,8,256]{2,1,0:T(8,128)S(1)}, f32[8,8,256]{2,1,0:T(8,128)S(1)}, u32[]{:S(2)}, u32[]{:S(2)}) collective-permute-start(f32[8,8,256]{2,1,0:T(8,128)S(1)} %slice.9.g0), channel_id=1, source_target_pairs={{0,32},{1,225},{2,34},{3,227},{4,36},{5,229},{6,38},{7,231},{8,40}... | collective-permute-start | bytes 196616 | tf_op jit(solution)/shard_map/ppermute | solution.py:203
  119.0 5.2 %collective-permute-start.8 = (f32[8,8,256]{2,1,0:T(8,128)S(1)}, f32[8,8,256]{2,1,0:T(8,128)S(1)}, u32[]{:S(2)}, u32[]{:S(2)}) collective-permute-start(f32[8,8,256]{2,1,0:T(8,128)S(1)} %slice.9.g0), channel_id=1, source_target_pairs={{0,8},{1,25},{2,10},{3,27},{4,12},{5,29},{6,14},{7,31},{8,0},{9,17... | collective-permute-start | bytes 196616 | tf_op jit(solution)/shard_map/ppermute | solution.py:203
  119.1 46.5 %collective-permute-start.7 = (f32[8,72,256]{2,1,0:T(8,128)S(1)}, f32[8,72,256]{2,1,0:T(8,128)S(1)}, u32[]{:S(2)}, u32[]{:S(2)}) collective-permute-start(f32[8,72,256]{2,1,0:T(8,128)S(1)} %slice.8.w0), channel_id=1, source_target_pairs={{0,40},{1,249},{2,42},{3,251},{4,44},{5,253},{6,46},{7,255},{8,32}... | collective-permute-start | bytes 1769480 | tf_op jit(solution)/shard_map/ppermute | solution.py:205
  121.6 44.0 %collective-permute-start.6 = (f32[8,72,256]{2,1,0:T(8,128)S(1)}, f32[8,72,256]{2,1,0:T(8,128)S(1)}, u32[]{:S(2)}, u32[]{:S(2)}) collective-permute-start(f32[8,72,256]{2,1,0:T(8,128)S(1)} %slice.8.w0), channel_id=1, source_target_pairs={{0,32},{1,225},{2,34},{3,227},{4,36},{5,229},{6,38},{7,231},{8,40}... | collective-permute-start | bytes 1769480 | tf_op jit(solution)/shard_map/ppermute | solution.py:205
  124.3 41.3 %collective-permute-start.5 = (f32[8,72,256]{2,1,0:T(8,128)S(1)}, f32[8,72,256]{2,1,0:T(8,128)S(1)}, u32[]{:S(2)}, u32[]{:S(2)}) collective-permute-start(f32[8,72,256]{2,1,0:T(8,128)S(1)} %slice.8.w0), channel_id=1, source_target_pairs={{0,8},{1,25},{2,10},{3,27},{4,12},{5,29},{6,14},{7,31},{8,0},{9,17... | collective-permute-start | bytes 1769480 | tf_op jit(solution)/shard_map/ppermute | solution.py:205
  149.3 8.2 %collective-permute-start.13 = (f32[256,256]{1,0:T(8,128)S(1)}, f32[256,256]{1,0:T(8,128)S(1)}, u32[]{:S(2)}, u32[]{:S(2)}) collective-permute-start(f32[256,256]{1,0:T(8,128)S(1)} %factor.1.l0), channel_id=1, source_target_pairs={{0,6},{2,0},{4,2},{6,4},{1,7},{3,1},{5,3},{7,5},{8,14},{10,8},{12,... | collective-permute-start | bytes 786440 | tf_op jit(solution)/shard_map/ppermute | solution.py:166
  150.2 9.4 %collective-permute-start.12 = (f32[256,256]{1,0:T(8,128)S(1)}, f32[256,256]{1,0:T(8,128)S(1)}, u32[]{:S(2)}, u32[]{:S(2)}) collective-permute-start(f32[256,256]{1,0:T(8,128)S(1)} %factor.1.l0), channel_id=1, source_target_pairs={{0,4},{2,6},{4,0},{6,2},{1,5},{3,7},{5,1},{7,3},{8,12},{10,14},{12... | collective-permute-start | bytes 786440 | tf_op jit(solution)/shard_map/ppermute | solution.py:166
  157.4 8.1 %collective-permute-start.11 = (f32[256,256]{1,0:T(8,128)S(1)}, f32[256,256]{1,0:T(8,128)S(1)}, u32[]{:S(2)}, u32[]{:S(2)}) collective-permute-start(f32[256,256]{1,0:T(8,128)S(1)} %factor.1.l0), channel_id=1, source_target_pairs={{0,2},{2,4},{4,6},{6,0},{1,3},{3,5},{5,7},{7,1},{8,10},{10,12},{12... | collective-permute-start | bytes 786440 | tf_op jit(solution)/shard_map/ppermute | solution.py:166
  183.7 1.6 copy-start.3
  185.3 1.2 copy-start.6

commit v2 on v1

--- a/solution.py
+++ b/solution.py
@@ -35,23 +35,39 @@
     return dot(lh, rh) + (dot(lh, rl) + dot(ll, rh))
 
 
-def call(kernel, outs, operands, scratch=(), name=None):
-    vmem = pl.BlockSpec(memory_space=pltpu.VMEM)
+def call(kernel, outs, operands, scratch=(), name=None, far_in=(), far_out=()):
+    vmem, hbm = pl.BlockSpec(memory_space=pltpu.VMEM), pl.BlockSpec(memory_space=pltpu.HBM)
     return pl.pallas_call(
         kernel,
         out_shape=[jax.ShapeDtypeStruct(s, d) for s, d in outs],
-        in_specs=[pl.BlockSpec(memory_space=pltpu.SMEM)] + [vmem] * (len(operands) - 1),
-        out_specs=[vmem] * len(outs),
+        in_specs=[pl.BlockSpec(memory_space=pltpu.SMEM)]
+        + [hbm if i in far_in else vmem for i in range(1, len(operands))],
+        out_specs=[hbm if i in far_out else vmem for i in range(len(outs))],
         scratch_shapes=list(scratch),
         compiler_params=pltpu.CompilerParams(vmem_limit_bytes=50 * 2**20),
         name=name,
-    )(*operands)
-
-
-def project_kernel(place, ms, gs, qs, mn, gn, qn, mine, theirs, left):
+    )(*[pltpu.with_memory_space_constraint(a, pltpu.HBM) if i in far_in else a for i, a in enumerate(operands)])
+
+
+def project_kernel(place, ms, gs, qs, mn, gn, qn, mine, theirs, left, m_in, g_in, q_in, mn_in, gn_in, qn_in, sem):
     core = place[0]
-    for k in range(4):
-        m, g, q = (ms, gs, qs) if k < 2 else (mn, gn, qn)
+    copies = [
+        [pltpu.make_async_copy(a.at[k], b.at[k], sem.at[i, k])
+         for i, (a, b) in enumerate(((ms, m_in), (gs, g_in), (qs, q_in)))]
+        for k in range(2)
+    ]
+    copies.append([
+        pltpu.make_async_copy(a, b, sem.at[3 + i, 0])
+        for i, (a, b) in enumerate(((mn, mn_in), (gn, gn_in), (qn, qn_in)))
+    ])
+    for group in copies:
+        for copy in group:
+            copy.start()
+    for k in range(4):
+        if k < 3:
+            for copy in copies[k]:
+                copy.wait()
+        m, g, q = (m_in, g_in, q_in) if k < 2 else (mn_in, gn_in, qn_in)
         buffer = split(m[k % 2] + g[k % 2].astype(F32))
         left[k] = dot3(buffer, split(q[k % 2]), NN)
     for x in range(4):
@@ -80,27 +96,37 @@
 
 def factor_kernel(place, g0, g1, g2, g3, out, w):
     q = place[2]
-    n, nb = RANK, 64
+    n, nb, step = RANK, 64, 8
     for j, g in enumerate((g0, g1, g2, g3)):
         w[pl.ds(pl.multiple_of((q ^ j) * 64, 64), 64), :n] = g[...].reshape(64, n)
     row = lax.broadcasted_iota(jnp.int32, (n, n), 0)
     col = lax.broadcasted_iota(jnp.int32, (n, n), 1)
     w[:, n:] = jnp.where(row == col, 1.0, 0.0)
-    sub = lax.broadcasted_iota(jnp.int32, (nb, 1), 0)
+    sub = lax.broadcasted_iota(jnp.int32, (nb, 128), 0)
     for o in range(0, n, nb):
         lo, hi = o // 128 * 128, n + (o + nb + 127) // 128 * 128
-        r = w[o:o + nb, lo:hi]
-        d = jnp.ones((nb, 1), F32)
-        for i in range(nb):
-            c = o + i - lo
-            pivot = r[i:i + 1, c:c + 1]
-            f = jnp.where(sub > i, r[:, c:c + 1] * (1.0 / pivot), 0.0)
-            d = jnp.where(sub == i, pivot, d)
-            r = r - f * r[i:i + 1, :]
-        s = r * lax.rsqrt(d)
-        out[o:o + nb, :hi - n] = s[:, n - lo:]
-        if hi < 2 * n:
-            out[o:o + nb, hi - n:] = jnp.zeros((nb, 2 * n - hi), F32)
+        r = [w[o:o + nb, t:t + 128] for t in range(lo, hi, 128)]
+        d = jnp.ones((nb, 128), F32)
+        for i in range(0, nb, step):
+            c = o - lo + i
+            cols = [jnp.broadcast_to(r[0][:, c + j:c + j + 1], (nb, 128)) for j in range(step)]
+            rows = [[a[i + j:i + j + 1, :] for a in r] for j in range(step)]
+            for j in range(step):
+                p = i + j
+                pivot = cols[j][p:p + 1, :]
+                d = jnp.where(sub == p, pivot, d)
+                f = jnp.where(sub > p, cols[j] * (1.0 / pivot), 0.0)
+                for t in range(j + 1, step):
+                    cols[t] = cols[t] - f * cols[t][p:p + 1, :]
+                    ft = f[i + t:i + t + 1, :]
+                    rows[t] = [a - ft * b for a, b in zip(rows[t], rows[j])]
+                r = [a - f * b for a, b in zip(r, rows[j])]
+        scale = lax.rsqrt(d)
+        s = jnp.concatenate([a * scale for a in r], axis=1)
+        half, at = o // 128, o % 128
+        out[half, at:at + nb, :] = s[:, n - lo:n - lo + 128]
+        if half:
+            out[2, at:at + nb, :] = s[:, n - lo + 128:n - lo + 256]
         if o + nb < n:
             change = lax.dot_general(
                 s[:, :n - lo], s, TN, precision=lax.Precision.HIGHEST, preferred_element_type=F32
@@ -108,11 +134,17 @@
             w[o + nb:, lo:hi] = w[o + nb:, lo:hi] - change[o + nb - lo:]
 
 
-def right_kernel(place, w0, w1, w2, w3, l0, l1, l2, l3, left, ms, gs, mn, gn,
-                 right_s, right_n, ortho, squares, mom_s, mom_n, inv):
-    x, q = place[1], place[2]
-    for d, linv in enumerate((l0, l1, l2, l3)):
-        inv[(x - d) & 3] = linv[...]
+def fill_inverse(inv, blocks):
+    for k in range(4):
+        inv[k, :128, :128] = blocks[k, 0]
+        inv[k, :128, 128:] = jnp.zeros((128, 128), F32)
+        inv[k, 128:, :128] = blocks[k, 1]
+        inv[k, 128:, 128:] = blocks[k, 2]
+
+
+def right_kernel(place, w0, w1, w2, w3, blocks, right_s, right_n, squares, inv):
+    q = place[2]
+    fill_inverse(inv, blocks)
     for j, w in enumerate((w0, w1, w2, w3)):
         p = q ^ j
         for k in range(2):
@@ -124,24 +156,44 @@
         )
     squares[...] = jnp.zeros_like(squares)
     for k in range(4):
-        m, g, right, mom = (ms, gs, right_s, mom_s) if k < 2 else (mn, gn, right_n, mom_n)
-        r = right[k % 2]
+        r = (right_s if k < 2 else right_n)[k % 2]
         squares[k:k + 1, :] = jnp.sum(r * r, axis=0, keepdims=True)
+
+
+def momentum_kernel(place, blocks, right_s, right_n, left, ms, gs, mn, gn, ortho, mom_s, mom_n, inv, s_out, n_out, sem):
+    fill_inverse(inv, blocks)
+    copies = []
+    for k in range(4):
+        m, g, right, mom, new = (ms, gs, right_s, mom_s, s_out) if k < 2 else (mn, gn, right_n, mom_n, n_out)
         o = dot3(split(left[k]), split(inv[k]), NT)
         ortho[k] = o
-        low_rank = lax.dot_general(o.astype(BF16), r.astype(BF16), NT, preferred_element_type=F32)
-        mom[k % 2] = (m[k % 2] + g[k % 2].astype(F32)) - (1.0 - 0.95) * low_rank
-
-
-def update_kernel(place, squares, right_s, right_n, ortho, up_s, basis_s, up_n, basis_n):
-    scale = lax.rsqrt(jnp.sum(squares[...], axis=0) + 1e-06)
-    for k in range(4):
-        right, up, basis, columns = (right_s, up_s, basis_s, D) if k < 2 else (right_n, up_n, basis_n, KVW)
+        low_rank = lax.dot_general(o.astype(BF16), right[k % 2].astype(BF16), NT, preferred_element_type=F32)
+        new[k % 2] = (m[k % 2] + g[k % 2].astype(F32)) - (1.0 - 0.95) * low_rank
+        copies.append(pltpu.make_async_copy(new.at[k % 2], mom.at[k % 2], sem.at[k]))
+        copies[k].start()
+    for copy in copies:
+        copy.wait()
+
+
+def update_kernel(place, q0, q1, q2, q3, right_s, right_n, ortho, up_s, basis_s, up_n, basis_n,
+                  us_out, bs_out, un_out, bn_out, sem):
+    scale = lax.rsqrt((q0[...] + q1[...]) + (q2[...] + q3[...]) + 1e-06)
+    copies = []
+    for k in range(4):
+        right, up, basis, columns, u_out, b_out = (
+            (right_s, up_s, basis_s, D, us_out, bs_out) if k < 2 else (right_n, up_n, basis_n, KVW, un_out, bn_out)
+        )
         s = scale[k:k + 1, :]
         r = right[k % 2]
-        basis[k % 2] = r * s
+        b_out[k % 2] = r * s
+        copies.append(pltpu.make_async_copy(b_out.at[k % 2], basis.at[k % 2], sem.at[0, k]))
+        copies[-1].start()
         o = ortho[k] * (s * (D * columns / RANK) ** 0.5)
-        up[k % 2] = dot3(split(o), split(r), NT).astype(BF16)
+        u_out[k % 2] = dot3(split(o), split(r), NT).astype(BF16)
+        copies.append(pltpu.make_async_copy(u_out.at[k % 2], up.at[k % 2], sem.at[1, k]))
+        copies[-1].start()
+    for copy in copies:
+        copy.wait()
 
 
 def partners():
@@ -180,8 +232,12 @@
         project_kernel,
         [((4, 4, 32, RANK), F32)] * 2,
         (place, mom_square, grad_square, basis_square, mom_narrow, grad_narrow, basis_narrow),
-        [pltpu.VMEM((4, 256, RANK), F32)],
+        [pltpu.VMEM((4, 256, RANK), F32)]
+        + [pltpu.VMEM(a.shape, a.dtype)
+           for a in (mom_square, grad_square, basis_square, mom_narrow, grad_narrow, basis_narrow)]
+        + [pltpu.SemaphoreType.DMA((6, 2))],
         name="project",
+        far_in=range(1, 7),
     )
     half = mine + swap_core(theirs)
     part = jnp.sum(lax.all_to_all(half, "x", 0, 0), axis=0)
@@ -203,28 +259,40 @@
     grams = [gram] + [lax.ppermute(gram, AXES, pairs) for pairs in in_block]
     w = own[:, :CHUNK, :]
     ws = [w] + [lax.ppermute(w, AXES, pairs) for pairs in in_block]
-    (inverse,) = call(
+    (blocks,) = call(
         factor_kernel,
-        [((RANK, RANK), F32)],
+        [((3, 128, 128), F32)],
         (place, *grams),
         [pltpu.VMEM((RANK, 2 * RANK), F32)],
         name="factor",
     )
-    inverses = around_x(inverse)
-    right_s, right_n, ortho, squares, new_mom_s, new_mom_n = call(
+    blocks = lax.all_to_all(jnp.broadcast_to(blocks[None], (4,) + blocks.shape), "x", 0, 0)
+    inverse = pltpu.VMEM((4, RANK, RANK), F32)
+    right_s, right_n, squares = call(
         right_kernel,
-        [((2, 1024, RANK), F32), ((2, 128, RANK), F32), ((4, 256, RANK), F32), ((8, RANK), F32),
-         (mom_square.shape, F32), (mom_narrow.shape, F32)],
-        (place, *ws, *inverses, left, mom_square, grad_square, mom_narrow, grad_narrow),
-        [pltpu.VMEM((4, RANK, RANK), F32)],
+        [((2, 1024, RANK), F32), ((2, 128, RANK), F32), ((8, RANK), F32)],
+        (place, *ws, blocks),
+        [inverse],
         name="right",
     )
-    squares = lax.all_to_all(jnp.broadcast_to(squares[None], (8,) + squares.shape), COLS, 0, 0)
+    squares, left = lax.optimization_barrier((squares + swap_core(squares), left))
+    four_squares = around_x(squares)
+    ortho, new_mom_s, new_mom_n = call(
+        momentum_kernel,
+        [((4, 256, RANK), F32), (mom_square.shape, F32), (mom_narrow.shape, F32)],
+        (place, blocks, right_s, right_n, left, mom_square, grad_square, mom_narrow, grad_narrow),
+        [inverse, pltpu.VMEM(mom_square.shape, F32), pltpu.VMEM(mom_narrow.shape, F32), pltpu.SemaphoreType.DMA((4,))],
+        name="momentum",
+        far_out=(1, 2),
+    )
+    outs = [(mom_square.shape, BF16), (basis_square.shape, F32), (mom_narrow.shape, BF16), (basis_narrow.shape, F32)]
     up_s, basis_s, up_n, basis_n = call(
         update_kernel,
-        [(mom_square.shape, BF16), (basis_square.shape, F32), (mom_narrow.shape, BF16), (basis_narrow.shape, F32)],
-        (place, squares, right_s, right_n, ortho),
+        outs,
+        (place, *four_squares, right_s, right_n, ortho),
+        [pltpu.VMEM(s, d) for s, d in outs] + [pltpu.SemaphoreType.DMA((2, 4))],
         name="update",
+        far_out=range(4),
     )
     return new_mom_s, up_s, basis_s, new_mom_n, up_n, basis_n
 

time: 190 us -> 164 us (0.86)
  Pallas kernels: 43.6 us -> 30.4 us
  blocking collectives: 80.6 us -> 69.6 us
  local copies, waits for them, and re-layouts: 7 us -> 1.11 us
  starting transfers between devices: 26.1 us -> 29.8 us
    ppermute x3, waiting for transfers between devices: 13.7 us -> 0.01 us  [around_x(): got[d] = lax.ppermute(value, 'x', [(i, (i + d) % 4) for i in range(4)])]
    pallas_call x5 -> x6, Pallas kernels: 43.6 us -> 30.4 us  [call(): pl.pallas_call(kernel, out_shape=[jax.ShapeDtypeStruct(s, d) for s, d in...]
    all_to_all x0 -> x1, waiting for transfers between devices: none -> 12.4 us  [local(): lax.all_to_all(jnp.broadcast_to(blocks[None], (4,) + blocks.shape), 'x',...]
    all_to_all x1 -> x0, blocking collectives: 11 us -> none  [local(): lax.all_to_all(jnp.broadcast_to(squares[None], (8,) + squares.shape), COL...]
    unnamed x16 -> x8, local copies, waits for them, and re-layouts: 6.86 us -> 0.02 us
    all_to_all x0 -> x1, starting transfers between devices: none -> 3.63 us  [local(): lax.all_to_all(jnp.broadcast_to(blocks[None], (4,) + blocks.shape), 'x',...]
    ppermute x2 -> x3, waiting for transfers between devices: 3.07 us -> 3.9 us  [swap_core(): return lax.ppermute(value, 'core', [(0, 1), (1, 0)])]
    ppermute x2 -> x3, starting transfers between devices: 5.45 us -> 6.1 us  [swap_core(): return lax.ppermute(value, 'core', [(0, 1), (1, 0)])]
  transfers between devices with their start and end apart: 14 -> 16, of which waited for: 8 -> 8; matrix products, arithmetic and copies ran while one was open for 0% -> 1% of each run, Pallas kernels for 13% -> 9%
where the time goes in v2:
time: 164 us; the launch traced here: 163 us
  blocking collectives  69.6 us (42%)
  waiting for transfers between devices  31.2 us (19%)
  Pallas kernels  30.4 us (19%)
  starting transfers between devices  29.8 us (18%)
    pallas_call x6, Pallas kernels, call(): pl.pallas_call(kernel, out_shape=[jax.ShapeDtypeStruct(s, d) for s, d in...  30.4 us
    all_to_all x1, blocking collectives, local(): part = jnp.sum(lax.all_to_all(own, FAR, 0, 0), axis=0)  26.2 us
    all_to_all x1, blocking collectives, local(): lax.all_to_all(jnp.broadcast_to(part[None], (8,) + part.shape), FAR, 0, 0)  21 us
    ppermute x3, waiting for transfers between devices, local(): own = own + lax.ppermute(value, AXES, pairs)  14.7 us
    all_to_all x1, waiting for transfers between devices, local(): lax.all_to_all(jnp.broadcast_to(blocks[None], (4,) + blocks.shape), 'x',...  12.4 us
    all_to_all x1, blocking collectives, local(): part = jnp.sum(lax.all_to_all(half, 'x', 0, 0), axis=0)  11.8 us
    all_to_all x1, blocking collectives, local(): lax.all_to_all(jnp.broadcast_to(part[None], (4,) + part.shape), 'x', 0, 0)  10.7 us
    ppermute x3, starting transfers between devices, local(): own = own + lax.ppermute(value, AXES, pairs)  7.38 us
  transfers between devices with their start and end apart: 16, of which 8 were waited for; matrix products, arithmetic and copies ran while one was open for 1% of the time, Pallas kernels for 9%

profile of v2, /device:TPU:1, one launch (start us, length us, event | category | flops | bytes accessed | tf_op | source)
XLA Modules:
  0.0 163.5 jit_solution(942753209853041044)
XLA Ops:
  0.6 0.1 pad_add_fusion.place
  0.7 4.7 %project.1 = (f32[4,4,32,256]{3,2,1,0:T(8,128)S(1)}, f32[4,4,32,256]{3,2,1,0:T(8,128)S(1)}) custom-call(s32[3]{0:T(128)S(1)} %pad_add_fusion.place, f32[2,256,1024]{2,1,0:T(8,128)} %ms.5, bf16[2,256,1024]{2,1,0:T(8,128)(2,1)} %gs.5, f32[2,1024,256]{2,1,0:T(8,128)} %qs.1, f32[2,256,128]{2,1,0:T(8,128)} %mn.5, bf16[2,256,128]{2,1,0:T(8,128)(2,1)} %gn.5, ...), custom_call_target="tpu_custom_call" | custom-call | tf_op jit(solution)/shard_map/project/pallas_call | solution.py:40
  5.4 3.3 %collective-permute-start = (f32[4,4,32,256]{3,2,1,0:T(8,128)S(1)}, f32[4,4,32,256]{3,2,1,0:T(8,128)S(1)}, u32[]{:S(2)}, u32[]{:S(2)}) collective-permute-start(f32[4,4,32,256]{3,2,1,0:T(8,128)S(1)} %get-tuple-element.26), channel_id=1, source_target_pairs={{0,1},{1,0},{2,3},{3,2},{4,5},{5,4},{6,7},{7,6},{8,9},{9,8},{10,11... | collective-permute-start | bytes 1572872 | tf_op jit(solution)/shard_map/ppermute | solution.py:223
  8.7 1.5 collective-permute-done
  10.3 0.1 add.19
  10.4 0.0 copy-start.1
  10.4 0.0 copy-start.2
  10.4 11.8 %all_to_all.25 = f32[4,4,32,256]{3,2,1,0:T(8,128)S(1)} all-to-all(f32[4,4,32,256]{3,2,1,0:T(8,128)S(1)} %add.19), channel_id=1, replica_groups=mesh['zh'=4,'zl'=2,'yh'=2,'yl'=2,'x'=4,'core'=2] {'x'}, dimensions={0} | all-to-all | bytes 1048576 | tf_op jit(solution)/shard_map/all_to_all | solution.py:243
  22.2 10.7 %all_to_all.26.own_half = f32[4,4,32,256]{3,2,1,0:T(8,128)S(1)} all-to-all(f32[4,4,32,256]{3,2,1,0:T(8,128)S(1)} %broadcast_in_dim.6), channel_id=1, replica_groups=mesh['zh'=4,'zl'=2,'yh'=2,'yl'=2,'x'=4,'core'=2] {'x'}, dimensions={0} | all-to-all | bytes 1048576 | tf_op jit(solution)/shard_map/all_to_all | solution.py:244
  32.9 2.1 %collective-permute-start.1 = (f32[4,4,32,256]{3,2,1,0:T(8,128)S(1)}, f32[4,4,32,256]{3,2,1,0:T(8,128)S(1)}, u32[]{:S(2)}, u32[]{:S(2)}) collective-permute-start(f32[4,4,32,256]{3,2,1,0:T(8,128)S(1)} %all_to_all.26.own_half), channel_id=1, source_target_pairs={{0,1},{1,0},{2,3},{3,2},{4,5},{5,4},{6,7},{7,6},{8,9},{9,8},{10,11... | collective-permute-start | bytes 1572872 | tf_op jit(solution)/shard_map/ppermute | solution.py:223
  35.1 1.5 collective-permute-done.1.other_half
  36.6 0.0 copy-done.1
  36.6 0.0 copy-done.2
  36.6 4.4 %back.1 = (f32[4,256,256]{2,1,0:T(8,128)}, f32[8,80,256]{2,1,0:T(8,128)S(1)}, f32[8,80,256]{2,1,0:T(8,128)S(1)}, f32[8,80,256]{2,1,0:T(8,128)S(1)}, f32[8,80,256]{2,1,0:T(8,128)S(1)}) custom-call(s32[3]{0:T(128)S(1)} %pad_add_fusion.place, f32[2,256,1024]{2,1,0:T(8,128)} %ms.5, bf16[2,256,1024]{2,1,0:T(8,128)(2,1)} %gs.5, f32[2,256,128]{2,1,0:T(8,128)S(1)} %copy-done.1, ...), custom_call_target="tpu_custom_call" | custom-call | tf_op jit(solution)/shard_map/back/pallas_call | solution.py:40
  41.0 1.8 %collective-permute-start.2 = (f32[8,80,256]{2,1,0:T(8,128)S(1)}, f32[8,80,256]{2,1,0:T(8,128)S(1)}, u32[]{:S(2)}, u32[]{:S(2)}) collective-permute-start(f32[8,80,256]{2,1,0:T(8,128)S(1)} %get-tuple-element.28), channel_id=1, source_target_pairs={{0,8},{1,25},{2,10},{3,27},{4,12},{5,29},{6,14},{7,31},{8,0},{9,17... | collective-permute-start | bytes 1966088 | tf_op jit(solution)/shard_map/ppermute | solution.py:255
  42.8 5.6 %collective-permute-start.3 = (f32[8,80,256]{2,1,0:T(8,128)S(1)}, f32[8,80,256]{2,1,0:T(8,128)S(1)}, u32[]{:S(2)}, u32[]{:S(2)}) collective-permute-start(f32[8,80,256]{2,1,0:T(8,128)S(1)} %get-tuple-element.29), channel_id=1, source_target_pairs={{0,32},{1,225},{2,34},{3,227},{4,36},{5,229},{6,38},{7,231},{8,40}... | collective-permute-start | bytes 1966088 | tf_op jit(solution)/shard_map/ppermute | solution.py:255
  48.4 0.0 collective-permute-start.4
  48.4 3.3 %collective-permute-done.2 = f32[8,80,256]{2,1,0:T(8,128)S(1)} collective-permute-done((f32[8,80,256]{2,1,0:T(8,128)S(1)}, f32[8,80,256]{2,1,0:T(8,128)S(1)}, u32[]{:S(2)}, u32[]{:S(2)}) %collective-permute-start.2) | collective-permute-done | bytes 655392 | tf_op jit(solution)/shard_map/ppermute | solution.py:255
  51.7 4.8 %collective-permute-done.3 = f32[8,80,256]{2,1,0:T(8,128)S(1)} collective-permute-done((f32[8,80,256]{2,1,0:T(8,128)S(1)}, f32[8,80,256]{2,1,0:T(8,128)S(1)}, u32[]{:S(2)}, u32[]{:S(2)}) %collective-permute-start.3) | collective-permute-done | bytes 655392 | tf_op jit(solution)/shard_map/ppermute | solution.py:255
  56.5 6.6 %collective-permute-done.4 = f32[8,80,256]{2,1,0:T(8,128)S(1)} collective-permute-done((f32[8,80,256]{2,1,0:T(8,128)S(1)}, f32[8,80,256]{2,1,0:T(8,128)S(1)}, u32[]{:S(2)}, u32[]{:S(2)}) %collective-permute-start.4) | collective-permute-done | bytes 655392 | tf_op jit(solution)/shard_map/ppermute | solution.py:255
  63.1 0.2 add_add_fusion
  63.3 26.2 %all_to_all.27 = f32[8,80,256]{2,1,0:T(8,128)S(1)} all-to-all(f32[8,80,256]{2,1,0:T(8,128)S(1)} %add_add_fusion), channel_id=1, replica_groups=mesh['zh'=4,'zl'=2,'yh'=2,'yl'=2,'x'=4,'core'=2] {'zh','yh'}, dimensions={0} | all-to-all | bytes 1310720 | tf_op jit(solution)/shard_map/all_to_all | solution.py:256
  89.6 21.0 %all_to_all.28 = f32[8,80,256]{2,1,0:T(8,128)S(1)} all-to-all(f32[8,80,256]{2,1,0:T(8,128)S(1)} %broadcast_in_dim.7), channel_id=1, replica_groups=mesh['zh'=4,'zl'=2,'yh'=2,'yl'=2,'x'=4,'core'=2] {'zh','yh'}, dimensions={0} | all-to-all | bytes 1310720 | tf_op jit(solution)/shard_map/all_to_all | solution.py:257
  110.6 0.0 collective-permute-start.7
  110.6 5.5 %collective-permute-start.6 = (f32[8,8,256]{2,1,0:T(8,128)S(1)}, f32[8,8,256]{2,1,0:T(8,128)S(1)}, u32[]{:S(2)}, u32[]{:S(2)}) collective-permute-start(f32[8,8,256]{2,1,0:T(8,128)S(1)} %slice.8.g0), channel_id=1, source_target_pairs={{0,32},{1,225},{2,34},{3,227},{4,36},{5,229},{6,38},{7,231},{8,40}... | collective-permute-start | bytes 196616 | tf_op jit(solution)/shard_map/ppermute | solution.py:259
  116.0 0.0 collective-permute-start.5
  116.1 2.5 %collective-permute-start.10 = (f32[8,72,256]{2,1,0:T(8,128)S(1)}, f32[8,72,256]{2,1,0:T(8,128)S(1)}, u32[]{:S(2)}, u32[]{:S(2)}) collective-permute-start(f32[8,72,256]{2,1,0:T(8,128)S(1)} %slice.9.w0), channel_id=1, source_target_pairs={{0,40},{1,249},{2,42},{3,251},{4,44},{5,253},{6,46},{7,255},{8,32}... | collective-permute-start | bytes 1769480 | tf_op jit(solution)/shard_map/ppermute | solution.py:261
  118.6 2.7 %collective-permute-start.9 = (f32[8,72,256]{2,1,0:T(8,128)S(1)}, f32[8,72,256]{2,1,0:T(8,128)}, u32[]{:S(2)}, u32[]{:S(2)}) collective-permute-start(f32[8,72,256]{2,1,0:T(8,128)S(1)} %slice.9.w0), channel_id=1, source_target_pairs={{0,32},{1,225},{2,34},{3,227},{4,36},{5,229},{6,38},{7,231},{8,40}... | collective-permute-start | bytes 1769480 | tf_op jit(solution)/shard_map/ppermute | solution.py:261
  121.2 0.0 collective-permute-done.7.g3
  121.2 0.0 collective-permute-start.8
  121.3 0.0 collective-permute-done.6.g2
  121.3 0.0 collective-permute-done.5.g1
  121.3 9.0 %factor.1 = f32[3,128,128]{2,1,0:T(8,128)S(1)} custom-call(s32[3]{0:T(128)S(1)} %pad_add_fusion.place, f32[8,8,256]{2,1,0:T(8,128)S(1)} %slice.8.g0, f32[8,8,256]{2,1,0:T(8,128)S(1)} %collective-permute-done.5.g1, f32[8,8,256]{2,1,0:T(8,128)S(1)} %collective-permute-done.6.g2, f32[8,8,256]{2,1,0:T(8,128)S(1)} %collective-permute-done.7.g3), custom_call_target="tpu_custom_call" | custom-call | tf_op jit(solution)/shard_map/factor/pallas_call | solution.py:40
  130.3 1.0 broadcast_in_dim.8
  131.2 0.0 copy-start.3
  131.2 3.6 %all-to-all-start.4 = ((f32[4,3,128,128]{3,2,1,0:T(8,128)}), f32[4,3,128,128]{3,2,1,0:T(8,128)S(1)}, u32[]{:S(2)}, u32[]{:S(2)}) async-start(f32[4,3,128,128]{3,2,1,0:T(8,128)} %broadcast_in_dim.8), calls=%async_computation.4 | async-start | bytes 1572864 | tf_op jit(solution)/shard_map/all_to_all | solution.py:269
  134.9 0.0 collective-permute-done.10.w3
  134.9 0.1 collective-permute-done.9.w2
  135.0 0.0 collective-permute-done.8.w1
  135.0 12.4 %all-to-all-done.4.blocks = f32[4,3,128,128]{3,2,1,0:T(8,128)S(1)} async-done(((f32[4,3,128,128]{3,2,1,0:T(8,128)}), f32[4,3,128,128]{3,2,1,0:T(8,128)S(1)}, u32[]{:S(2)}, u32[]{:S(2)}) %all-to-all-start.4) | async-done | bytes 786464 | tf_op jit(solution)/shard_map/all_to_all | solution.py:269
  147.4 4.1 %right.1 = (f32[2,1024,256]{2,1,0:T(8,128)}, f32[2,128,256]{2,1,0:T(8,128)S(1)}, f32[8,256]{1,0:T(8,128)S(1)}) custom-call(s32[3]{0:T(128)S(1)} %pad_add_fusion.place, f32[8,72,256]{2,1,0:T(8,128)S(1)} %slice.9.w0, f32[8,72,256]{2,1,0:T(8,128)} %collective-permute-done.8.w1, f32[8,72,256]{2,1,0:T(8,128)} %collective-permute-done.9.w2, ...), custom_call_target="tpu_custom_call" | custom-call | tf_op jit(solution)/shard_map/right/pallas_call | solution.py:40
  151.5 0.7 collective-permute-start.11
  152.2 0.8 collective-permute-done.11
  153.0 0.9 collective-permute-start.14
  153.9 1.2 collective-permute-start.13
  155.1 0.0 collective-permute-start.12
  155.1 0.0 copy-done.3
  155.1 0.0 copy-start
  155.1 5.2 %momentum.1 = (f32[4,256,256]{2,1,0:T(8,128)S(1)}, f32[2,256,1024]{2,1,0:T(8,128)}, f32[2,256,128]{2,1,0:T(8,128)}) custom-call(s32[3]{0:T(128)S(1)} %pad_add_fusion.place, f32[4,3,128,128]{3,2,1,0:T(8,128)S(1)} %all-to-all-done.4.blocks, f32[2,1024,256]{2,1,0:T(8,128)} %get-tuple-element.31.right_s, f32[2,128,256]{2,1,0:T(8,128)S(1)} %get-tuple-element.32.right_n, ...), custom_call_target="tpu_custom_call" | custom-call | tf_op jit(solution)/shard_map/momentum/pallas_call | solution.py:40
  160.3 0.0 collective-permute-done.14.q3
  160.3 0.0 collective-permute-done.13.q2
  160.3 0.0 collective-permute-done.12.q1
  160.3 0.0 copy-done
  160.3 3.0 %update.1 = (bf16[2,256,1024]{2,1,0:T(8,128)(2,1)}, f32[2,1024,256]{2,1,0:T(8,128)}, bf16[2,256,128]{2,1,0:T(8,128)(2,1)}, f32[2,128,256]{2,1,0:T(8,128)}) custom-call(s32[3]{0:T(128)S(1)} %pad_add_fusion.place, f32[8,256]{1,0:T(8,128)S(1)} %add.23.q0, f32[8,256]{1,0:T(8,128)S(1)} %collective-permute-done.12.q1, f32[8,256]{1,0:T(8,128)S(1)} %collective-permute-done.13.q2, ...), custom_call_target="tpu_custom_call" | custom-call | tf_op jit(solution)/shard_map/update/pallas_call | solution.py:40
  (7 shorter events, 0.2 us)
Async XLA Ops:
  5.4 4.9 %collective-permute-start = (f32[4,4,32,256]{3,2,1,0:T(8,128)S(1)}, f32[4,4,32,256]{3,2,1,0:T(8,128)S(1)}, u32[]{:S(2)}, u32[]{:S(2)}) collective-permute-start(f32[4,4,32,256]{3,2,1,0:T(8,128)S(1)} %get-tuple-element.26), channel_id=1, source_target_pairs={{0,1},{1,0},{2,3},{3,2},{4,5},{5,4},{6,7},{7,6},{8,9},{9,8},{10,11... | collective-permute-start | bytes 1572872 | tf_op jit(solution)/shard_map/ppermute | solution.py:223
  10.4 26.2 %copy-start.1 = (f32[2,256,128]{2,1,0:T(8,128)S(1)}, f32[2,256,128]{2,1,0:T(8,128)}, u32[]{:S(2)}) copy-start(f32[2,256,128]{2,1,0:T(8,128)} %mn.5) | copy-start | bytes 786436
  10.4 26.2 %copy-start.2 = (bf16[2,256,128]{2,1,0:T(8,128)(2,1)S(1)}, bf16[2,256,128]{2,1,0:T(8,128)(2,1)}, u32[]{:S(2)}) copy-start(bf16[2,256,128]{2,1,0:T(8,128)(2,1)} %gn.5) | copy-start | bytes 393220
  32.9 3.7 %collective-permute-start.1 = (f32[4,4,32,256]{3,2,1,0:T(8,128)S(1)}, f32[4,4,32,256]{3,2,1,0:T(8,128)S(1)}, u32[]{:S(2)}, u32[]{:S(2)}) collective-permute-start(f32[4,4,32,256]{3,2,1,0:T(8,128)S(1)} %all_to_all.26.own_half), channel_id=1, source_target_pairs={{0,1},{1,0},{2,3},{3,2},{4,5},{5,4},{6,7},{7,6},{8,9},{9,8},{10,11... | collective-permute-start | bytes 1572872 | tf_op jit(solution)/shard_map/ppermute | solution.py:223
  41.0 10.6 %collective-permute-start.2 = (f32[8,80,256]{2,1,0:T(8,128)S(1)}, f32[8,80,256]{2,1,0:T(8,128)S(1)}, u32[]{:S(2)}, u32[]{:S(2)}) collective-permute-start(f32[8,80,256]{2,1,0:T(8,128)S(1)} %get-tuple-element.28), channel_id=1, source_target_pairs={{0,8},{1,25},{2,10},{3,27},{4,12},{5,29},{6,14},{7,31},{8,0},{9,17... | collective-permute-start | bytes 1966088 | tf_op jit(solution)/shard_map/ppermute | solution.py:255
  42.8 13.7 %collective-permute-start.3 = (f32[8,80,256]{2,1,0:T(8,128)S(1)}, f32[8,80,256]{2,1,0:T(8,128)S(1)}, u32[]{:S(2)}, u32[]{:S(2)}) collective-permute-start(f32[8,80,256]{2,1,0:T(8,128)S(1)} %get-tuple-element.29), channel_id=1, source_target_pairs={{0,32},{1,225},{2,34},{3,227},{4,36},{5,229},{6,38},{7,231},{8,40}... | collective-permute-start | bytes 1966088 | tf_op jit(solution)/shard_map/ppermute | solution.py:255
  48.4 14.7 %collective-permute-start.4 = (f32[8,80,256]{2,1,0:T(8,128)S(1)}, f32[8,80,256]{2,1,0:T(8,128)S(1)}, u32[]{:S(2)}, u32[]{:S(2)}) collective-permute-start(f32[8,80,256]{2,1,0:T(8,128)S(1)} %get-tuple-element.30), channel_id=1, source_target_pairs={{0,40},{1,249},{2,42},{3,251},{4,44},{5,253},{6,46},{7,255},{8,32}... | collective-permute-start | bytes 1966088 | tf_op jit(solution)/shard_map/ppermute | solution.py:255
  110.6 10.7 %collective-permute-start.7 = (f32[8,8,256]{2,1,0:T(8,128)S(1)}, f32[8,8,256]{2,1,0:T(8,128)S(1)}, u32[]{:S(2)}, u32[]{:S(2)}) collective-permute-start(f32[8,8,256]{2,1,0:T(8,128)S(1)} %slice.8.g0), channel_id=1, source_target_pairs={{0,40},{1,249},{2,42},{3,251},{4,44},{5,253},{6,46},{7,255},{8,32}... | collective-permute-start | bytes 196616 | tf_op jit(solution)/shard_map/ppermute | solution.py:259
  110.6 10.7 %collective-permute-start.6 = (f32[8,8,256]{2,1,0:T(8,128)S(1)}, f32[8,8,256]{2,1,0:T(8,128)S(1)}, u32[]{:S(2)}, u32[]{:S(2)}) collective-permute-start(f32[8,8,256]{2,1,0:T(8,128)S(1)} %slice.8.g0), channel_id=1, source_target_pairs={{0,32},{1,225},{2,34},{3,227},{4,36},{5,229},{6,38},{7,231},{8,40}... | collective-permute-start | bytes 196616 | tf_op jit(solution)/shard_map/ppermute | solution.py:259
  116.0 5.2 %collective-permute-start.5 = (f32[8,8,256]{2,1,0:T(8,128)S(1)}, f32[8,8,256]{2,1,0:T(8,128)S(1)}, u32[]{:S(2)}, u32[]{:S(2)}) collective-permute-start(f32[8,8,256]{2,1,0:T(8,128)S(1)} %slice.8.g0), channel_id=1, source_target_pairs={{0,8},{1,25},{2,10},{3,27},{4,12},{5,29},{6,14},{7,31},{8,0},{9,17... | collective-permute-start | bytes 196616 | tf_op jit(solution)/shard_map/ppermute | solution.py:259
  116.1 18.8 %collective-permute-start.10 = (f32[8,72,256]{2,1,0:T(8,128)S(1)}, f32[8,72,256]{2,1,0:T(8,128)S(1)}, u32[]{:S(2)}, u32[]{:S(2)}) collective-permute-start(f32[8,72,256]{2,1,0:T(8,128)S(1)} %slice.9.w0), channel_id=1, source_target_pairs={{0,40},{1,249},{2,42},{3,251},{4,44},{5,253},{6,46},{7,255},{8,32}... | collective-permute-start | bytes 1769480 | tf_op jit(solution)/shard_map/ppermute | solution.py:261
  118.6 16.4 %collective-permute-start.9 = (f32[8,72,256]{2,1,0:T(8,128)S(1)}, f32[8,72,256]{2,1,0:T(8,128)}, u32[]{:S(2)}, u32[]{:S(2)}) collective-permute-start(f32[8,72,256]{2,1,0:T(8,128)S(1)} %slice.9.w0), channel_id=1, source_target_pairs={{0,32},{1,225},{2,34},{3,227},{4,36},{5,229},{6,38},{7,231},{8,40}... | collective-permute-start | bytes 1769480 | tf_op jit(solution)/shard_map/ppermute | solution.py:261
  121.2 13.7 %collective-permute-start.8 = (f32[8,72,256]{2,1,0:T(8,128)S(1)}, f32[8,72,256]{2,1,0:T(8,128)}, u32[]{:S(2)}, u32[]{:S(2)}) collective-permute-start(f32[8,72,256]{2,1,0:T(8,128)S(1)} %slice.9.w0), channel_id=1, source_target_pairs={{0,8},{1,25},{2,10},{3,27},{4,12},{5,29},{6,14},{7,31},{8,0},{9,17... | collective-permute-start | bytes 1769480 | tf_op jit(solution)/shard_map/ppermute | solution.py:261
  131.2 23.9 %copy-start.3 = (f32[4,256,256]{2,1,0:T(8,128)S(1)}, f32[4,256,256]{2,1,0:T(8,128)}, u32[]{:S(2)}) copy-start(f32[4,256,256]{2,1,0:T(8,128)} %get-tuple-element.35.left) | copy-start | bytes 3145732
  131.2 16.2 %all-to-all-start.4 = ((f32[4,3,128,128]{3,2,1,0:T(8,128)}), f32[4,3,128,128]{3,2,1,0:T(8,128)S(1)}, u32[]{:S(2)}, u32[]{:S(2)}) async-start(f32[4,3,128,128]{3,2,1,0:T(8,128)} %broadcast_in_dim.8), calls=%async_computation.4 | async-start | bytes 1572864 | tf_op jit(solution)/shard_map/all_to_all | solution.py:269
  151.5 1.5 collective-permute-start.11
  153.0 7.3 %collective-permute-start.14 = (f32[8,256]{1,0:T(8,128)S(1)}, f32[8,256]{1,0:T(8,128)S(1)}, u32[]{:S(2)}, u32[]{:S(2)}) collective-permute-start(f32[8,256]{1,0:T(8,128)S(1)} %add.23.q0), channel_id=1, source_target_pairs={{0,6},{2,0},{4,2},{6,4},{1,7},{3,1},{5,3},{7,5},{8,14},{10,8},{12,... | collective-permute-start | bytes 24584 | tf_op jit(solution)/shard_map/ppermute | solution.py:218
  153.9 6.4 %collective-permute-start.13 = (f32[8,256]{1,0:T(8,128)S(1)}, f32[8,256]{1,0:T(8,128)S(1)}, u32[]{:S(2)}, u32[]{:S(2)}) collective-permute-start(f32[8,256]{1,0:T(8,128)S(1)} %add.23.q0), channel_id=1, source_target_pairs={{0,4},{2,6},{4,0},{6,2},{1,5},{3,7},{5,1},{7,3},{8,12},{10,14},{12... | collective-permute-start | bytes 24584 | tf_op jit(solution)/shard_map/ppermute | solution.py:218
  155.1 5.2 %collective-permute-start.12 = (f32[8,256]{1,0:T(8,128)S(1)}, f32[8,256]{1,0:T(8,128)S(1)}, u32[]{:S(2)}, u32[]{:S(2)}) collective-permute-start(f32[8,256]{1,0:T(8,128)S(1)} %add.23.q0), channel_id=1, source_target_pairs={{0,2},{2,4},{4,6},{6,0},{1,3},{3,5},{5,7},{7,1},{8,10},{10,12},{12... | collective-permute-start | bytes 24584 | tf_op jit(solution)/shard_map/ppermute | solution.py:218
  155.1 5.2 %copy-start = (f32[2,1024,256]{2,1,0:T(8,128)S(1)}, f32[2,1024,256]{2,1,0:T(8,128)}, u32[]{:S(2)}) copy-start(f32[2,1024,256]{2,1,0:T(8,128)} %get-tuple-element.31.right_s) | copy-start | bytes 6291460

commit v3 on v2

v3 whole, which is shorter than its diff:
```python
import functools

import jax
import jax.numpy as jnp
from jax import lax
from jax.experimental import pallas as pl
from jax.experimental.pallas import tpu as pltpu
from jax.sharding import Mesh, PartitionSpec as P

D = 8192
KVW = 1024
RANK = 256

F32 = jnp.float32
BF16 = jnp.bfloat16
AXES = ("zh", "zl", "yh", "yl", "x", "core")
ROWS = ("zh", "zl", "yh", "yl")
COLS = ("x", "core")
NN = (((1,), (0,)), ((), ()))
NT = (((1,), (1,)), ((), ()))
TN = (((0,), (0,)), ((), ()))
SQ, NA = 32, 8
CHUNK = 2 * SQ + NA


def split(value):
    high = value.astype(BF16)
    return high, (value - high.astype(F32)).astype(BF16)


def dot3(left, right, dims):
    (lh, ll), (rh, rl) = left, right
    dot = functools.partial(lax.dot_general, dimension_numbers=dims, preferred_element_type=F32)
    return dot(lh, rh) + (dot(lh, rl) + dot(ll, rh))


def call(kernel, outs, operands, scratch=(), name=None, far_in=(), far_out=()):
    vmem, hbm = pl.BlockSpec(memory_space=pltpu.VMEM), pl.BlockSpec(memory_space=pltpu.HBM)
    return pl.pallas_call(
        kernel,
        out_shape=[jax.ShapeDtypeStruct(s, d) for s, d in outs],
        in_specs=[pl.BlockSpec(memory_space=pltpu.SMEM)]
        + [hbm if i in far_in else vmem for i in range(1, len(operands))],
        out_specs=[hbm if i in far_out else vmem for i in range(len(outs))],
        scratch_shapes=list(scratch),
        compiler_params=pltpu.CompilerParams(vmem_limit_bytes=28 * 2**20),
        name=name,
    )(*[pltpu.with_memory_space_constraint(a, pltpu.HBM) if i in far_in else a for i, a in enumerate(operands)])


def project_kernel(place, ms, gs, qs, mn, gn, qn, mine, theirs, left, m_in, g_in, q_in, mn_in, gn_in, qn_in, sem):
    core = place[0]
    copies = [
        [pltpu.make_async_copy(a.at[k], b.at[k], sem.at[i, k])
         for i, (a, b) in enumerate(((ms, m_in), (gs, g_in), (qs, q_in)))]
        for k in range(2)
    ]
    copies.append([
        pltpu.make_async_copy(a, b, sem.at[3 + i, 0])
        for i, (a, b) in enumerate(((mn, mn_in), (gn, gn_in), (qn, qn_in)))
    ])
    for group in copies:
        for copy in group:
            copy.start()
    for k in range(4):
        if k < 3:
            for copy in copies[k]:
                copy.wait()
        m, g, q = (m_in, g_in, q_in) if k < 2 else (mn_in, gn_in, qn_in)
        buffer = split(m[k % 2] + g[k % 2].astype(F32))
        left[k] = dot3(buffer, split(q[k % 2]), NN)
    for x in range(4):
        for k in range(4):
            mine[x, k] = left[k, pl.ds(pl.multiple_of(core * 128 + x * 32, 32), 32), :]
            theirs[x, k] = left[k, pl.ds(pl.multiple_of((1 - core) * 128 + x * 32, 32), 32), :]


def back_kernel(place, ms, gs, mn, gn, own_half, other_half, left, gram, own, to_y, to_z, to_d, w):
    core, x, q = place[0], place[1], place[2]
    for i in range(4):
        for k in range(4):
            left[k, pl.ds(pl.multiple_of(core * 128 + i * 32, 32), 32), :] = own_half[i, k]
            left[k, pl.ds(pl.multiple_of((1 - core) * 128 + i * 32, 32), 32), :] = other_half[i, k]
    for k in range(2):
        buffer = split(ms[k] + gs[k].astype(F32))
        w[:, k * SQ:(k + 1) * SQ, :] = dot3(buffer, split(left[k]), TN).reshape(32, SQ, RANK)
    for k in range(2):
        buffer = split(mn[k] + gn[k].astype(F32))
        w[k * 16:(k + 1) * 16, 2 * SQ:, :] = dot3(buffer, split(left[2 + k]), TN).reshape(16, NA, RANK)
    one = split(left[x])
    gram[...] = dot3(one, one, TN).reshape(32, 8, RANK)
    for j, out in enumerate((own, to_y, to_z, to_d)):
        out[...] = w[pl.ds((q ^ j) * 8, 8)]


def factor_kernel(place, gram, out, w):
    n, nb, step = RANK, 64, 8
    w[:, :n] = gram[...]
    row = lax.broadcasted_iota(jnp.int32, (n, n), 0)
    col = lax.broadcasted_iota(jnp.int32, (n, n), 1)
    w[:, n:] = jnp.where(row == col, 1.0, 0.0)
    sub = lax.broadcasted_iota(jnp.int32, (nb, 128), 0)
    for o in range(0, n, nb):
        lo, hi = o // 128 * 128, n + (o + nb + 127) // 128 * 128
        r = [w[o:o + nb, t:t + 128] for t in range(lo, hi, 128)]
        d = jnp.ones((nb, 128), F32)
        for i in range(0, nb, step):
            c = o - lo + i
            cols = [jnp.broadcast_to(r[0][:, c + j:c + j + 1], (nb, 128)) for j in range(step)]
            rows = [[a[i + j:i + j + 1, :] for a in r] for j in range(step)]
            for j in range(step):
                p = i + j
                pivot = cols[j][p:p + 1, :]
                d = jnp.where(sub == p, pivot, d)
                f = jnp.where(sub > p, cols[j] * (1.0 / pivot), 0.0)
                for t in range(j + 1, step):
                    cols[t] = cols[t] - f * cols[t][p:p + 1, :]
                    ft = f[i + t:i + t + 1, :]
                    rows[t] = [a - ft * b for a, b in zip(rows[t], rows[j])]
                r = [a - f * b for a, b in zip(r, rows[j])]
        scale = lax.rsqrt(d)
        s = jnp.concatenate([a * scale for a in r], axis=1)
        half, at = o // 128, o % 128
        out[half, at:at + nb, :] = s[:, n - lo:n - lo + 128]
        if half:
            out[2, at:at + nb, :] = s[:, n - lo + 128:n - lo + 256]
        if o + nb < n:
            change = lax.dot_general(
                s[:, :n - lo], s, TN, precision=lax.Precision.HIGHEST, preferred_element_type=F32
            )
            w[o + nb:, lo:hi] = w[o + nb:, lo:hi] - change[o + nb - lo:]


def fill_inverse(inv, place, around):
    for d, blocks in enumerate(around):
        k = (place[1] - d) & 3
        inv[k, :128, :128] = blocks[0]
        inv[k, :128, 128:] = jnp.zeros((128, 128), F32)
        inv[k, 128:, :128] = blocks[1]
        inv[k, 128:, 128:] = blocks[2]


def right_kernel(place, w0, w1, w2, w3, l0, l1, l2, l3, right, squares, inv, w):
    q, b, yh = place[2], place[3], place[4]
    fill_inverse(inv, place, (l0, l1, l2, l3))
    for j, pair in enumerate((w0, w1, w2, w3)):
        for a in range(2):
            w[a * 4 + (b ^ (j >> 1)) * 2 + (yh ^ (j & 1))] = pair[a]
    row = lax.broadcasted_iota(jnp.int32, (8, RANK), 0)
    total = jnp.zeros((8, RANK), F32)
    for k in range(3):
        at, size, matrix = (k * SQ, SQ, k) if k < 2 else (2 * SQ, NA, 2 + (q >> 1))
        r = dot3(split(w[:, at:at + size, :].reshape(8 * size, RANK)), split(inv[matrix]), NT)
        right[:, at:at + size, :] = r.reshape(8, size, RANK)
        total = total + jnp.where(row == matrix, jnp.sum(r * r, axis=0, keepdims=True), 0.0)
    squares[...] = total


def ortho_kernel(place, l0, l1, l2, l3, left, ortho, inv):
    fill_inverse(inv, place, (l0, l1, l2, l3))
    for k in range(4):
        ortho[k] = dot3(split(left[k]), split(inv[k]), NT)


def finish_kernel(place, r0, r1, r2, r3, squares, ortho, ms, gs, mn, gn, mom_s, up_s, basis_s, mom_n, up_n, basis_n,
                  ms_out, us_out, bs_out, mn_out, un_out, bn_out, narrow, sem):
    q = place[2]
    scale = lax.rsqrt(squares[...] + 1e-06)
    copies = []

    def one(k, r, at):
        m, g, mom, up, basis, columns = (
            (ms, gs, ms_out, us_out, bs_out, D) if k < 2 else (mn, gn, mn_out, un_out, bn_out, KVW)
        )
        s = scale[k:k + 1, :]
        o = ortho[k]
        high, low = split(r)
        basis[k % 2, at, :] = r * s
        low_rank = lax.dot_general(o.astype(BF16), high, NT, preferred_element_type=F32)
        mom[k % 2, :, at] = (m[k % 2, :, at] + g[k % 2, :, at].astype(F32)) - (1.0 - 0.95) * low_rank
        scaled = split(o * (s * (D * columns / RANK) ** 0.5))
        up[k % 2, :, at] = dot3(scaled, (high, low), NT).astype(BF16)

    def send(k):
        pairs = ((ms_out, mom_s), (us_out, up_s), (bs_out, basis_s)) if k < 2 else (
            (mn_out, mom_n), (un_out, up_n), (bn_out, basis_n))
        for i, (source, target) in enumerate(pairs):
            copies.append(pltpu.make_async_copy(source.at[k % 2], target.at[k % 2], sem.at[i, k]))
            copies[-1].start()

    pieces = (r0, r1, r2, r3)
    for k in range(2):
        for j, piece in enumerate(pieces):
            at = pl.ds(pl.multiple_of((q ^ j) * 256, 256), 256)
            one(k, piece[:, k * SQ:(k + 1) * SQ, :].reshape(8 * SQ, RANK), at)
        send(k)
    for j, piece in enumerate(pieces):
        narrow[pl.ds(pl.multiple_of((q ^ j) * 64, 64), 64), :] = piece[:, 2 * SQ:, :].reshape(8 * NA, RANK)
    for k in range(2, 4):
        one(k, narrow[(k - 2) * 128:(k - 1) * 128, :], slice(0, 128))
        send(k)
    for copy in copies:
        copy.wait()


def partners():
    def pair(i, core, n):
        return ((i - core) % n ^ 1) + core

    def perm(move):
        at = [(i // 32, i // 8 % 4, i // 2 % 4, i % 2) for i in range(256)]
        out = []
        for i, (z, y, x, core) in enumerate(at):
            z, y = move(z, y, core)
            out.append((i, z % 8 * 32 + y % 4 * 8 + x * 2 + core))
        return out

    near_z = lambda z, core: pair(z, core, 8)
    near_y = lambda y, core: pair(y, core, 4)
    far_z = lambda z, core: pair(z // 2, core, 4) * 2 + z % 2
    near = [
        perm(lambda z, y, c: (z, near_y(y, c))),
        perm(lambda z, y, c: (near_z(z, c), y)),
        perm(lambda z, y, c: (near_z(z, c), near_y(y, c))),
    ]
    far = [
        perm(lambda z, y, c: (z, y + 2)),
        perm(lambda z, y, c: (far_z(z, c), y)),
        perm(lambda z, y, c: (far_z(z, c), y + 2)),
    ]
    return near, far, perm(lambda z, y, c: (z + 4, y))


def around_x(value):
    got = {0: value}
    for d in (2, 1, 3):
        got[d] = lax.ppermute(value, "x", [(i, (i + d) % 4) for i in range(4)])
    return [got[d] for d in range(4)]


def swap_core(value):
    return lax.ppermute(value, "core", [(0, 1), (1, 0)])


def local(mom_square, grad_square, basis_square, mom_narrow, grad_narrow, basis_narrow):
    zh, yh = lax.axis_index("zh"), lax.axis_index("yh")
    a, b = zh // 2, zh % 2
    q = lax.axis_index("zl") * 2 + lax.axis_index("yl")
    place = jnp.stack([lax.axis_index("core"), lax.axis_index("x"), q, b, yh]).astype(jnp.int32)
    near, far, across = partners()
    send = lambda value, pairs: lax.ppermute(value, AXES, pairs)
    spread = lambda value, axes, n: lax.all_to_all(jnp.broadcast_to(value[None], (n,) + value.shape), axes, 0, 0)
    inputs = (mom_square, grad_square, basis_square, mom_narrow, grad_narrow, basis_narrow)

    mine, theirs = call(
        project_kernel,
        [((4, 4, 32, RANK), F32)] * 2,
        (place,) + inputs,
        [pltpu.VMEM((4, 256, RANK), F32)]
        + [pltpu.VMEM(v.shape, v.dtype) for v in inputs]
        + [pltpu.SemaphoreType.DMA((6, 2))],
        name="project",
        far_in=range(1, 7),
    )
    half = mine + swap_core(theirs)
    part = jnp.sum(lax.all_to_all(half, "x", 0, 0), axis=0)
    own_half = spread(part, "x", 4)
    other_half = swap_core(own_half)

    left, gram, own, *others = call(
        back_kernel,
        [((4, 256, RANK), F32), ((32, 8, RANK), F32)] + [((8, CHUNK, RANK), F32)] * 4,
        (place, mom_square, grad_square, mom_narrow, grad_narrow, own_half, other_half),
        [pltpu.VMEM((32, CHUNK, RANK), F32)],
        name="back",
    )
    got = [send(value, pairs) for value, pairs in zip(others, near)]
    gram, got = lax.optimization_barrier((jnp.sum(lax.all_to_all(gram, ROWS, 0, 0), axis=0), got))
    own = (own + got[0] + got[1] + got[2]).reshape(2, 2, 2, CHUNK, RANK)
    take = lambda i, j: lax.dynamic_slice(own, (0, i, j, 0, 0), (2, 1, 1, CHUNK, RANK)).reshape(2, CHUNK, RANK)
    got = [send(value, pairs) for value, pairs in zip((take(b, 1 - yh), take(1 - b, yh), take(1 - b, 1 - yh)), far)]
    gram, got = lax.optimization_barrier((spread(gram, ROWS, 32), got))
    own = take(b, yh) + got[0] + got[1] + got[2]
    got = send(lax.dynamic_index_in_dim(own, 1 - a, 0, keepdims=False), across)
    (blocks,) = call(
        factor_kernel,
        [((3, 128, 128), F32)],
        (place, gram.reshape(RANK, RANK)),
        [pltpu.VMEM((RANK, 2 * RANK), F32)],
        name="factor",
    )
    blocks, got = lax.optimization_barrier((blocks, got))
    own = lax.dynamic_index_in_dim(own, a, 0, keepdims=False) + got
    got = send(own, across)
    pair = jnp.where(a == 0, jnp.stack([own, got]), jnp.stack([got, own]))
    pairs = [pair] + [send(pair, p) for p in far]
    around = around_x(blocks)
    inverse = pltpu.VMEM((4, RANK, RANK), F32)
    right, squares = call(
        right_kernel,
        [((8, CHUNK, RANK), F32), ((8, RANK), F32)],
        (place, *pairs, *around),
        [inverse, pltpu.VMEM((8, CHUNK, RANK), F32)],
        name="right",
    )
    rights = [right] + [send(right, p) for p in near]
    squares = jnp.sum(spread(squares, ("zl", "yl", "x", "core"), 32), axis=0)
    (ortho,) = call(ortho_kernel, [((4, 256, RANK), F32)], (place, *around, left), [inverse], name="ortho")
    outs = [(v.shape, d) for v, d in zip(
        (mom_square, mom_square, basis_square, mom_narrow, mom_narrow, basis_narrow), (F32, BF16, F32) * 2)]
    return tuple(call(
        finish_kernel,
        outs,
        (place, *rights, squares, ortho, mom_square, grad_square, mom_narrow, grad_narrow),
        [pltpu.VMEM(*o) for o in outs] + [pltpu.VMEM((256, RANK), F32), pltpu.SemaphoreType.DMA((3, 4))],
        name="finish",
        far_out=range(6),
    ))


def solution(mesh):
    fine = Mesh(mesh.devices.reshape(4, 2, 2, 2, 4, 2), AXES)
    matrix, factor = P(None, ROWS, COLS), P(None, COLS, None)
    return jax.shard_map(
        local,
        mesh=fine,
        in_specs=(matrix, matrix, factor) * 2,
        out_specs=(matrix, matrix, factor) * 2,
        check_vma=False,
    )
```

time: 164 us -> 175 us (1.067)
  blocking collectives: 69.6 us -> 23.3 us
  starting transfers between devices: 29.8 us -> 57.3 us
  local copies, waits for them, and re-layouts: 1.11 us -> 13.8 us
  waiting for transfers between devices: 31.2 us -> 41.8 us
  other arithmetic: 0.4 us -> 9.27 us
  Pallas kernels: 30.4 us -> 27.4 us
    all_to_all x3 -> x1, blocking collectives: 57.9 us -> 10.7 us  [local(): lax.all_to_all(jnp.broadcast_to(value[None], (n,) + value.shape), axes, 0...]
    all_to_all x1 -> x3, starting transfers between devices: 3.63 us -> 19.9 us  [the longest x2 12 us: local(): lax.all_to_all(jnp.broadcast_to(value[None], (n,) + value.shape), axes, 0...]
    ppermute x9 -> x14, starting transfers between devices: 18 us -> 29.8 us  [local(): send = lambda value, pairs: lax.ppermute(value, AXES, pairs)]
    unnamed x8 -> x32, local copies, waits for them, and re-layouts: 0.02 us -> 9.94 us
    ppermute x9 -> x14, waiting for transfers between devices: 14.8 us -> 20.9 us  [local(): send = lambda value, pairs: lax.ppermute(value, AXES, pairs)]
    all_to_all x1 -> x3, waiting for transfers between devices: 12.4 us -> 17.7 us  [the longest x1 12.3 us: local(): lax.all_to_all(gram, ROWS, 0, 0)]
    add x2 -> x3, other arithmetic: 0.18 us -> 4.47 us  [the longest x1 1.75 us: local(): own = (own + got[0] + got[1] + got[2]).reshape(2, 2, 2, CHUNK, RANK)]
    pallas_call x6, Pallas kernels: 30.4 us -> 27.4 us  [call(): pl.pallas_call(kernel, out_shape=[jax.ShapeDtypeStruct(s, d) for s, d in...]
  transfers between devices with their start and end apart: 16 -> 22, of which waited for: 8 -> 10; matrix products, arithmetic and copies ran while one was open for 1% -> 4% of each run, Pallas kernels for 9% -> 7%
where the time goes in v3:
time: 175 us; the launch traced here: 174 us
  starting transfers between devices  57.3 us (33%)
  waiting for transfers between devices  41.8 us (24%)
  Pallas kernels  27.4 us (16%)
  blocking collectives  23.3 us (13%)
  local copies, waits for them, and re-layouts  13.8 us (8%)
  other arithmetic  9.27 us (5%)
    ppermute x14, starting transfers between devices, local(): send = lambda value, pairs: lax.ppermute(value, AXES, pairs)  29.8 us
    pallas_call x6, Pallas kernels, call(): pl.pallas_call(kernel, out_shape=[jax.ShapeDtypeStruct(s, d) for s, d in...  27.4 us
    ppermute x14, waiting for transfers between devices, local(): send = lambda value, pairs: lax.ppermute(value, AXES, pairs)  20.9 us
    all_to_all x1, blocking collectives, local(): part = jnp.sum(lax.all_to_all(half, 'x', 0, 0), axis=0)  12.6 us
    all_to_all x1, waiting for transfers between devices, local(): lax.all_to_all(gram, ROWS, 0, 0)  12.3 us
    all_to_all x2, starting transfers between devices, local(): lax.all_to_all(jnp.broadcast_to(value[None], (n,) + value.shape), axes, 0...  12 us
    all_to_all x1, blocking collectives, local(): lax.all_to_all(jnp.broadcast_to(value[None], (n,) + value.shape), axes, 0...  10.7 us
    unnamed x32, local copies, waits for them, and re-layouts  9.94 us
  transfers between devices with their start and end apart: 22, of which 10 were waited for; matrix products, arithmetic and copies ran while one was open for 4% of the time, Pallas kernels for 7%

profile of v3, /device:TPU:1, one launch (start us, length us, event | category | flops | bytes accessed | tf_op | source)
XLA Modules:
  0.0 173.9 jit_solution(15740939939302243378)
XLA Ops:
  0.7 0.1 stack.37.place
  0.7 4.7 %project.1 = (f32[4,4,32,256]{3,2,1,0:T(8,128)S(1)}, f32[4,4,32,256]{3,2,1,0:T(8,128)S(1)}) custom-call(s32[5]{0:T(128)S(1)} %stack.37.place, f32[2,256,1024]{2,1,0:T(8,128)} %ms.5, bf16[2,256,1024]{2,1,0:T(8,128)(2,1)} %gs.5, f32[2,1024,256]{2,1,0:T(8,128)} %qs.1, f32[2,256,128]{2,1,0:T(8,128)} %mn.5, bf16[2,256,128]{2,1,0:T(8,128)(2,1)} %gn.5, ...), custom_call_target="tpu_custom_call" | custom-call | tf_op jit(solution)/shard_map/project/pallas_call | solution.py:39
  5.4 3.3 %collective-permute-start = (f32[4,4,32,256]{3,2,1,0:T(8,128)S(1)}, f32[4,4,32,256]{3,2,1,0:T(8,128)S(1)}, u32[]{:S(2)}, u32[]{:S(2)}) collective-permute-start(f32[4,4,32,256]{3,2,1,0:T(8,128)S(1)} %get-tuple-element.27), channel_id=1, source_target_pairs={{0,1},{1,0},{2,3},{3,2},{4,5},{5,4},{6,7},{7,6},{8,9},{9,8},{10,11... | collective-permute-start | bytes 1572872 | tf_op jit(solution)/shard_map/ppermute | solution.py:242
  8.8 1.5 collective-permute-done
  10.3 0.1 add.60
  10.4 0.0 copy-start
  10.4 12.6 %all_to_all.25 = f32[4,4,32,256]{3,2,1,0:T(8,128)} all-to-all(f32[4,4,32,256]{3,2,1,0:T(8,128)S(1)} %add.60), channel_id=1, replica_groups=mesh['zh'=4,'zl'=2,'yh'=2,'yl'=2,'x'=4,'core'=2] {'x'}, dimensions={0} | all-to-all | bytes 1048576 | tf_op jit(solution)/shard_map/all_to_all | solution.py:266
  23.0 1.7 %reduce_sum.27 = f32[4,32,256]{2,1,0:T(8,128)} reduce(f32[4,4,32,256]{3,2,1,0:T(8,128)} %all_to_all.25, f32[]{:T(128)} %constant.59.clone.1), dimensions={0}, to_apply=%region_0.1 | reduce | flops 98304 | bytes 655364 | tf_op jit(solution)/shard_map/reduce_sum | solution.py:266
  24.7 0.9 broadcast_in_dim.6
  25.7 10.7 %all_to_all.26.own_half = f32[4,4,32,256]{3,2,1,0:T(8,128)S(1)} all-to-all(f32[4,4,32,256]{3,2,1,0:T(8,128)S(1)} %broadcast_in_dim.6), channel_id=1, replica_groups=mesh['zh'=4,'zl'=2,'yh'=2,'yl'=2,'x'=4,'core'=2] {'x'}, dimensions={0} | all-to-all | bytes 1048576 | tf_op jit(solution)/shard_map/all_to_all | solution.py:252
  36.4 2.1 %collective-permute-start.1 = (f32[4,4,32,256]{3,2,1,0:T(8,128)S(1)}, f32[4,4,32,256]{3,2,1,0:T(8,128)S(1)}, u32[]{:S(2)}, u32[]{:S(2)}) collective-permute-start(f32[4,4,32,256]{3,2,1,0:T(8,128)S(1)} %all_to_all.26.own_half), channel_id=1, source_target_pairs={{0,1},{1,0},{2,3},{3,2},{4,5},{5,4},{6,7},{7,6},{8,9},{9,8},{10,11... | collective-permute-start | bytes 1572872 | tf_op jit(solution)/shard_map/ppermute | solution.py:242
  38.5 1.5 collective-permute-done.1.other_half
  40.1 3.3 %back.1 = (f32[4,256,256]{2,1,0:T(8,128)S(1)}, f32[32,8,256]{2,1,0:T(8,128)S(1)}, f32[8,72,256]{2,1,0:T(8,128)S(1)}, f32[8,72,256]{2,1,0:T(8,128)}, f32[8,72,256]{2,1,0:T(8,128)}, /*index=5*/f32[8,72,256]{2,1,0:T(8,128)}) custom-call(s32[5]{0:T(128)S(1)} %stack.37.place, f32[2,256,1024]{2,1,0:T(8,128)S(1)} %copy-done, bf16[2,256,1024]{2,1,0:T(8,128)(2,1)S(1)} %copy-done.1, ...), custom_call_target="tpu_custom_call" | custom-call | tf_op jit(solution)/shard_map/back/pallas_call | solution.py:39
  43.4 1.0 copy-done.6
  44.3 0.8 copy-done.12
  45.2 0.7 copy-done.13
  45.9 1.2 collective-permute-start.2
  47.1 5.6 %collective-permute-start.3 = (f32[8,72,256]{2,1,0:T(8,128)}, f32[8,72,256]{2,1,0:T(8,128)}, u32[]{:S(2)}, u32[]{:S(2)}) collective-permute-start(f32[8,72,256]{2,1,0:T(8,128)} %get-tuple-element.31), channel_id=1, source_target_pairs={{0,32},{1,225},{2,34},{3,227},{4,36},{5,229},{6,38},{7,231},{8,40}... | collective-permute-start | bytes 1769480 | tf_op jit(solution)/shard_map/ppermute | solution.py:251
  52.7 7.9 %all-to-all-start.2 = ((f32[32,8,256]{2,1,0:T(8,128)}), f32[32,8,256]{2,1,0:T(8,128)}, u32[]{:S(2)}, u32[]{:S(2)}) async-start(f32[32,8,256]{2,1,0:T(8,128)} %copy-done.13), calls=%async_computation.2 | async-start | bytes 524288 | tf_op jit(solution)/shard_map/all_to_all | solution.py:278
  60.6 12.3 %all-to-all-done.2 = f32[32,8,256]{2,1,0:T(8,128)} async-done(((f32[32,8,256]{2,1,0:T(8,128)}), f32[32,8,256]{2,1,0:T(8,128)}, u32[]{:S(2)}, u32[]{:S(2)}) %all-to-all-start.2) | async-done | bytes 262176 | tf_op jit(solution)/shard_map/all_to_all | solution.py:278
  72.9 1.0 reduce_sum.28
  74.0 0.7 broadcast_in_dim.7
  74.7 7.6 %all-to-all-start.3 = ((f32[32,8,256]{2,1,0:T(8,128)}), f32[32,8,256]{2,1,0:T(8,128)}, u32[]{:S(2)}, u32[]{:S(2)}) async-start(f32[32,8,256]{2,1,0:T(8,128)} %broadcast_in_dim.7), calls=%async_computation.3 | async-start | bytes 524288 | tf_op jit(solution)/shard_map/all_to_all | solution.py:252
  82.3 1.8 %add_add_fusion = f32[8,72,256]{2,1,0:T(8,128)S(1)} fusion(f32[8,72,256]{2,1,0:T(8,128)} %collective-permute-done.4, f32[8,72,256]{2,1,0:T(8,128)} %collective-permute-done.3, f32[8,72,256]{2,1,0:T(8,128)} %copy-done.12, f32[8,72,256]{2,1,0:T(8,128)} %collective-permute-done.2), kind=kLoop, calls=%fused_computation | loop fusion | flops 442368 | bytes 2949120 | tf_op jit(solution)/shard_map/add | solution.py:279
  84.0 0.8 copy-done.14
  84.8 0.8 dynamic-slice_bitcast_fusion
  85.6 5.7 %collective-permute-start.7 = (f32[2,72,256]{2,1,0:T(8,128)}, f32[2,72,256]{2,1,0:T(8,128)}, u32[]{:S(2)}, u32[]{:S(2)}) collective-permute-start(f32[2,72,256]{2,1,0:T(8,128)} %get-tuple-element.46), channel_id=1, source_target_pairs={{0,80},{1,209},{2,82},{3,211},{4,84},{5,213},{6,86},{7,215},{8,88}... | collective-permute-start | bytes 442376 | tf_op jit(solution)/shard_map/ppermute | solution.py:251
  91.3 0.2 collective-permute-start.6
  91.6 0.3 collective-permute-start.5
  91.9 6.2 %collective-permute-done.7 = f32[2,72,256]{2,1,0:T(8,128)} collective-permute-done((f32[2,72,256]{2,1,0:T(8,128)}, f32[2,72,256]{2,1,0:T(8,128)}, u32[]{:S(2)}, u32[]{:S(2)}) %collective-permute-start.7) | collective-permute-done | bytes 147488 | tf_op jit(solution)/shard_map/ppermute | solution.py:251
  98.1 1.0 collective-permute-done.6
  99.1 1.2 collective-permute-done.5
  100.2 1.2 fusion.1
  101.4 0.7 copy-done.15
  102.1 0.6 dynamic-slice_bitcast_fusion.3
  102.7 4.5 %collective-permute-start.8 = (f32[72,256]{1,0:T(8,128)}, f32[72,256]{1,0:T(8,128)}, u32[]{:S(2)}, u32[]{:S(2)}) collective-permute-start(f32[72,256]{1,0:T(8,128)} %dynamic-slice_bitcast_fusion.3), channel_id=1, source_target_pairs={{0,128},{1,129},{2,130},{3,131},{4,132},{5,133},{6,134},{7,135},{8... | collective-permute-start | bytes 221192 | tf_op jit(solution)/shard_map/ppermute | solution.py:251
  107.2 10.1 %factor.1.l0 = f32[3,128,128]{2,1,0:T(8,128)} custom-call(s32[5]{0:T(128)S(1)} %stack.37.place, f32[256,256]{1,0:T(8,128)} %bitcast.11.gram), custom_call_target="tpu_custom_call" | custom-call | tf_op jit(solution)/shard_map/factor/pallas_call | solution.py:39
  117.3 0.9 collective-permute-start.15
  118.2 1.6 bitcast_add_fusion.1
  119.7 0.9 collective-permute-start.9
  120.6 1.2 collective-permute-start.14
  121.8 5.4 %collective-permute-done.9 = f32[72,256]{1,0:T(8,128)} collective-permute-done((f32[72,256]{1,0:T(8,128)}, f32[72,256]{1,0:T(8,128)}, u32[]{:S(2)}, u32[]{:S(2)}) %collective-permute-start.9) | collective-permute-done | bytes 73760 | tf_op jit(solution)/shard_map/ppermute | solution.py:251
  127.2 1.0 maximum_select_fusion.w0
  128.2 4.3 %collective-permute-start.12 = (f32[2,72,256]{2,1,0:T(8,128)S(1)}, f32[2,72,256]{2,1,0:T(8,128)S(1)}, u32[]{:S(2)}, u32[]{:S(2)}) collective-permute-start(f32[2,72,256]{2,1,0:T(8,128)S(1)} %maximum_select_fusion.w0), channel_id=1, source_target_pairs={{0,80},{1,209},{2,82},{3,211},{4,84},{5,213},{6,86},{7,215},{8,88}... | collective-permute-start | bytes 442376 | tf_op jit(solution)/shard_map/ppermute | solution.py:251
  132.5 1.7 collective-permute-start.11
  134.2 0.4 collective-permute-start.10
  134.6 2.3 %collective-permute-done.12.w3 = f32[2,72,256]{2,1,0:T(8,128)S(1)} collective-permute-done((f32[2,72,256]{2,1,0:T(8,128)S(1)}, f32[2,72,256]{2,1,0:T(8,128)S(1)}, u32[]{:S(2)}, u32[]{:S(2)}) %collective-permute-start.12) | collective-permute-done | bytes 147488 | tf_op jit(solution)/shard_map/ppermute | solution.py:251
  136.9 4.9 %collective-permute-done.11.w2 = f32[2,72,256]{2,1,0:T(8,128)S(1)} collective-permute-done((f32[2,72,256]{2,1,0:T(8,128)S(1)}, f32[2,72,256]{2,1,0:T(8,128)S(1)}, u32[]{:S(2)}, u32[]{:S(2)}) %collective-permute-start.11) | collective-permute-done | bytes 147488 | tf_op jit(solution)/shard_map/ppermute | solution.py:251
  141.8 2.5 %right.1 = (f32[8,72,256]{2,1,0:T(8,128)}, f32[8,256]{1,0:T(8,128)S(1)}) custom-call(s32[5]{0:T(128)S(1)} %stack.37.place, f32[2,72,256]{2,1,0:T(8,128)S(1)} %maximum_select_fusion.w0, f32[2,72,256]{2,1,0:T(8,128)S(1)} %collective-permute-done.10.w1, f32[2,72,256]{2,1,0:T(8,128)S(1)} %collective-permute-done.11.w2, ...), custom_call_target="tpu_custom_call" | custom-call | tf_op jit(solution)/shard_map/right/pallas_call | solution.py:39
  144.2 0.7 copy-done.8
  144.9 1.2 collective-permute-start.18
  146.1 2.6 %collective-permute-start.17 = (f32[8,72,256]{2,1,0:T(8,128)}, f32[8,72,256]{2,1,0:T(8,128)}, u32[]{:S(2)}, u32[]{:S(2)}) collective-permute-start(f32[8,72,256]{2,1,0:T(8,128)} %get-tuple-element.43.r0), channel_id=1, source_target_pairs={{0,32},{1,225},{2,34},{3,227},{4,36},{5,229},{6,38},{7,231},{8,40}... | collective-permute-start | bytes 1769480 | tf_op jit(solution)/shard_map/ppermute | solution.py:251
  148.7 1.3 collective-permute-start.16
  150.0 0.7 broadcast_in_dim.8
  150.7 4.4 %all-to-all-start.4 = ((f32[32,8,256]{2,1,0:T(8,128)}), f32[32,8,256]{2,1,0:T(8,128)}, u32[]{:S(2)}, u32[]{:S(2)}) async-start(f32[32,8,256]{2,1,0:T(8,128)} %broadcast_in_dim.8), calls=%async_computation.4 | async-start | bytes 524288 | tf_op jit(solution)/shard_map/all_to_all | solution.py:252
  155.1 1.2 copy-done.7
  156.3 0.9 copy-done.9
  157.2 0.9 copy-done.11
  158.2 1.8 %ortho.1 = f32[4,256,256]{2,1,0:T(8,128)S(1)} custom-call(s32[5]{0:T(128)S(1)} %stack.37.place, f32[3,128,128]{2,1,0:T(8,128)} %factor.1.l0, f32[3,128,128]{2,1,0:T(8,128)S(1)} %copy-done.11, f32[3,128,128]{2,1,0:T(8,128)S(1)} %copy-done.9, f32[3,128,128]{2,1,0:T(8,128)} %collective-permute-done.15.l3, f32[4,256,256]{2,1,0:T(8,128)S(1)} %copy-done.7), custom_call_target="tpu_custom_call" | custom-call | tf_op jit(solution)/shard_map/ortho/pallas_call | solution.py:39
  160.0 1.0 copy-done.2
  161.0 5.4 %all-to-all-done.4 = f32[32,8,256]{2,1,0:T(8,128)} async-done(((f32[32,8,256]{2,1,0:T(8,128)}), f32[32,8,256]{2,1,0:T(8,128)}, u32[]{:S(2)}, u32[]{:S(2)}) %all-to-all-start.4) | async-done | bytes 262176 | tf_op jit(solution)/shard_map/all_to_all | solution.py:252
  166.4 1.0 reduce_sum.29.squares
  167.4 1.2 copy-done.3
  168.6 5.1 %finish.1 = (f32[2,256,1024]{2,1,0:T(8,128)}, bf16[2,256,1024]{2,1,0:T(8,128)(2,1)}, f32[2,1024,256]{2,1,0:T(8,128)}, f32[2,256,128]{2,1,0:T(8,128)}, bf16[2,256...) custom-call(s32[5]{0:T(128)S(1)} %stack.37.place, f32[8,72,256]{2,1,0:T(8,128)} %get-tuple-element.43.r0, ...), custom_call_target="tpu_custom_call" | custom-call | tf_op jit(solution)/shard_map/finish/pallas_call | solution.py:39
  (34 shorter events, 0.1 us)
Async XLA Ops:
  5.4 4.9 %collective-permute-start = (f32[4,4,32,256]{3,2,1,0:T(8,128)S(1)}, f32[4,4,32,256]{3,2,1,0:T(8,128)S(1)}, u32[]{:S(2)}, u32[]{:S(2)}) collective-permute-start(f32[4,4,32,256]{3,2,1,0:T(8,128)S(1)} %get-tuple-element.27), channel_id=1, source_target_pairs={{0,1},{1,0},{2,3},{3,2},{4,5},{5,4},{6,7},{7,6},{8,9},{9,8},{10,11... | collective-permute-start | bytes 1572872 | tf_op jit(solution)/shard_map/ppermute | solution.py:242
  10.3 29.8 %copy-start.5 = (bf16[2,256,128]{2,1,0:T(8,128)(2,1)S(1)}, bf16[2,256,128]{2,1,0:T(8,128)(2,1)}, u32[]{:S(2)}) copy-start(bf16[2,256,128]{2,1,0:T(8,128)(2,1)} %gn.5) | copy-start | bytes 393220
  10.4 29.7 %copy-start = (f32[2,256,1024]{2,1,0:T(8,128)S(1)}, f32[2,256,1024]{2,1,0:T(8,128)}, u32[]{:S(2)}) copy-start(f32[2,256,1024]{2,1,0:T(8,128)} %ms.5) | copy-start | bytes 6291460
  10.4 29.7 %copy-start.1 = (bf16[2,256,1024]{2,1,0:T(8,128)(2,1)S(1)}, bf16[2,256,1024]{2,1,0:T(8,128)(2,1)}, u32[]{:S(2)}) copy-start(bf16[2,256,1024]{2,1,0:T(8,128)(2,1)} %gs.5) | copy-start | bytes 3145732
  10.4 29.7 %copy-start.4 = (f32[2,256,128]{2,1,0:T(8,128)S(1)}, f32[2,256,128]{2,1,0:T(8,128)}, u32[]{:S(2)}) copy-start(f32[2,256,128]{2,1,0:T(8,128)} %mn.5) | copy-start | bytes 786436
  36.4 3.7 %collective-permute-start.1 = (f32[4,4,32,256]{3,2,1,0:T(8,128)S(1)}, f32[4,4,32,256]{3,2,1,0:T(8,128)S(1)}, u32[]{:S(2)}, u32[]{:S(2)}) collective-permute-start(f32[4,4,32,256]{3,2,1,0:T(8,128)S(1)} %all_to_all.26.own_half), channel_id=1, source_target_pairs={{0,1},{1,0},{2,3},{3,2},{4,5},{5,4},{6,7},{7,6},{8,9},{9,8},{10,11... | collective-permute-start | bytes 1572872 | tf_op jit(solution)/shard_map/ppermute | solution.py:242
  43.3 1.0 copy-start.6
  44.3 0.8 copy-start.12
  45.2 0.7 copy-start.13
  45.9 28.1 %collective-permute-start.2 = (f32[8,72,256]{2,1,0:T(8,128)}, f32[8,72,256]{2,1,0:T(8,128)}, u32[]{:S(2)}, u32[]{:S(2)}) collective-permute-start(f32[8,72,256]{2,1,0:T(8,128)} %get-tuple-element.30), channel_id=1, source_target_pairs={{0,8},{1,25},{2,10},{3,27},{4,12},{5,29},{6,14},{7,31},{8,0},{9,17... | collective-permute-start | bytes 1769480 | tf_op jit(solution)/shard_map/ppermute | solution.py:251
  47.1 26.9 %collective-permute-start.3 = (f32[8,72,256]{2,1,0:T(8,128)}, f32[8,72,256]{2,1,0:T(8,128)}, u32[]{:S(2)}, u32[]{:S(2)}) collective-permute-start(f32[8,72,256]{2,1,0:T(8,128)} %get-tuple-element.31), channel_id=1, source_target_pairs={{0,32},{1,225},{2,34},{3,227},{4,36},{5,229},{6,38},{7,231},{8,40}... | collective-permute-start | bytes 1769480 | tf_op jit(solution)/shard_map/ppermute | solution.py:251
  52.7 21.3 %collective-permute-start.4 = (f32[8,72,256]{2,1,0:T(8,128)}, f32[8,72,256]{2,1,0:T(8,128)}, u32[]{:S(2)}, u32[]{:S(2)}) collective-permute-start(f32[8,72,256]{2,1,0:T(8,128)} %get-tuple-element.32), channel_id=1, source_target_pairs={{0,40},{1,249},{2,42},{3,251},{4,44},{5,253},{6,46},{7,255},{8,32}... | collective-permute-start | bytes 1769480 | tf_op jit(solution)/shard_map/ppermute | solution.py:251
  52.7 20.3 %all-to-all-start.2 = ((f32[32,8,256]{2,1,0:T(8,128)}), f32[32,8,256]{2,1,0:T(8,128)}, u32[]{:S(2)}, u32[]{:S(2)}) async-start(f32[32,8,256]{2,1,0:T(8,128)} %copy-done.13), calls=%async_computation.2 | async-start | bytes 524288 | tf_op jit(solution)/shard_map/all_to_all | solution.py:278
  74.7 25.5 %all-to-all-start.3 = ((f32[32,8,256]{2,1,0:T(8,128)}), f32[32,8,256]{2,1,0:T(8,128)}, u32[]{:S(2)}, u32[]{:S(2)}) async-start(f32[32,8,256]{2,1,0:T(8,128)} %broadcast_in_dim.7), calls=%async_computation.3 | async-start | bytes 524288 | tf_op jit(solution)/shard_map/all_to_all | solution.py:252
  84.0 0.8 copy-start.14
  85.6 12.5 %collective-permute-start.7 = (f32[2,72,256]{2,1,0:T(8,128)}, f32[2,72,256]{2,1,0:T(8,128)}, u32[]{:S(2)}, u32[]{:S(2)}) collective-permute-start(f32[2,72,256]{2,1,0:T(8,128)} %get-tuple-element.46), channel_id=1, source_target_pairs={{0,80},{1,209},{2,82},{3,211},{4,84},{5,213},{6,86},{7,215},{8,88}... | collective-permute-start | bytes 442376 | tf_op jit(solution)/shard_map/ppermute | solution.py:251
  91.3 7.7 %collective-permute-start.6 = (f32[2,72,256]{2,1,0:T(8,128)}, f32[2,72,256]{2,1,0:T(8,128)}, u32[]{:S(2)}, u32[]{:S(2)}) collective-permute-start(f32[2,72,256]{2,1,0:T(8,128)} %get-tuple-element.47), channel_id=1, source_target_pairs={{0,64},{1,193},{2,66},{3,195},{4,68},{5,197},{6,70},{7,199},{8,72}... | collective-permute-start | bytes 442376 | tf_op jit(solution)/shard_map/ppermute | solution.py:251
  91.6 8.7 %collective-permute-start.5 = (f32[2,72,256]{2,1,0:T(8,128)}, f32[2,72,256]{2,1,0:T(8,128)}, u32[]{:S(2)}, u32[]{:S(2)}) collective-permute-start(f32[2,72,256]{2,1,0:T(8,128)} %get-tuple-element.48), channel_id=1, source_target_pairs={{0,16},{1,17},{2,18},{3,19},{4,20},{5,21},{6,22},{7,23},{8,24},{9,... | collective-permute-start | bytes 442376 | tf_op jit(solution)/shard_map/ppermute | solution.py:251
  101.4 0.7 copy-start.15
  102.7 14.6 %collective-permute-start.8 = (f32[72,256]{1,0:T(8,128)}, f32[72,256]{1,0:T(8,128)}, u32[]{:S(2)}, u32[]{:S(2)}) collective-permute-start(f32[72,256]{1,0:T(8,128)} %dynamic-slice_bitcast_fusion.3), channel_id=1, source_target_pairs={{0,128},{1,129},{2,130},{3,131},{4,132},{5,133},{6,134},{7,135},{8... | collective-permute-start | bytes 221192 | tf_op jit(solution)/shard_map/ppermute | solution.py:251
  117.3 16.9 %collective-permute-start.15 = (f32[3,128,128]{2,1,0:T(8,128)}, f32[3,128,128]{2,1,0:T(8,128)}, u32[]{:S(2)}, u32[]{:S(2)}) collective-permute-start(f32[3,128,128]{2,1,0:T(8,128)} %factor.1.l0), channel_id=1, source_target_pairs={{0,6},{2,0},{4,2},{6,4},{1,7},{3,1},{5,3},{7,5},{8,14},{10,8},{12,... | collective-permute-start | bytes 589832 | tf_op jit(solution)/shard_map/ppermute | solution.py:237
  119.7 7.5 %collective-permute-start.9 = (f32[72,256]{1,0:T(8,128)}, f32[72,256]{1,0:T(8,128)}, u32[]{:S(2)}, u32[]{:S(2)}) collective-permute-start(f32[72,256]{1,0:T(8,128)} %bitcast_add_fusion.1), channel_id=1, source_target_pairs={{0,128},{1,129},{2,130},{3,131},{4,132},{5,133},{6,134},{7,135},{8... | collective-permute-start | bytes 221192 | tf_op jit(solution)/shard_map/ppermute | solution.py:251
  120.6 13.9 %collective-permute-start.14 = (f32[3,128,128]{2,1,0:T(8,128)}, f32[3,128,128]{2,1,0:T(8,128)S(1)}, u32[]{:S(2)}, u32[]{:S(2)}) collective-permute-start(f32[3,128,128]{2,1,0:T(8,128)} %factor.1.l0), channel_id=1, source_target_pairs={{0,4},{2,6},{4,0},{6,2},{1,5},{3,7},{5,1},{7,3},{8,12},{10,14},{12... | collective-permute-start | bytes 589832 | tf_op jit(solution)/shard_map/ppermute | solution.py:237
  121.8 12.8 %collective-permute-start.13 = (f32[3,128,128]{2,1,0:T(8,128)}, f32[3,128,128]{2,1,0:T(8,128)S(1)}, u32[]{:S(2)}, u32[]{:S(2)}) collective-permute-start(f32[3,128,128]{2,1,0:T(8,128)} %factor.1.l0), channel_id=1, source_target_pairs={{0,2},{2,4},{4,6},{6,0},{1,3},{3,5},{5,7},{7,1},{8,10},{10,12},{12... | collective-permute-start | bytes 589832 | tf_op jit(solution)/shard_map/ppermute | solution.py:237
  128.2 8.7 %collective-permute-start.12 = (f32[2,72,256]{2,1,0:T(8,128)S(1)}, f32[2,72,256]{2,1,0:T(8,128)S(1)}, u32[]{:S(2)}, u32[]{:S(2)}) collective-permute-start(f32[2,72,256]{2,1,0:T(8,128)S(1)} %maximum_select_fusion.w0), channel_id=1, source_target_pairs={{0,80},{1,209},{2,82},{3,211},{4,84},{5,213},{6,86},{7,215},{8,88}... | collective-permute-start | bytes 442376 | tf_op jit(solution)/shard_map/ppermute | solution.py:251
  132.5 9.3 %collective-permute-start.11 = (f32[2,72,256]{2,1,0:T(8,128)S(1)}, f32[2,72,256]{2,1,0:T(8,128)S(1)}, u32[]{:S(2)}, u32[]{:S(2)}) collective-permute-start(f32[2,72,256]{2,1,0:T(8,128)S(1)} %maximum_select_fusion.w0), channel_id=1, source_target_pairs={{0,64},{1,193},{2,66},{3,195},{4,68},{5,197},{6,70},{7,199},{8,72}... | collective-permute-start | bytes 442376 | tf_op jit(solution)/shard_map/ppermute | solution.py:251
  134.2 7.6 %collective-permute-start.10 = (f32[2,72,256]{2,1,0:T(8,128)S(1)}, f32[2,72,256]{2,1,0:T(8,128)S(1)}, u32[]{:S(2)}, u32[]{:S(2)}) collective-permute-start(f32[2,72,256]{2,1,0:T(8,128)S(1)} %maximum_select_fusion.w0), channel_id=1, source_target_pairs={{0,16},{1,17},{2,18},{3,19},{4,20},{5,21},{6,22},{7,23},{8,24},{9,... | collective-permute-start | bytes 442376 | tf_op jit(solution)/shard_map/ppermute | solution.py:251
  134.6 9.7 %copy-start.10 = (f32[3,128,128]{2,1,0:T(8,128)}, f32[3,128,128]{2,1,0:T(8,128)S(1)}, u32[]{:S(2)}) copy-start(f32[3,128,128]{2,1,0:T(8,128)S(1)} %collective-permute-done.13.l1) | copy-start | bytes 589828
  144.2 0.7 copy-start.8
  144.9 22.4 %collective-permute-start.18 = (f32[8,72,256]{2,1,0:T(8,128)}, f32[8,72,256]{2,1,0:T(8,128)}, u32[]{:S(2)}, u32[]{:S(2)}) collective-permute-start(f32[8,72,256]{2,1,0:T(8,128)} %get-tuple-element.43.r0), channel_id=1, source_target_pairs={{0,40},{1,249},{2,42},{3,251},{4,44},{5,253},{6,46},{7,255},{8,32}... | collective-permute-start | bytes 1769480 | tf_op jit(solution)/shard_map/ppermute | solution.py:251
  146.1 21.3 %collective-permute-start.17 = (f32[8,72,256]{2,1,0:T(8,128)}, f32[8,72,256]{2,1,0:T(8,128)}, u32[]{:S(2)}, u32[]{:S(2)}) collective-permute-start(f32[8,72,256]{2,1,0:T(8,128)} %get-tuple-element.43.r0), channel_id=1, source_target_pairs={{0,32},{1,225},{2,34},{3,227},{4,36},{5,229},{6,38},{7,231},{8,40}... | collective-permute-start | bytes 1769480 | tf_op jit(solution)/shard_map/ppermute | solution.py:251
  148.7 18.6 %collective-permute-start.16 = (f32[8,72,256]{2,1,0:T(8,128)}, f32[8,72,256]{2,1,0:T(8,128)}, u32[]{:S(2)}, u32[]{:S(2)}) collective-permute-start(f32[8,72,256]{2,1,0:T(8,128)} %get-tuple-element.43.r0), channel_id=1, source_target_pairs={{0,8},{1,25},{2,10},{3,27},{4,12},{5,29},{6,14},{7,31},{8,0},{9,17... | collective-permute-start | bytes 1769480 | tf_op jit(solution)/shard_map/ppermute | solution.py:251
  150.7 15.7 %all-to-all-start.4 = ((f32[32,8,256]{2,1,0:T(8,128)}), f32[32,8,256]{2,1,0:T(8,128)}, u32[]{:S(2)}, u32[]{:S(2)}) async-start(f32[32,8,256]{2,1,0:T(8,128)} %broadcast_in_dim.8), calls=%async_computation.4 | async-start | bytes 524288 | tf_op jit(solution)/shard_map/all_to_all | solution.py:252
  155.1 1.2 copy-start.7
  156.3 0.9 copy-start.9
  157.2 0.9 copy-start.11
  160.0 1.0 copy-start.2
  167.4 1.2 copy-start.3

commit v4 on v2

--- a/solution.py
+++ b/solution.py
@@ -16,11 +16,10 @@
 AXES = ("zh", "zl", "yh", "yl", "x", "core")
 ROWS = ("zh", "zl", "yh", "yl")
 COLS = ("x", "core")
-FAR = ("zh", "yh")
 NN = (((1,), (0,)), ((), ()))
 NT = (((1,), (1,)), ((), ()))
 TN = (((0,), (0,)), ((), ()))
-SQ, NA, GR = 32, 8, 8
+SQ, NA = 32, 8
 CHUNK = 2 * SQ + NA
 
 
@@ -44,7 +43,7 @@
         + [hbm if i in far_in else vmem for i in range(1, len(operands))],
         out_specs=[hbm if i in far_out else vmem for i in range(len(outs))],
         scratch_shapes=list(scratch),
-        compiler_params=pltpu.CompilerParams(vmem_limit_bytes=50 * 2**20),
+        compiler_params=pltpu.CompilerParams(vmem_limit_bytes=20 * 2**20),
         name=name,
     )(*[pltpu.with_memory_space_constraint(a, pltpu.HBM) if i in far_in else a for i, a in enumerate(operands)])
 
@@ -76,29 +75,52 @@
             theirs[x, k] = left[k, pl.ds(pl.multiple_of((1 - core) * 128 + x * 32, 32), 32), :]
 
 
-def back_kernel(place, ms, gs, mn, gn, own_half, other_half, left, own, to_y, to_z, to_d, w):
+def fetch(sources, targets, sem):
+    copies = [pltpu.make_async_copy(a, b, sem.at[i]) for i, (a, b) in enumerate(zip(sources, targets))]
+    for copy in copies:
+        copy.start()
+    return copies
+
+
+def back_kernel(place, ms, gs, mn, gn, own_half, other_half, left, own, to_y, to_z, to_d,
+                w, gram, ms_in, gs_in, mn_in, gn_in, sem):
+    copies = fetch((ms, gs, mn, gn), (ms_in, gs_in, mn_in, gn_in), sem)
     core, x, q = place[0], place[1], place[2]
     for i in range(4):
         for k in range(4):
             left[k, pl.ds(pl.multiple_of(core * 128 + i * 32, 32), 32), :] = own_half[i, k]
             left[k, pl.ds(pl.multiple_of((1 - core) * 128 + i * 32, 32), 32), :] = other_half[i, k]
+    half = left[x, :, pl.ds(pl.multiple_of(core * 128, 128), 128)]
+    gram[...] = dot3(split(half), split(left[x]), TN)
+    for copy in copies:
+        copy.wait()
     for k in range(2):
-        buffer = split(ms[k] + gs[k].astype(F32))
+        buffer = split(ms_in[k] + gs_in[k].astype(F32))
         w[:, k * SQ:(k + 1) * SQ, :] = dot3(buffer, split(left[k]), TN).reshape(32, SQ, RANK)
     for k in range(2):
-        buffer = split(mn[k] + gn[k].astype(F32))
-        w[k * 16:(k + 1) * 16, 2 * SQ:CHUNK, :] = dot3(buffer, split(left[2 + k]), TN).reshape(16, NA, RANK)
-    one = split(left[x])
-    w[:, CHUNK:, :] = dot3(one, one, TN).reshape(32, GR, RANK)
+        buffer = split(mn_in[k] + gn_in[k].astype(F32))
+        w[k * 16:(k + 1) * 16, 2 * SQ:, :] = dot3(buffer, split(left[2 + k]), TN).reshape(16, NA, RANK)
     for j, out in enumerate((own, to_y, to_z, to_d)):
-        out[...] = w[pl.ds((q ^ j) * 8, 8)]
+        out[:8 * CHUNK] = w[pl.ds((q ^ j) * 8, 8)].reshape(8 * CHUNK, RANK)
+        out[8 * CHUNK:] = gram[pl.ds(pl.multiple_of((q ^ j) * 32, 32), 32), :]
+
+
+def meet_kernel(place, own, r0, r1, r2, mine, to_y, to_z, to_d):
+    b, yh = place[3], place[4]
+    meet = lambda at: (own[at, :] + r0[at, :]) + (r1[at, :] + r2[at, :])
+    gram = meet(slice(8 * CHUNK, None))
+    for j, out in enumerate((mine, to_y, to_z, to_d)):
+        for a in range(2):
+            i = a * 4 + (b ^ (j >> 1)) * 2 + (yh ^ (j & 1))
+            out[a * CHUNK:(a + 1) * CHUNK] = meet(pl.ds(pl.multiple_of(i * CHUNK, CHUNK), CHUNK))
+        out[2 * CHUNK:] = gram
 
 
 def factor_kernel(place, g0, g1, g2, g3, out, w):
-    q = place[2]
     n, nb, step = RANK, 64, 8
     for j, g in enumerate((g0, g1, g2, g3)):
-        w[pl.ds(pl.multiple_of((q ^ j) * 64, 64), 64), :n] = g[...].reshape(64, n)
+        for half in range(2):
+            w[pl.ds(pl.multiple_of(half * 128 + (place[2] ^ j) * 32, 32), 32), :n] = g[half]
     row = lax.broadcasted_iota(jnp.int32, (n, n), 0)
     col = lax.broadcasted_iota(jnp.int32, (n, n), 1)
     w[:, n:] = jnp.where(row == col, 1.0, 0.0)
@@ -134,17 +156,24 @@
             w[o + nb:, lo:hi] = w[o + nb:, lo:hi] - change[o + nb - lo:]
 
 
-def fill_inverse(inv, blocks):
-    for k in range(4):
-        inv[k, :128, :128] = blocks[k, 0]
+def fill_inverse(inv, place, around):
+    for d, blocks in enumerate(around):
+        k = (place[1] - d) & 3
+        inv[k, :128, :128] = blocks[0]
         inv[k, :128, 128:] = jnp.zeros((128, 128), F32)
-        inv[k, 128:, :128] = blocks[k, 1]
-        inv[k, 128:, 128:] = blocks[k, 2]
-
-
-def right_kernel(place, w0, w1, w2, w3, blocks, right_s, right_n, squares, inv):
+        inv[k, 128:, :128] = blocks[1]
+        inv[k, 128:, 128:] = blocks[2]
+
+
+def arrange_kernel(place, w0, w1, w2, w3, out):
+    for j, pair in enumerate((w0, w1, w2, w3)):
+        for a in range(2):
+            out[a * 4 + (place[3] ^ (j >> 1)) * 2 + (place[4] ^ (j & 1))] = pair[a]
+
+
+def right_kernel(place, w0, w1, w2, w3, l0, l1, l2, l3, right_s, right_n, squares, inv):
     q = place[2]
-    fill_inverse(inv, blocks)
+    fill_inverse(inv, place, (l0, l1, l2, l3))
     for j, w in enumerate((w0, w1, w2, w3)):
         p = q ^ j
         for k in range(2):
@@ -160,8 +189,8 @@
         squares[k:k + 1, :] = jnp.sum(r * r, axis=0, keepdims=True)
 
 
-def momentum_kernel(place, blocks, right_s, right_n, left, ms, gs, mn, gn, ortho, mom_s, mom_n, inv, s_out, n_out, sem):
-    fill_inverse(inv, blocks)
+def momentum_kernel(place, l0, l1, l2, l3, right_s, right_n, left, ms, gs, mn, gn, ortho, mom_s, mom_n, inv, s_out, n_out, sem):
+    fill_inverse(inv, place, (l0, l1, l2, l3))
     copies = []
     for k in range(4):
         m, g, right, mom, new = (ms, gs, right_s, mom_s, s_out) if k < 2 else (mn, gn, right_n, mom_n, n_out)
@@ -198,18 +227,30 @@
 
 def partners():
     def pair(i, core, n):
-        return i ^ 1 if core == 0 else (((i - 1) ^ 1) + 1) % n
-
-    y_pairs, z_pairs, d_pairs = [], [], []
-    for i in range(256):
-        z, y, x, core = i // 32, i // 8 % 4, i // 2 % 4, i % 2
-        z2, y2 = pair(z, core, 8), pair((y - core) % 4, 0, 4)
-        y2 = (y2 + core) % 4
-        at = lambda a, b: a * 32 + b * 8 + x * 2 + core
-        y_pairs.append((i, at(z, y2)))
-        z_pairs.append((i, at(z2, y)))
-        d_pairs.append((i, at(z2, y2)))
-    return y_pairs, z_pairs, d_pairs
+        return ((i - core) % n ^ 1) + core
+
+    def perm(move):
+        at = [(i // 32, i // 8 % 4, i // 2 % 4, i % 2) for i in range(256)]
+        out = []
+        for i, (z, y, x, core) in enumerate(at):
+            z, y = move(z, y, core)
+            out.append((i, z % 8 * 32 + y % 4 * 8 + x * 2 + core))
+        return out
+
+    near_z = lambda z, core: pair(z, core, 8)
+    near_y = lambda y, core: pair(y, core, 4)
+    far_z = lambda z, core: pair(z // 2, core, 4) * 2 + z % 2
+    near = [
+        perm(lambda z, y, c: (z, near_y(y, c))),
+        perm(lambda z, y, c: (near_z(z, c), y)),
+        perm(lambda z, y, c: (near_z(z, c), near_y(y, c))),
+    ]
+    far = [
+        perm(lambda z, y, c: (z, y + 2)),
+        perm(lambda z, y, c: (far_z(z, c), y)),
+        perm(lambda z, y, c: (far_z(z, c), y + 2)),
+    ]
+    return near, far, perm(lambda z, y, c: (z + 4, y))
 
 
 def around_x(value):
@@ -224,41 +265,53 @@
 
 
 def local(mom_square, grad_square, basis_square, mom_narrow, grad_narrow, basis_narrow):
+    zh, yh = lax.axis_index("zh"), lax.axis_index("yh")
+    a, b = zh // 2, zh % 2
     q = lax.axis_index("zl") * 2 + lax.axis_index("yl")
-    place = jnp.stack([lax.axis_index("core"), lax.axis_index("x"), q]).astype(jnp.int32)
-    in_block = partners()
+    place = jnp.stack([lax.axis_index("core"), lax.axis_index("x"), q, b, yh]).astype(jnp.int32)
+    near, far, across = partners()
+    send = lambda value, pairs: lax.ppermute(value, AXES, pairs)
+    spread = lambda value, axes, n: lax.all_to_all(jnp.broadcast_to(value[None], (n,) + value.shape), axes, 0, 0)
+    inputs = (mom_square, grad_square, basis_square, mom_narrow, grad_narrow, basis_narrow)
+
+    buffers = (mom_square, grad_square, mom_narrow, grad_narrow)
+    fetched = [pltpu.VMEM(v.shape, v.dtype) for v in buffers] + [pltpu.SemaphoreType.DMA((4,))]
 
     mine, theirs = call(
         project_kernel,
         [((4, 4, 32, RANK), F32)] * 2,
-        (place, mom_square, grad_square, basis_square, mom_narrow, grad_narrow, basis_narrow),
+        (place,) + inputs,
         [pltpu.VMEM((4, 256, RANK), F32)]
-        + [pltpu.VMEM(a.shape, a.dtype)
-           for a in (mom_square, grad_square, basis_square, mom_narrow, grad_narrow, basis_narrow)]
+        + [pltpu.VMEM(v.shape, v.dtype) for v in inputs]
         + [pltpu.SemaphoreType.DMA((6, 2))],
         name="project",
         far_in=range(1, 7),
     )
     half = mine + swap_core(theirs)
     part = jnp.sum(lax.all_to_all(half, "x", 0, 0), axis=0)
-    own_half = lax.all_to_all(jnp.broadcast_to(part[None], (4,) + part.shape), "x", 0, 0)
+    own_half = spread(part, "x", 4)
     other_half = swap_core(own_half)
 
-    left, own, *send = call(
+    left, own, *others = call(
         back_kernel,
-        [((4, 256, RANK), F32)] + [((8, CHUNK + GR, RANK), F32)] * 4,
-        (place, mom_square, grad_square, mom_narrow, grad_narrow, own_half, other_half),
-        [pltpu.VMEM((32, CHUNK + GR, RANK), F32)],
+        [((4, 256, RANK), F32)] + [((8 * CHUNK + 32, RANK), F32)] * 4,
+        (place,) + buffers + (own_half, other_half),
+        [pltpu.VMEM((32, CHUNK, RANK), F32), pltpu.VMEM((128, RANK), F32)] + fetched,
         name="back",
-    )
-    for value, pairs in zip(send, in_block):
-        own = own + lax.ppermute(value, AXES, pairs)
-    part = jnp.sum(lax.all_to_all(own, FAR, 0, 0), axis=0)
-    own = lax.all_to_all(jnp.broadcast_to(part[None], (8,) + part.shape), FAR, 0, 0)
-    gram = own[:, CHUNK:, :]
-    grams = [gram] + [lax.ppermute(gram, AXES, pairs) for pairs in in_block]
-    w = own[:, :CHUNK, :]
-    ws = [w] + [lax.ppermute(w, AXES, pairs) for pairs in in_block]
+        far_in=range(1, 5),
+    )
+    got = [send(value, pairs) for value, pairs in zip(others, near)]
+    mine, *others = call(meet_kernel, [((2 * CHUNK + 32, RANK), F32)] * 4, (place, own, *got), name="meet")
+    got = [send(value, pairs) for value, pairs in zip(others, far)]
+    own = mine + got[0] + got[1] + got[2]
+    part = lambda i: jnp.concatenate([lax.dynamic_slice(own, (i * CHUNK, 0), (CHUNK, RANK)), own[2 * CHUNK:]])
+    own = part(a) + send(part(1 - a), across)
+    own, gram = own[:CHUNK], own[CHUNK:]
+    got = send(own, across)
+    other_gram = swap_core(gram)
+    gram = jnp.where(place[0] == 0, jnp.stack([gram, other_gram]), jnp.stack([other_gram, gram]))
+    grams = [gram] + [send(gram, pairs) for pairs in near]
+    grams, got = lax.optimization_barrier((grams, got))
     (blocks,) = call(
         factor_kernel,
         [((3, 128, 128), F32)],
@@ -266,12 +319,17 @@
         [pltpu.VMEM((RANK, 2 * RANK), F32)],
         name="factor",
     )
-    blocks = lax.all_to_all(jnp.broadcast_to(blocks[None], (4,) + blocks.shape), "x", 0, 0)
+    pair = jnp.where(a == 0, jnp.stack([own, got]), jnp.stack([got, own]))
+    pairs = [pair] + [send(pair, p) for p in far]
+    blocks, pairs = lax.optimization_barrier((blocks, pairs))
+    (quarter,) = call(arrange_kernel, [((8, CHUNK, RANK), F32)], (place, *pairs), name="arrange")
+    quarters = [quarter] + [send(quarter, p) for p in near]
+    around = around_x(blocks)
     inverse = pltpu.VMEM((4, RANK, RANK), F32)
     right_s, right_n, squares = call(
         right_kernel,
         [((2, 1024, RANK), F32), ((2, 128, RANK), F32), ((8, RANK), F32)],
-        (place, *ws, blocks),
+        (place, *quarters, *around),
         [inverse],
         name="right",
     )
@@ -280,7 +338,7 @@
     ortho, new_mom_s, new_mom_n = call(
         momentum_kernel,
         [((4, 256, RANK), F32), (mom_square.shape, F32), (mom_narrow.shape, F32)],
-        (place, blocks, right_s, right_n, left, mom_square, grad_square, mom_narrow, grad_narrow),
+        (place, *around, right_s, right_n, left) + buffers,
         [inverse, pltpu.VMEM(mom_square.shape, F32), pltpu.VMEM(mom_narrow.shape, F32), pltpu.SemaphoreType.DMA((4,))],
         name="momentum",
         far_out=(1, 2),
@@ -290,7 +348,7 @@
         update_kernel,
         outs,
         (place, *four_squares, right_s, right_n, ortho),
-        [pltpu.VMEM(s, d) for s, d in outs] + [pltpu.SemaphoreType.DMA((2, 4))],
+        [pltpu.VMEM(*v) for v in outs] + [pltpu.SemaphoreType.DMA((2, 4))],
         name="update",
         far_out=range(4),
     )

time: 164 us -> 150 us (0.915)
  blocking collectives: 69.6 us -> 22.3 us
  starting transfers between devices: 29.8 us -> 57.4 us
  waiting for transfers between devices: 31.2 us -> 39.7 us
  Pallas kernels: 30.4 us -> 27.5 us
    all_to_all x3 -> x1, blocking collectives: 57.9 us -> 10.7 us  [local(): lax.all_to_all(jnp.broadcast_to(value[None], (n,) + value.shape), axes, 0...]
    ppermute x9 -> x17, starting transfers between devices: 18 us -> 42.7 us  [local(): send = lambda value, pairs: lax.ppermute(value, AXES, pairs)]
    ppermute x9 -> x17, waiting for transfers between devices: 14.8 us -> 27.3 us  [local(): send = lambda value, pairs: lax.ppermute(value, AXES, pairs)]
    all_to_all x1 -> x0, waiting for transfers between devices: 12.4 us -> none  [local(): lax.all_to_all(jnp.broadcast_to(blocks[None], (4,) + blocks.shape), 'x',...]
    ppermute x3 -> x6, waiting for transfers between devices: 0.01 us -> 8.21 us  [around_x(): got[d] = lax.ppermute(value, 'x', [(i, (i + d) % 4) for i in range(4)])]
    ppermute x3 -> x6, starting transfers between devices: 2.08 us -> 7.88 us  [around_x(): got[d] = lax.ppermute(value, 'x', [(i, (i + d) % 4) for i in range(4)])]
    all_to_all x1 -> x0, starting transfers between devices: 3.63 us -> none  [local(): lax.all_to_all(jnp.broadcast_to(blocks[None], (4,) + blocks.shape), 'x',...]
    pallas_call x6 -> x8, Pallas kernels: 30.4 us -> 27.5 us  [call(): pl.pallas_call(kernel, out_shape=[jax.ShapeDtypeStruct(s, d) for s, d in...]
  transfers between devices with their start and end apart: 16 -> 27, of which waited for: 8 -> 16; matrix products, arithmetic and copies ran while one was open for 1% -> 0% of each run, Pallas kernels for 9% -> 8%
where the time goes in v4:
time: 150 us; the launch traced here: 148 us
  starting transfers between devices  57.4 us (38%)
  waiting for transfers between devices  39.7 us (26%)
  Pallas kernels  27.5 us (18%)
  blocking collectives  22.3 us (15%)
    ppermute x17, starting transfers between devices, local(): send = lambda value, pairs: lax.ppermute(value, AXES, pairs)  42.7 us
    pallas_call x8, Pallas kernels, call(): pl.pallas_call(kernel, out_shape=[jax.ShapeDtypeStruct(s, d) for s, d in...  27.5 us
    ppermute x17, waiting for transfers between devices, local(): send = lambda value, pairs: lax.ppermute(value, AXES, pairs)  27.3 us
    all_to_all x1, blocking collectives, local(): part = jnp.sum(lax.all_to_all(half, 'x', 0, 0), axis=0)  11.6 us
    all_to_all x1, blocking collectives, local(): lax.all_to_all(jnp.broadcast_to(value[None], (n,) + value.shape), axes, 0...  10.7 us
    ppermute x6, waiting for transfers between devices, around_x(): got[d] = lax.ppermute(value, 'x', [(i, (i + d) % 4) for i in range(4)])  8.21 us
    ppermute x6, starting transfers between devices, around_x(): got[d] = lax.ppermute(value, 'x', [(i, (i + d) % 4) for i in range(4)])  7.88 us
    ppermute x4, starting transfers between devices, swap_core(): return lax.ppermute(value, 'core', [(0, 1), (1, 0)])  6.87 us
  transfers between devices with their start and end apart: 27, of which 16 were waited for; matrix products, arithmetic and copies ran while one was open for 0% of the time, Pallas kernels for 8%

profile of v4, /device:TPU:1, one launch (start us, length us, event | category | flops | bytes accessed | tf_op | source)
XLA Modules:
  0.0 148.5 jit_solution(8481049741922412401)
XLA Ops:
  0.7 0.1 stack.51.place
  0.7 4.7 %project.1 = (f32[4,4,32,256]{3,2,1,0:T(8,128)S(1)}, f32[4,4,32,256]{3,2,1,0:T(8,128)S(1)}) custom-call(s32[5]{0:T(128)S(1)} %stack.51.place, f32[2,256,1024]{2,1,0:T(8,128)} %ms.5, bf16[2,256,1024]{2,1,0:T(8,128)(2,1)} %gs.5, f32[2,1024,256]{2,1,0:T(8,128)} %qs.1, f32[2,256,128]{2,1,0:T(8,128)} %mn.5, bf16[2,256,128]{2,1,0:T(8,128)(2,1)} %gn.5, ...), custom_call_target="tpu_custom_call" | custom-call | tf_op jit(solution)/shard_map/project/pallas_call | solution.py:39
  5.4 3.3 %collective-permute-start = (f32[4,4,32,256]{3,2,1,0:T(8,128)S(1)}, f32[4,4,32,256]{3,2,1,0:T(8,128)S(1)}, u32[]{:S(2)}, u32[]{:S(2)}) collective-permute-start(f32[4,4,32,256]{3,2,1,0:T(8,128)S(1)} %get-tuple-element.40), channel_id=1, source_target_pairs={{0,1},{1,0},{2,3},{3,2},{4,5},{5,4},{6,7},{7,6},{8,9},{9,8},{10,11... | collective-permute-start | bytes 1572872 | tf_op jit(solution)/shard_map/ppermute | solution.py:264
  8.8 1.5 %collective-permute-done = f32[4,4,32,256]{3,2,1,0:T(8,128)S(1)} collective-permute-done((f32[4,4,32,256]{3,2,1,0:T(8,128)S(1)}, f32[4,4,32,256]{3,2,1,0:T(8,128)S(1)}, u32[]{:S(2)}, u32[]{:S(2)}) %collective-permute-start) | collective-permute-done | bytes 524320 | tf_op jit(solution)/shard_map/ppermute | solution.py:264
  10.3 0.1 add.34
  10.4 11.6 %all_to_all.10 = f32[4,4,32,256]{3,2,1,0:T(8,128)S(1)} all-to-all(f32[4,4,32,256]{3,2,1,0:T(8,128)S(1)} %add.34), channel_id=1, replica_groups=mesh['zh'=4,'zl'=2,'yh'=2,'yl'=2,'x'=4,'core'=2] {'x'}, dimensions={0} | all-to-all | bytes 1048576 | tf_op jit(solution)/shard_map/all_to_all | solution.py:291
  22.1 10.7 %all_to_all.11.own_half = f32[4,4,32,256]{3,2,1,0:T(8,128)S(1)} all-to-all(f32[4,4,32,256]{3,2,1,0:T(8,128)S(1)} %broadcast_in_dim.2), channel_id=1, replica_groups=mesh['zh'=4,'zl'=2,'yh'=2,'yl'=2,'x'=4,'core'=2] {'x'}, dimensions={0} | all-to-all | bytes 1048576 | tf_op jit(solution)/shard_map/all_to_all | solution.py:274
  32.8 2.1 %collective-permute-start.1 = (f32[4,4,32,256]{3,2,1,0:T(8,128)S(1)}, f32[4,4,32,256]{3,2,1,0:T(8,128)S(1)}, u32[]{:S(2)}, u32[]{:S(2)}) collective-permute-start(f32[4,4,32,256]{3,2,1,0:T(8,128)S(1)} %all_to_all.11.own_half), channel_id=1, source_target_pairs={{0,1},{1,0},{2,3},{3,2},{4,5},{5,4},{6,7},{7,6},{8,9},{9,8},{10,11... | collective-permute-start | bytes 1572872 | tf_op jit(solution)/shard_map/ppermute | solution.py:264
  34.9 1.5 %collective-permute-done.1.other_half = f32[4,4,32,256]{3,2,1,0:T(8,128)S(1)} collective-permute-done((f32[4,4,32,256]{3,2,1,0:T(8,128)S(1)}, f32[4,4,32,256]{3,2,1,0:T(8,128)S(1)}, u32[]{:S(2)}, u32[]{:S(2)}) %collective-permute-start.1) | collective-permute-done | bytes 524320 | tf_op jit(solution)/shard_map/ppermute | solution.py:264
  36.5 3.9 %back.1 = (f32[4,256,256]{2,1,0:T(8,128)S(1)}, f32[608,256]{1,0:T(8,128)S(1)}, f32[608,256]{1,0:T(8,128)S(1)}, f32[608,256]{1,0:T(8,128)S(1)}, f32[608,256]{1,0:T(8,128)S(1)}) custom-call(s32[5]{0:T(128)S(1)} %stack.51.place, f32[2,256,1024]{2,1,0:T(8,128)} %ms.5, bf16[2,256,1024]{2,1,0:T(8,128)(2,1)} %gs.5, f32[2,256,128]{2,1,0:T(8,128)} %mn.5, ...), custom_call_target="tpu_custom_call" | custom-call | tf_op jit(solution)/shard_map/back/pallas_call | solution.py:39
  40.4 1.9 %collective-permute-start.2 = (f32[608,256]{1,0:T(8,128)S(1)}, f32[608,256]{1,0:T(8,128)S(1)}, u32[]{:S(2)}, u32[]{:S(2)}) collective-permute-start(f32[608,256]{1,0:T(8,128)S(1)} %get-tuple-element.42), channel_id=1, source_target_pairs={{0,8},{1,25},{2,10},{3,27},{4,12},{5,29},{6,14},{7,31},{8,0},{9,17... | collective-permute-start | bytes 1867784 | tf_op jit(solution)/shard_map/ppermute | solution.py:273
  42.3 5.6 %collective-permute-start.3 = (f32[608,256]{1,0:T(8,128)S(1)}, f32[608,256]{1,0:T(8,128)S(1)}, u32[]{:S(2)}, u32[]{:S(2)}) collective-permute-start(f32[608,256]{1,0:T(8,128)S(1)} %get-tuple-element.43), channel_id=1, source_target_pairs={{0,32},{1,225},{2,34},{3,227},{4,36},{5,229},{6,38},{7,231},{8,40}... | collective-permute-start | bytes 1867784 | tf_op jit(solution)/shard_map/ppermute | solution.py:273
  47.9 0.0 collective-permute-start.4
  47.9 2.9 %collective-permute-done.2.r0 = f32[608,256]{1,0:T(8,128)S(1)} collective-permute-done((f32[608,256]{1,0:T(8,128)S(1)}, f32[608,256]{1,0:T(8,128)S(1)}, u32[]{:S(2)}, u32[]{:S(2)}) %collective-permute-start.2) | collective-permute-done | bytes 622624 | tf_op jit(solution)/shard_map/ppermute | solution.py:273
  50.8 4.8 %collective-permute-done.3.r1 = f32[608,256]{1,0:T(8,128)S(1)} collective-permute-done((f32[608,256]{1,0:T(8,128)S(1)}, f32[608,256]{1,0:T(8,128)S(1)}, u32[]{:S(2)}, u32[]{:S(2)}) %collective-permute-start.3) | collective-permute-done | bytes 622624 | tf_op jit(solution)/shard_map/ppermute | solution.py:273
  55.6 6.4 %collective-permute-done.4.r2 = f32[608,256]{1,0:T(8,128)S(1)} collective-permute-done((f32[608,256]{1,0:T(8,128)S(1)}, f32[608,256]{1,0:T(8,128)S(1)}, u32[]{:S(2)}, u32[]{:S(2)}) %collective-permute-start.4) | collective-permute-done | bytes 622624 | tf_op jit(solution)/shard_map/ppermute | solution.py:273
  62.0 0.7 meet.1
  62.7 1.6 %collective-permute-start.5 = (f32[176,256]{1,0:T(8,128)S(1)}, f32[176,256]{1,0:T(8,128)S(1)}, u32[]{:S(2)}, u32[]{:S(2)}) collective-permute-start(f32[176,256]{1,0:T(8,128)S(1)} %get-tuple-element.46), channel_id=1, source_target_pairs={{0,16},{1,17},{2,18},{3,19},{4,20},{5,21},{6,22},{7,23},{8,24},{9,... | collective-permute-start | bytes 540680 | tf_op jit(solution)/shard_map/ppermute | solution.py:273
  64.3 2.2 %collective-permute-start.6 = (f32[176,256]{1,0:T(8,128)S(1)}, f32[176,256]{1,0:T(8,128)S(1)}, u32[]{:S(2)}, u32[]{:S(2)}) collective-permute-start(f32[176,256]{1,0:T(8,128)S(1)} %get-tuple-element.47), channel_id=1, source_target_pairs={{0,64},{1,193},{2,66},{3,195},{4,68},{5,197},{6,70},{7,199},{8,72}... | collective-permute-start | bytes 540680 | tf_op jit(solution)/shard_map/ppermute | solution.py:273
  66.5 2.5 %collective-permute-start.7 = (f32[176,256]{1,0:T(8,128)S(1)}, f32[176,256]{1,0:T(8,128)S(1)}, u32[]{:S(2)}, u32[]{:S(2)}) collective-permute-start(f32[176,256]{1,0:T(8,128)S(1)} %get-tuple-element.48), channel_id=1, source_target_pairs={{0,80},{1,209},{2,82},{3,211},{4,84},{5,213},{6,86},{7,215},{8,88}... | collective-permute-start | bytes 540680 | tf_op jit(solution)/shard_map/ppermute | solution.py:273
  69.0 1.8 %collective-permute-done.6 = f32[176,256]{1,0:T(8,128)S(1)} collective-permute-done((f32[176,256]{1,0:T(8,128)S(1)}, f32[176,256]{1,0:T(8,128)S(1)}, u32[]{:S(2)}, u32[]{:S(2)}) %collective-permute-start.6) | collective-permute-done | bytes 180256 | tf_op jit(solution)/shard_map/ppermute | solution.py:273
  70.8 5.4 %collective-permute-done.7 = f32[176,256]{1,0:T(8,128)S(1)} collective-permute-done((f32[176,256]{1,0:T(8,128)S(1)}, f32[176,256]{1,0:T(8,128)S(1)}, u32[]{:S(2)}, u32[]{:S(2)}) %collective-permute-start.7) | collective-permute-done | bytes 180256 | tf_op jit(solution)/shard_map/ppermute | solution.py:273
  76.4 5.5 %collective-permute-start.8 = (f32[104,256]{1,0:T(8,128)S(1)}, f32[104,256]{1,0:T(8,128)S(1)}, u32[]{:S(2)}, u32[]{:S(2)}) collective-permute-start(f32[104,256]{1,0:T(8,128)S(1)} %pad_maximum_fusion), channel_id=1, source_target_pairs={{0,128},{1,129},{2,130},{3,131},{4,132},{5,133},{6,134},{7,135},{8... | collective-permute-start | bytes 319496 | tf_op jit(solution)/shard_map/ppermute | solution.py:273
  81.9 2.8 %collective-permute-done.8 = f32[104,256]{1,0:T(8,128)S(1)} collective-permute-done((f32[104,256]{1,0:T(8,128)S(1)}, f32[104,256]{1,0:T(8,128)S(1)}, u32[]{:S(2)}, u32[]{:S(2)}) %collective-permute-start.8) | collective-permute-done | bytes 106528 | tf_op jit(solution)/shard_map/ppermute | solution.py:273
  84.7 1.3 collective-permute-start.9
  86.0 6.5 %collective-permute-start.13 = (f32[72,256]{1,0:T(8,128)S(1)}, f32[72,256]{1,0:T(8,128)S(1)}, u32[]{:S(2)}, u32[]{:S(2)}) collective-permute-start(f32[72,256]{1,0:T(8,128)S(1)} %get-tuple-element.75), channel_id=1, source_target_pairs={{0,128},{1,129},{2,130},{3,131},{4,132},{5,133},{6,134},{7,135},{8... | collective-permute-start | bytes 221192 | tf_op jit(solution)/shard_map/ppermute | solution.py:273
  92.5 0.0 collective-permute-done.9
  92.6 3.3 %collective-permute-start.12 = (f32[2,32,256]{2,1,0:T(8,128)S(1)}, f32[2,32,256]{2,1,0:T(8,128)S(1)}, u32[]{:S(2)}, u32[]{:S(2)}) collective-permute-start(f32[2,32,256]{2,1,0:T(8,128)S(1)} %maximum_select_fusion.1.g0), channel_id=1, source_target_pairs={{0,40},{1,249},{2,42},{3,251},{4,44},{5,253},{6,46},{7,255},{8,32}... | collective-permute-start | bytes 196616 | tf_op jit(solution)/shard_map/ppermute | solution.py:273
  95.9 0.1 collective-permute-start.11
  95.9 1.8 %collective-permute-start.10 = (f32[2,32,256]{2,1,0:T(8,128)S(1)}, f32[2,32,256]{2,1,0:T(8,128)S(1)}, u32[]{:S(2)}, u32[]{:S(2)}) collective-permute-start(f32[2,32,256]{2,1,0:T(8,128)S(1)} %maximum_select_fusion.1.g0), channel_id=1, source_target_pairs={{0,8},{1,25},{2,10},{3,27},{4,12},{5,29},{6,14},{7,31},{8,0},{9,17... | collective-permute-start | bytes 196616 | tf_op jit(solution)/shard_map/ppermute | solution.py:273
  97.7 1.4 collective-permute-done.12.g3
  99.1 1.1 collective-permute-done.11.g2
  100.2 0.1 collective-permute-done.10.g1
  100.3 2.9 %collective-permute-start.16 = (f32[2,72,256]{2,1,0:T(8,128)S(1)}, f32[2,72,256]{2,1,0:T(8,128)S(1)}, u32[]{:S(2)}, u32[]{:S(2)}) collective-permute-start(f32[2,72,256]{2,1,0:T(8,128)S(1)} %maximum_select_fusion.w0), channel_id=1, source_target_pairs={{0,80},{1,209},{2,82},{3,211},{4,84},{5,213},{6,86},{7,215},{8,88}... | collective-permute-start | bytes 442376 | tf_op jit(solution)/shard_map/ppermute | solution.py:273
  103.2 1.5 %collective-permute-start.15 = (f32[2,72,256]{2,1,0:T(8,128)S(1)}, f32[2,72,256]{2,1,0:T(8,128)S(1)}, u32[]{:S(2)}, u32[]{:S(2)}) collective-permute-start(f32[2,72,256]{2,1,0:T(8,128)S(1)} %maximum_select_fusion.w0), channel_id=1, source_target_pairs={{0,64},{1,193},{2,66},{3,195},{4,68},{5,197},{6,70},{7,199},{8,72}... | collective-permute-start | bytes 442376 | tf_op jit(solution)/shard_map/ppermute | solution.py:273
  104.7 2.1 %collective-permute-start.14 = (f32[2,72,256]{2,1,0:T(8,128)S(1)}, f32[2,72,256]{2,1,0:T(8,128)S(1)}, u32[]{:S(2)}, u32[]{:S(2)}) collective-permute-start(f32[2,72,256]{2,1,0:T(8,128)S(1)} %maximum_select_fusion.w0), channel_id=1, source_target_pairs={{0,16},{1,17},{2,18},{3,19},{4,20},{5,21},{6,22},{7,23},{8,24},{9,... | collective-permute-start | bytes 442376 | tf_op jit(solution)/shard_map/ppermute | solution.py:273
  106.8 9.0 %factor.1.l0 = f32[3,128,128]{2,1,0:T(8,128)S(1)} custom-call(s32[5]{0:T(128)S(1)} %stack.51.place, f32[2,32,256]{2,1,0:T(8,128)S(1)} %maximum_select_fusion.1.g0, f32[2,32,256]{2,1,0:T(8,128)S(1)} %collective-permute-done.10.g1, f32[2,32,256]{2,1,0:T(8,128)S(1)} %collective-permute-done.11.g2, f32[2,32,256]{2,1,0:T(8,128)S(1)} %collective-permute-done.12.g3), custom_call_target="tpu_custom_call" | custom-call | tf_op jit(solution)/shard_map/factor/pallas_call | solution.py:39
  115.8 0.0 copy-start
  115.8 0.0 copy-start.1
  115.8 0.0 copy-start.2
  115.9 0.0 copy-start.3
  115.9 0.0 collective-permute-done.16.w3
  115.9 0.6 arrange.1.w0
  116.5 3.1 %collective-permute-start.22 = (f32[8,72,256]{2,1,0:T(8,128)S(1)}, f32[8,72,256]{2,1,0:T(8,128)S(1)}, u32[]{:S(2)}, u32[]{:S(2)}) collective-permute-start(f32[8,72,256]{2,1,0:T(8,128)S(1)} %arrange.1.w0), channel_id=1, source_target_pairs={{0,40},{1,249},{2,42},{3,251},{4,44},{5,253},{6,46},{7,255},{8,32}... | collective-permute-start | bytes 1769480 | tf_op jit(solution)/shard_map/ppermute | solution.py:273
  119.6 1.2 collective-permute-start.21
  120.8 0.9 collective-permute-start.20
  121.7 0.9 collective-permute-start.19
  122.5 1.2 collective-permute-start.18
  123.7 4.9 %collective-permute-done.19.l3 = f32[3,128,128]{2,1,0:T(8,128)S(1)} collective-permute-done((f32[3,128,128]{2,1,0:T(8,128)S(1)}, f32[3,128,128]{2,1,0:T(8,128)S(1)}, u32[]{:S(2)}, u32[]{:S(2)}) %collective-permute-start.19) | collective-permute-done | bytes 196640 | tf_op jit(solution)/shard_map/ppermute | solution.py:259
  128.6 2.9 %collective-permute-start.17 = (f32[3,128,128]{2,1,0:T(8,128)S(1)}, f32[3,128,128]{2,1,0:T(8,128)S(1)}, u32[]{:S(2)}, u32[]{:S(2)}) collective-permute-start(f32[3,128,128]{2,1,0:T(8,128)S(1)} %factor.1.l0), channel_id=1, source_target_pairs={{0,2},{2,4},{4,6},{6,0},{1,3},{3,5},{5,7},{7,1},{8,10},{10,12},{12... | collective-permute-start | bytes 589832 | tf_op jit(solution)/shard_map/ppermute | solution.py:259
  131.5 0.0 collective-permute-done.18.l2
  131.5 2.8 %collective-permute-done.17.l1 = f32[3,128,128]{2,1,0:T(8,128)S(1)} collective-permute-done((f32[3,128,128]{2,1,0:T(8,128)S(1)}, f32[3,128,128]{2,1,0:T(8,128)S(1)}, u32[]{:S(2)}, u32[]{:S(2)}) %collective-permute-start.17) | collective-permute-done | bytes 196640 | tf_op jit(solution)/shard_map/ppermute | solution.py:259
  134.4 0.0 collective-permute-done.22.w3
  134.4 0.0 collective-permute-done.21.w2
  134.4 0.6 collective-permute-done.20.w1
  135.0 2.4 %right.1 = (f32[2,1024,256]{2,1,0:T(8,128)S(1)}, f32[2,128,256]{2,1,0:T(8,128)S(1)}, f32[8,256]{1,0:T(8,128)S(1)}) custom-call(s32[5]{0:T(128)S(1)} %stack.51.place, f32[8,72,256]{2,1,0:T(8,128)S(1)} %arrange.1.w0, f32[8,72,256]{2,1,0:T(8,128)S(1)} %collective-permute-done.20.w1, f32[8,72,256]{2,1,0:T(8,128)S(1)} %collective-permute-done.21.w2, ...), custom_call_target="tpu_custom_call" | custom-call | tf_op jit(solution)/shard_map/right/pallas_call | solution.py:39
  137.4 0.1 collective-permute-start.23
  137.5 1.2 collective-permute-done.23
  138.7 0.9 collective-permute-start.26
  139.5 2.0 %collective-permute-start.25 = (f32[8,256]{1,0:T(8,128)S(1)}, f32[8,256]{1,0:T(8,128)S(1)}, u32[]{:S(2)}, u32[]{:S(2)}) collective-permute-start(f32[8,256]{1,0:T(8,128)S(1)} %add.41.q0), channel_id=1, source_target_pairs={{0,4},{2,6},{4,0},{6,2},{1,5},{3,7},{5,1},{7,3},{8,12},{10,14},{12... | collective-permute-start | bytes 24584 | tf_op jit(solution)/shard_map/ppermute | solution.py:259
  141.6 0.0 collective-permute-start.24
  141.6 3.2 %momentum.1 = (f32[4,256,256]{2,1,0:T(8,128)S(1)}, f32[2,256,1024]{2,1,0:T(8,128)}, f32[2,256,128]{2,1,0:T(8,128)}) custom-call(s32[5]{0:T(128)S(1)} %stack.51.place, f32[3,128,128]{2,1,0:T(8,128)S(1)} %factor.1.l0, f32[3,128,128]{2,1,0:T(8,128)S(1)} %collective-permute-done.17.l1, f32[3,128,128]{2,1,0:T(8,128)S(1)} %collective-permute-done.18.l2, ...), custom_call_target="tpu_custom_call" | custom-call | tf_op jit(solution)/shard_map/momentum/pallas_call | solution.py:39
  144.8 0.5 collective-permute-done.24.q1
  145.3 3.0 %update.1 = (bf16[2,256,1024]{2,1,0:T(8,128)(2,1)}, f32[2,1024,256]{2,1,0:T(8,128)}, bf16[2,256,128]{2,1,0:T(8,128)(2,1)}, f32[2,128,256]{2,1,0:T(8,128)}) custom-call(s32[5]{0:T(128)S(1)} %stack.51.place, f32[8,256]{1,0:T(8,128)S(1)} %add.41.q0, f32[8,256]{1,0:T(8,128)S(1)} %collective-permute-done.24.q1, f32[8,256]{1,0:T(8,128)S(1)} %collective-permute-done.25.q2, ...), custom_call_target="tpu_custom_call" | custom-call | tf_op jit(solution)/shard_map/update/pallas_call | solution.py:39
  (22 shorter events, 0.2 us)
Async XLA Ops:
  5.4 4.9 %collective-permute-start = (f32[4,4,32,256]{3,2,1,0:T(8,128)S(1)}, f32[4,4,32,256]{3,2,1,0:T(8,128)S(1)}, u32[]{:S(2)}, u32[]{:S(2)}) collective-permute-start(f32[4,4,32,256]{3,2,1,0:T(8,128)S(1)} %get-tuple-element.40), channel_id=1, source_target_pairs={{0,1},{1,0},{2,3},{3,2},{4,5},{5,4},{6,7},{7,6},{8,9},{9,8},{10,11... | collective-permute-start | bytes 1572872 | tf_op jit(solution)/shard_map/ppermute | solution.py:264
  32.8 3.7 %collective-permute-start.1 = (f32[4,4,32,256]{3,2,1,0:T(8,128)S(1)}, f32[4,4,32,256]{3,2,1,0:T(8,128)S(1)}, u32[]{:S(2)}, u32[]{:S(2)}) collective-permute-start(f32[4,4,32,256]{3,2,1,0:T(8,128)S(1)} %all_to_all.11.own_half), channel_id=1, source_target_pairs={{0,1},{1,0},{2,3},{3,2},{4,5},{5,4},{6,7},{7,6},{8,9},{9,8},{10,11... | collective-permute-start | bytes 1572872 | tf_op jit(solution)/shard_map/ppermute | solution.py:264
  40.4 10.4 %collective-permute-start.2 = (f32[608,256]{1,0:T(8,128)S(1)}, f32[608,256]{1,0:T(8,128)S(1)}, u32[]{:S(2)}, u32[]{:S(2)}) collective-permute-start(f32[608,256]{1,0:T(8,128)S(1)} %get-tuple-element.42), channel_id=1, source_target_pairs={{0,8},{1,25},{2,10},{3,27},{4,12},{5,29},{6,14},{7,31},{8,0},{9,17... | collective-permute-start | bytes 1867784 | tf_op jit(solution)/shard_map/ppermute | solution.py:273
  42.3 13.3 %collective-permute-start.3 = (f32[608,256]{1,0:T(8,128)S(1)}, f32[608,256]{1,0:T(8,128)S(1)}, u32[]{:S(2)}, u32[]{:S(2)}) collective-permute-start(f32[608,256]{1,0:T(8,128)S(1)} %get-tuple-element.43), channel_id=1, source_target_pairs={{0,32},{1,225},{2,34},{3,227},{4,36},{5,229},{6,38},{7,231},{8,40}... | collective-permute-start | bytes 1867784 | tf_op jit(solution)/shard_map/ppermute | solution.py:273
  47.9 14.1 %collective-permute-start.4 = (f32[608,256]{1,0:T(8,128)S(1)}, f32[608,256]{1,0:T(8,128)S(1)}, u32[]{:S(2)}, u32[]{:S(2)}) collective-permute-start(f32[608,256]{1,0:T(8,128)S(1)} %get-tuple-element.44), channel_id=1, source_target_pairs={{0,40},{1,249},{2,42},{3,251},{4,44},{5,253},{6,46},{7,255},{8,32}... | collective-permute-start | bytes 1867784 | tf_op jit(solution)/shard_map/ppermute | solution.py:273
  62.7 6.4 %collective-permute-start.5 = (f32[176,256]{1,0:T(8,128)S(1)}, f32[176,256]{1,0:T(8,128)S(1)}, u32[]{:S(2)}, u32[]{:S(2)}) collective-permute-start(f32[176,256]{1,0:T(8,128)S(1)} %get-tuple-element.46), channel_id=1, source_target_pairs={{0,16},{1,17},{2,18},{3,19},{4,20},{5,21},{6,22},{7,23},{8,24},{9,... | collective-permute-start | bytes 540680 | tf_op jit(solution)/shard_map/ppermute | solution.py:273
  64.3 6.6 %collective-permute-start.6 = (f32[176,256]{1,0:T(8,128)S(1)}, f32[176,256]{1,0:T(8,128)S(1)}, u32[]{:S(2)}, u32[]{:S(2)}) collective-permute-start(f32[176,256]{1,0:T(8,128)S(1)} %get-tuple-element.47), channel_id=1, source_target_pairs={{0,64},{1,193},{2,66},{3,195},{4,68},{5,197},{6,70},{7,199},{8,72}... | collective-permute-start | bytes 540680 | tf_op jit(solution)/shard_map/ppermute | solution.py:273
  66.5 9.8 %collective-permute-start.7 = (f32[176,256]{1,0:T(8,128)S(1)}, f32[176,256]{1,0:T(8,128)S(1)}, u32[]{:S(2)}, u32[]{:S(2)}) collective-permute-start(f32[176,256]{1,0:T(8,128)S(1)} %get-tuple-element.48), channel_id=1, source_target_pairs={{0,80},{1,209},{2,82},{3,211},{4,84},{5,213},{6,86},{7,215},{8,88}... | collective-permute-start | bytes 540680 | tf_op jit(solution)/shard_map/ppermute | solution.py:273
  76.4 8.3 %collective-permute-start.8 = (f32[104,256]{1,0:T(8,128)S(1)}, f32[104,256]{1,0:T(8,128)S(1)}, u32[]{:S(2)}, u32[]{:S(2)}) collective-permute-start(f32[104,256]{1,0:T(8,128)S(1)} %pad_maximum_fusion), channel_id=1, source_target_pairs={{0,128},{1,129},{2,130},{3,131},{4,132},{5,133},{6,134},{7,135},{8... | collective-permute-start | bytes 319496 | tf_op jit(solution)/shard_map/ppermute | solution.py:273
  84.7 7.8 %collective-permute-start.9 = (f32[32,256]{1,0:T(8,128)S(1)}, f32[32,256]{1,0:T(8,128)S(1)}, u32[]{:S(2)}, u32[]{:S(2)}) collective-permute-start(f32[32,256]{1,0:T(8,128)S(1)} %get-tuple-element.77), channel_id=1, source_target_pairs={{0,1},{1,0},{2,3},{3,2},{4,5},{5,4},{6,7},{7,6},{8,9},{9,8},{10,11... | collective-permute-start | bytes 98312 | tf_op jit(solution)/shard_map/ppermute | solution.py:264
  86.0 11.7 %collective-permute-start.13 = (f32[72,256]{1,0:T(8,128)S(1)}, f32[72,256]{1,0:T(8,128)S(1)}, u32[]{:S(2)}, u32[]{:S(2)}) collective-permute-start(f32[72,256]{1,0:T(8,128)S(1)} %get-tuple-element.75), channel_id=1, source_target_pairs={{0,128},{1,129},{2,130},{3,131},{4,132},{5,133},{6,134},{7,135},{8... | collective-permute-start | bytes 221192 | tf_op jit(solution)/shard_map/ppermute | solution.py:273
  92.6 6.5 %collective-permute-start.12 = (f32[2,32,256]{2,1,0:T(8,128)S(1)}, f32[2,32,256]{2,1,0:T(8,128)S(1)}, u32[]{:S(2)}, u32[]{:S(2)}) collective-permute-start(f32[2,32,256]{2,1,0:T(8,128)S(1)} %maximum_select_fusion.1.g0), channel_id=1, source_target_pairs={{0,40},{1,249},{2,42},{3,251},{4,44},{5,253},{6,46},{7,255},{8,32}... | collective-permute-start | bytes 196616 | tf_op jit(solution)/shard_map/ppermute | solution.py:273
  95.9 4.3 %collective-permute-start.11 = (f32[2,32,256]{2,1,0:T(8,128)S(1)}, f32[2,32,256]{2,1,0:T(8,128)S(1)}, u32[]{:S(2)}, u32[]{:S(2)}) collective-permute-start(f32[2,32,256]{2,1,0:T(8,128)S(1)} %maximum_select_fusion.1.g0), channel_id=1, source_target_pairs={{0,32},{1,225},{2,34},{3,227},{4,36},{5,229},{6,38},{7,231},{8,40}... | collective-permute-start | bytes 196616 | tf_op jit(solution)/shard_map/ppermute | solution.py:273
  95.9 4.3 %collective-permute-start.10 = (f32[2,32,256]{2,1,0:T(8,128)S(1)}, f32[2,32,256]{2,1,0:T(8,128)S(1)}, u32[]{:S(2)}, u32[]{:S(2)}) collective-permute-start(f32[2,32,256]{2,1,0:T(8,128)S(1)} %maximum_select_fusion.1.g0), channel_id=1, source_target_pairs={{0,8},{1,25},{2,10},{3,27},{4,12},{5,29},{6,14},{7,31},{8,0},{9,17... | collective-permute-start | bytes 196616 | tf_op jit(solution)/shard_map/ppermute | solution.py:273
  100.3 15.6 %collective-permute-start.16 = (f32[2,72,256]{2,1,0:T(8,128)S(1)}, f32[2,72,256]{2,1,0:T(8,128)S(1)}, u32[]{:S(2)}, u32[]{:S(2)}) collective-permute-start(f32[2,72,256]{2,1,0:T(8,128)S(1)} %maximum_select_fusion.w0), channel_id=1, source_target_pairs={{0,80},{1,209},{2,82},{3,211},{4,84},{5,213},{6,86},{7,215},{8,88}... | collective-permute-start | bytes 442376 | tf_op jit(solution)/shard_map/ppermute | solution.py:273
  103.2 12.7 %collective-permute-start.15 = (f32[2,72,256]{2,1,0:T(8,128)S(1)}, f32[2,72,256]{2,1,0:T(8,128)S(1)}, u32[]{:S(2)}, u32[]{:S(2)}) collective-permute-start(f32[2,72,256]{2,1,0:T(8,128)S(1)} %maximum_select_fusion.w0), channel_id=1, source_target_pairs={{0,64},{1,193},{2,66},{3,195},{4,68},{5,197},{6,70},{7,199},{8,72}... | collective-permute-start | bytes 442376 | tf_op jit(solution)/shard_map/ppermute | solution.py:273
  104.7 11.2 %collective-permute-start.14 = (f32[2,72,256]{2,1,0:T(8,128)S(1)}, f32[2,72,256]{2,1,0:T(8,128)S(1)}, u32[]{:S(2)}, u32[]{:S(2)}) collective-permute-start(f32[2,72,256]{2,1,0:T(8,128)S(1)} %maximum_select_fusion.w0), channel_id=1, source_target_pairs={{0,16},{1,17},{2,18},{3,19},{4,20},{5,21},{6,22},{7,23},{8,24},{9,... | collective-permute-start | bytes 442376 | tf_op jit(solution)/shard_map/ppermute | solution.py:273
  115.8 25.8 %copy-start = (f32[2,256,1024]{2,1,0:T(8,128)S(1)}, f32[2,256,1024]{2,1,0:T(8,128)}, u32[]{:S(2)}) copy-start(f32[2,256,1024]{2,1,0:T(8,128)} %ms.5) | copy-start | bytes 6291460
  115.8 25.7 %copy-start.1 = (bf16[2,256,1024]{2,1,0:T(8,128)(2,1)S(1)}, bf16[2,256,1024]{2,1,0:T(8,128)(2,1)}, u32[]{:S(2)}) copy-start(bf16[2,256,1024]{2,1,0:T(8,128)(2,1)} %gs.5) | copy-start | bytes 3145732
  115.8 25.7 %copy-start.2 = (f32[2,256,128]{2,1,0:T(8,128)S(1)}, f32[2,256,128]{2,1,0:T(8,128)}, u32[]{:S(2)}) copy-start(f32[2,256,128]{2,1,0:T(8,128)} %mn.5) | copy-start | bytes 786436
  115.9 25.7 %copy-start.3 = (bf16[2,256,128]{2,1,0:T(8,128)(2,1)S(1)}, bf16[2,256,128]{2,1,0:T(8,128)(2,1)}, u32[]{:S(2)}) copy-start(bf16[2,256,128]{2,1,0:T(8,128)(2,1)} %gn.5) | copy-start | bytes 393220
  116.5 17.9 %collective-permute-start.22 = (f32[8,72,256]{2,1,0:T(8,128)S(1)}, f32[8,72,256]{2,1,0:T(8,128)S(1)}, u32[]{:S(2)}, u32[]{:S(2)}) collective-permute-start(f32[8,72,256]{2,1,0:T(8,128)S(1)} %arrange.1.w0), channel_id=1, source_target_pairs={{0,40},{1,249},{2,42},{3,251},{4,44},{5,253},{6,46},{7,255},{8,32}... | collective-permute-start | bytes 1769480 | tf_op jit(solution)/shard_map/ppermute | solution.py:273
  119.6 14.8 %collective-permute-start.21 = (f32[8,72,256]{2,1,0:T(8,128)S(1)}, f32[8,72,256]{2,1,0:T(8,128)S(1)}, u32[]{:S(2)}, u32[]{:S(2)}) collective-permute-start(f32[8,72,256]{2,1,0:T(8,128)S(1)} %arrange.1.w0), channel_id=1, source_target_pairs={{0,32},{1,225},{2,34},{3,227},{4,36},{5,229},{6,38},{7,231},{8,40}... | collective-permute-start | bytes 1769480 | tf_op jit(solution)/shard_map/ppermute | solution.py:273
  120.8 14.2 %collective-permute-start.20 = (f32[8,72,256]{2,1,0:T(8,128)S(1)}, f32[8,72,256]{2,1,0:T(8,128)S(1)}, u32[]{:S(2)}, u32[]{:S(2)}) collective-permute-start(f32[8,72,256]{2,1,0:T(8,128)S(1)} %arrange.1.w0), channel_id=1, source_target_pairs={{0,8},{1,25},{2,10},{3,27},{4,12},{5,29},{6,14},{7,31},{8,0},{9,17... | collective-permute-start | bytes 1769480 | tf_op jit(solution)/shard_map/ppermute | solution.py:273
  121.7 7.0 %collective-permute-start.19 = (f32[3,128,128]{2,1,0:T(8,128)S(1)}, f32[3,128,128]{2,1,0:T(8,128)S(1)}, u32[]{:S(2)}, u32[]{:S(2)}) collective-permute-start(f32[3,128,128]{2,1,0:T(8,128)S(1)} %factor.1.l0), channel_id=1, source_target_pairs={{0,6},{2,0},{4,2},{6,4},{1,7},{3,1},{5,3},{7,5},{8,14},{10,8},{12,... | collective-permute-start | bytes 589832 | tf_op jit(solution)/shard_map/ppermute | solution.py:259
  122.5 9.0 %collective-permute-start.18 = (f32[3,128,128]{2,1,0:T(8,128)S(1)}, f32[3,128,128]{2,1,0:T(8,128)S(1)}, u32[]{:S(2)}, u32[]{:S(2)}) collective-permute-start(f32[3,128,128]{2,1,0:T(8,128)S(1)} %factor.1.l0), channel_id=1, source_target_pairs={{0,4},{2,6},{4,0},{6,2},{1,5},{3,7},{5,1},{7,3},{8,12},{10,14},{12... | collective-permute-start | bytes 589832 | tf_op jit(solution)/shard_map/ppermute | solution.py:259
  128.6 5.7 %collective-permute-start.17 = (f32[3,128,128]{2,1,0:T(8,128)S(1)}, f32[3,128,128]{2,1,0:T(8,128)S(1)}, u32[]{:S(2)}, u32[]{:S(2)}) collective-permute-start(f32[3,128,128]{2,1,0:T(8,128)S(1)} %factor.1.l0), channel_id=1, source_target_pairs={{0,2},{2,4},{4,6},{6,0},{1,3},{3,5},{5,7},{7,1},{8,10},{10,12},{12... | collective-permute-start | bytes 589832 | tf_op jit(solution)/shard_map/ppermute | solution.py:259
  137.4 1.3 collective-permute-start.23
  138.7 6.1 %collective-permute-start.26 = (f32[8,256]{1,0:T(8,128)S(1)}, f32[8,256]{1,0:T(8,128)S(1)}, u32[]{:S(2)}, u32[]{:S(2)}) collective-permute-start(f32[8,256]{1,0:T(8,128)S(1)} %add.41.q0), channel_id=1, source_target_pairs={{0,6},{2,0},{4,2},{6,4},{1,7},{3,1},{5,3},{7,5},{8,14},{10,8},{12,... | collective-permute-start | bytes 24584 | tf_op jit(solution)/shard_map/ppermute | solution.py:259
  139.5 5.3 %collective-permute-start.25 = (f32[8,256]{1,0:T(8,128)S(1)}, f32[8,256]{1,0:T(8,128)S(1)}, u32[]{:S(2)}, u32[]{:S(2)}) collective-permute-start(f32[8,256]{1,0:T(8,128)S(1)} %add.41.q0), channel_id=1, source_target_pairs={{0,4},{2,6},{4,0},{6,2},{1,5},{3,7},{5,1},{7,3},{8,12},{10,14},{12... | collective-permute-start | bytes 24584 | tf_op jit(solution)/shard_map/ppermute | solution.py:259
  141.6 3.7 %collective-permute-start.24 = (f32[8,256]{1,0:T(8,128)S(1)}, f32[8,256]{1,0:T(8,128)S(1)}, u32[]{:S(2)}, u32[]{:S(2)}) collective-permute-start(f32[8,256]{1,0:T(8,128)S(1)} %add.41.q0), channel_id=1, source_target_pairs={{0,2},{2,4},{4,6},{6,0},{1,3},{3,5},{5,7},{7,1},{8,10},{10,12},{12... | collective-permute-start | bytes 24584 | tf_op jit(solution)/shard_map/ppermute | solution.py:259

commit v5 on v4

--- a/solution.py
+++ b/solution.py
@@ -82,24 +82,27 @@
     return copies
 
 
-def back_kernel(place, ms, gs, mn, gn, own_half, other_half, left, own, to_y, to_z, to_d,
-                w, gram, ms_in, gs_in, mn_in, gn_in, sem):
-    copies = fetch((ms, gs, mn, gn), (ms_in, gs_in, mn_in, gn_in), sem)
+def prepare_kernel(place, ms, gs, mn, gn, high_s, low_s, high_n, low_n, ms_in, gs_in, mn_in, gn_in, sem):
+    for copy in fetch((ms, gs, mn, gn), (ms_in, gs_in, mn_in, gn_in), sem):
+        copy.wait()
+    for k in range(4):
+        m, g, high, low = (ms_in, gs_in, high_s, low_s) if k < 2 else (mn_in, gn_in, high_n, low_n)
+        high[k % 2], low[k % 2] = split((m[k % 2] + g[k % 2].astype(F32)).T)
+
+
+def back_kernel(place, high_s, low_s, high_n, low_n, own_half, other_half, left, own, to_y, to_z, to_d, w, gram):
     core, x, q = place[0], place[1], place[2]
     for i in range(4):
+        at = ((x - i) & 3) * 32
         for k in range(4):
-            left[k, pl.ds(pl.multiple_of(core * 128 + i * 32, 32), 32), :] = own_half[i, k]
-            left[k, pl.ds(pl.multiple_of((1 - core) * 128 + i * 32, 32), 32), :] = other_half[i, k]
+            left[k, pl.ds(pl.multiple_of(core * 128 + at, 32), 32), :] = own_half[i, k]
+            left[k, pl.ds(pl.multiple_of((1 - core) * 128 + at, 32), 32), :] = other_half[i, k]
     half = left[x, :, pl.ds(pl.multiple_of(core * 128, 128), 128)]
     gram[...] = dot3(split(half), split(left[x]), TN)
-    for copy in copies:
-        copy.wait()
     for k in range(2):
-        buffer = split(ms_in[k] + gs_in[k].astype(F32))
-        w[:, k * SQ:(k + 1) * SQ, :] = dot3(buffer, split(left[k]), TN).reshape(32, SQ, RANK)
+        w[:, k * SQ:(k + 1) * SQ, :] = dot3((high_s[k], low_s[k]), split(left[k]), NN).reshape(32, SQ, RANK)
     for k in range(2):
-        buffer = split(mn_in[k] + gn_in[k].astype(F32))
-        w[k * 16:(k + 1) * 16, 2 * SQ:, :] = dot3(buffer, split(left[2 + k]), TN).reshape(16, NA, RANK)
+        w[k * 16:(k + 1) * 16, 2 * SQ:, :] = dot3((high_n[k], low_n[k]), split(left[2 + k]), NN).reshape(16, NA, RANK)
     for j, out in enumerate((own, to_y, to_z, to_d)):
         out[:8 * CHUNK] = w[pl.ds((q ^ j) * 8, 8)].reshape(8 * CHUNK, RANK)
         out[8 * CHUNK:] = gram[pl.ds(pl.multiple_of((q ^ j) * 32, 32), 32), :]
@@ -116,11 +119,21 @@
         out[2 * CHUNK:] = gram
 
 
-def factor_kernel(place, g0, g1, g2, g3, out, w):
+def stack_kernel(place, a0, a1, a2, a3, out):
+    for i, a in enumerate((a0, a1, a2, a3)):
+        out[i] = a[...]
+
+
+def stack(place, arrays):
+    return call(stack_kernel, [((4,) + arrays[0].shape, F32)], (place, *arrays), name="stack")
+
+
+def factor_kernel(place, own_half, other_half, out, w):
     n, nb, step = RANK, 64, 8
-    for j, g in enumerate((g0, g1, g2, g3)):
-        for half in range(2):
-            w[pl.ds(pl.multiple_of(half * 128 + (place[2] ^ j) * 32, 32), 32), :n] = g[half]
+    core, q = place[0], place[2]
+    for j in range(4):
+        w[pl.ds(pl.multiple_of(core * 128 + (q ^ j) * 32, 32), 32), :n] = own_half[j]
+        w[pl.ds(pl.multiple_of((1 - core) * 128 + (q ^ j) * 32, 32), 32), :n] = other_half[j]
     row = lax.broadcasted_iota(jnp.int32, (n, n), 0)
     col = lax.broadcasted_iota(jnp.int32, (n, n), 1)
     w[:, n:] = jnp.where(row == col, 1.0, 0.0)
@@ -253,10 +266,14 @@
     return near, far, perm(lambda z, y, c: (z + 4, y))
 
 
+def shift_x(value, d):
+    return lax.ppermute(value, "x", [(i, (i + d) % 4) for i in range(4)])
+
+
 def around_x(value):
     got = {0: value}
     for d in (2, 1, 3):
-        got[d] = lax.ppermute(value, "x", [(i, (i + d) % 4) for i in range(4)])
+        got[d] = shift_x(value, d)
     return [got[d] for d in range(4)]
 
 
@@ -271,7 +288,6 @@
     place = jnp.stack([lax.axis_index("core"), lax.axis_index("x"), q, b, yh]).astype(jnp.int32)
     near, far, across = partners()
     send = lambda value, pairs: lax.ppermute(value, AXES, pairs)
-    spread = lambda value, axes, n: lax.all_to_all(jnp.broadcast_to(value[None], (n,) + value.shape), axes, 0, 0)
     inputs = (mom_square, grad_square, basis_square, mom_narrow, grad_narrow, basis_narrow)
 
     buffers = (mom_square, grad_square, mom_narrow, grad_narrow)
@@ -288,34 +304,43 @@
         far_in=range(1, 7),
     )
     half = mine + swap_core(theirs)
-    part = jnp.sum(lax.all_to_all(half, "x", 0, 0), axis=0)
-    own_half = spread(part, "x", 4)
+    chunks = [lax.dynamic_index_in_dim(half, (lax.axis_index("x") + d) % 4, 0, keepdims=False) for d in range(4)]
+    chunks, buffers_late = lax.optimization_barrier((chunks, buffers))
+    got = [shift_x(chunks[d], d) for d in (2, 1, 3)]
+    transposes = call(
+        prepare_kernel,
+        [(v, BF16) for v in ((2, 1024, 256),) * 2 + ((2, 128, 256),) * 2],
+        (place,) + buffers_late,
+        fetched,
+        name="prepare",
+        far_in=range(1, 5),
+    )
+    got, transposes = lax.optimization_barrier((got, transposes))
+    own_half = jnp.stack(around_x((chunks[0] + got[0]) + (got[1] + got[2])))
     other_half = swap_core(own_half)
 
     left, own, *others = call(
         back_kernel,
         [((4, 256, RANK), F32)] + [((8 * CHUNK + 32, RANK), F32)] * 4,
-        (place,) + buffers + (own_half, other_half),
-        [pltpu.VMEM((32, CHUNK, RANK), F32), pltpu.VMEM((128, RANK), F32)] + fetched,
+        (place, *transposes, own_half, other_half),
+        [pltpu.VMEM((32, CHUNK, RANK), F32), pltpu.VMEM((128, RANK), F32)],
         name="back",
-        far_in=range(1, 5),
-    )
-    got = [send(value, pairs) for value, pairs in zip(others, near)]
+    )
+    got = [send(value, pairs) for value, pairs in zip(others[::-1], near[::-1])][::-1]
     mine, *others = call(meet_kernel, [((2 * CHUNK + 32, RANK), F32)] * 4, (place, own, *got), name="meet")
-    got = [send(value, pairs) for value, pairs in zip(others, far)]
+    got = [send(value, pairs) for value, pairs in zip(others[::-1], far[::-1])][::-1]
     own = mine + got[0] + got[1] + got[2]
     part = lambda i: jnp.concatenate([lax.dynamic_slice(own, (i * CHUNK, 0), (CHUNK, RANK)), own[2 * CHUNK:]])
     own = part(a) + send(part(1 - a), across)
     own, gram = own[:CHUNK], own[CHUNK:]
     got = send(own, across)
+    (gram,) = stack(place, [gram] + [send(gram, pairs) for pairs in near])
+    gram, got = lax.optimization_barrier((gram, got))
     other_gram = swap_core(gram)
-    gram = jnp.where(place[0] == 0, jnp.stack([gram, other_gram]), jnp.stack([other_gram, gram]))
-    grams = [gram] + [send(gram, pairs) for pairs in near]
-    grams, got = lax.optimization_barrier((grams, got))
     (blocks,) = call(
         factor_kernel,
         [((3, 128, 128), F32)],
-        (place, *grams),
+        (place, gram, other_gram),
         [pltpu.VMEM((RANK, 2 * RANK), F32)],
         name="factor",
     )

time: 150 us -> 144 us (0.960)
  blocking collectives: 22.3 us -> 0 us
  waiting for transfers between devices: 39.7 us -> 56.1 us
  Pallas kernels: 27.5 us -> 29.3 us
    all_to_all x2 -> x0, blocking collectives: 22.3 us -> none  [the longest x1 11.6 us: local(): part = jnp.sum(lax.all_to_all(half, 'x', 0, 0), axis=0)]
    ppermute x6 -> x12, waiting for transfers between devices: 8.21 us -> 22.5 us  [shift_x(): return lax.ppermute(value, 'x', [(i, (i + d) % 4) for i in range(4)])]
    ppermute x4, starting transfers between devices: 6.87 us -> 4.78 us  [swap_core(): return lax.ppermute(value, 'core', [(0, 1), (1, 0)])]
    pallas_call x8 -> x10, Pallas kernels: 27.5 us -> 29.3 us  [call(): pl.pallas_call(kernel, out_shape=[jax.ShapeDtypeStruct(s, d) for s, d in...]
    ppermute x6 -> x12, starting transfers between devices: 7.88 us -> 8.63 us  [shift_x(): return lax.ppermute(value, 'x', [(i, (i + d) % 4) for i in range(4)])]
  transfers between devices with their start and end apart: 27 -> 33, of which waited for: 16 -> 21; matrix products, arithmetic and copies ran while one was open for 0% -> 0% of each run, Pallas kernels for 8% -> 11%
where the time goes in v5:
time: 144 us; the launch traced here: 143 us
  starting transfers between devices  56.5 us (39%)
  waiting for transfers between devices  56.1 us (39%)
  Pallas kernels  29.3 us (20%)
    ppermute x17, starting transfers between devices, local(): send = lambda value, pairs: lax.ppermute(value, AXES, pairs)  43.1 us
    pallas_call x10, Pallas kernels, call(): pl.pallas_call(kernel, out_shape=[jax.ShapeDtypeStruct(s, d) for s, d in...  29.3 us
    ppermute x17, waiting for transfers between devices, local(): send = lambda value, pairs: lax.ppermute(value, AXES, pairs)  28 us
    ppermute x12, waiting for transfers between devices, shift_x(): return lax.ppermute(value, 'x', [(i, (i + d) % 4) for i in range(4)])  22.5 us
    ppermute x12, starting transfers between devices, shift_x(): return lax.ppermute(value, 'x', [(i, (i + d) % 4) for i in range(4)])  8.63 us
    ppermute x4, waiting for transfers between devices, swap_core(): return lax.ppermute(value, 'core', [(0, 1), (1, 0)])  5.58 us
    ppermute x4, starting transfers between devices, swap_core(): return lax.ppermute(value, 'core', [(0, 1), (1, 0)])  4.78 us
  transfers between devices with their start and end apart: 33, of which 21 were waited for; matrix products, arithmetic and copies ran while one was open for 0% of the time, Pallas kernels for 11%

profile of v5, /device:TPU:1, one launch (start us, length us, event | category | flops | bytes accessed | tf_op | source)
XLA Modules:
  0.0 143.5 jit_solution(2174495916167384772)
XLA Ops:
  0.7 0.1 stack.53.place
  0.7 4.7 %project.1 = (f32[4,4,32,256]{3,2,1,0:T(8,128)S(1)}, f32[4,4,32,256]{3,2,1,0:T(8,128)S(1)}) custom-call(s32[5]{0:T(128)S(1)} %stack.53.place, f32[2,256,1024]{2,1,0:T(8,128)} %ms.4, bf16[2,256,1024]{2,1,0:T(8,128)(2,1)} %gs.4, f32[2,1024,256]{2,1,0:T(8,128)} %qs.1, f32[2,256,128]{2,1,0:T(8,128)} %mn.4, bf16[2,256,128]{2,1,0:T(8,128)(2,1)} %gn.4, ...), custom_call_target="tpu_custom_call" | custom-call | tf_op jit(solution)/shard_map/project/pallas_call | solution.py:39
  5.4 3.3 %collective-permute-start = (f32[4,4,32,256]{3,2,1,0:T(8,128)S(1)}, f32[4,4,32,256]{3,2,1,0:T(8,128)S(1)}, u32[]{:S(2)}, u32[]{:S(2)}) collective-permute-start(f32[4,4,32,256]{3,2,1,0:T(8,128)S(1)} %get-tuple-element.56), channel_id=1, source_target_pairs={{0,1},{1,0},{2,3},{3,2},{4,5},{5,4},{6,7},{7,6},{8,9},{9,8},{10,11... | collective-permute-start | bytes 1572872 | tf_op jit(solution)/shard_map/ppermute | solution.py:281
  8.8 1.5 %collective-permute-done = f32[4,4,32,256]{3,2,1,0:T(8,128)S(1)} collective-permute-done((f32[4,4,32,256]{3,2,1,0:T(8,128)S(1)}, f32[4,4,32,256]{3,2,1,0:T(8,128)S(1)}, u32[]{:S(2)}, u32[]{:S(2)}) %collective-permute-start) | collective-permute-done | bytes 524320 | tf_op jit(solution)/shard_map/ppermute | solution.py:281
  10.3 0.1 add.77
  10.4 1.1 collective-permute-start.1
  11.5 0.3 collective-permute-start.2
  11.8 2.4 %collective-permute-start.3 = (f32[4,32,256]{2,1,0:T(8,128)S(1)}, f32[4,32,256]{2,1,0:T(8,128)S(1)}, u32[]{:S(2)}, u32[]{:S(2)}) collective-permute-start(f32[4,32,256]{2,1,0:T(8,128)S(1)} %get-tuple-element.59), channel_id=1, source_target_pairs={{0,6},{2,0},{4,2},{6,4},{1,7},{3,1},{5,3},{7,5},{8,14},{10,8},{12,... | collective-permute-start | bytes 393224 | tf_op jit(solution)/shard_map/ppermute | solution.py:270
  14.2 3.2 %prepare.1 = (bf16[2,1024,256]{2,1,0:T(8,128)(2,1)S(1)}, bf16[2,1024,256]{2,1,0:T(8,128)(2,1)S(1)}, bf16[2,128,256]{2,1,0:T(8,128)(2,1)S(1)}, bf16[2,128,256]{2,1,0:T(8,128)(2,1)S(1)}) custom-call(s32[5]{0:T(128)S(1)} %stack.53.place, f32[2,256,1024]{2,1,0:T(8,128)} %ms.4, bf16[2,256,1024]{2,1,0:T(8,128)(2,1)} %gs.4, f32[2,256,128]{2,1,0:T(8,128)} %mn.4, ...), custom_call_target="tpu_custom_call" | custom-call | tf_op jit(solution)/shard_map/prepare/pallas_call | solution.py:39
  17.4 2.8 %collective-permute-done.2 = f32[4,32,256]{2,1,0:T(8,128)S(1)} collective-permute-done((f32[4,32,256]{2,1,0:T(8,128)S(1)}, f32[4,32,256]{2,1,0:T(8,128)S(1)}, u32[]{:S(2)}, u32[]{:S(2)}) %collective-permute-start.2) | collective-permute-done | bytes 131104 | tf_op jit(solution)/shard_map/ppermute | solution.py:270
  20.3 0.3 collective-permute-start.6
  20.6 0.9 collective-permute-start.5
  21.5 0.8 collective-permute-start.4
  22.2 2.7 %collective-permute-done.6 = f32[4,32,256]{2,1,0:T(8,128)S(1)} collective-permute-done((f32[4,32,256]{2,1,0:T(8,128)S(1)}, f32[4,32,256]{2,1,0:T(8,128)S(1)}, u32[]{:S(2)}, u32[]{:S(2)}) %collective-permute-start.6) | collective-permute-done | bytes 131104 | tf_op jit(solution)/shard_map/ppermute | solution.py:270
  25.0 1.0 collective-permute-done.5
  26.0 3.6 %collective-permute-done.4 = f32[4,32,256]{2,1,0:T(8,128)S(1)} collective-permute-done((f32[4,32,256]{2,1,0:T(8,128)S(1)}, f32[4,32,256]{2,1,0:T(8,128)S(1)}, u32[]{:S(2)}, u32[]{:S(2)}) %collective-permute-start.4) | collective-permute-done | bytes 131104 | tf_op jit(solution)/shard_map/ppermute | solution.py:270
  29.6 1.4 collective-permute-start.7
  30.9 1.5 %collective-permute-done.7.other_half = f32[4,4,32,256]{3,2,1,0:T(8,128)S(1)} collective-permute-done((f32[4,4,32,256]{3,2,1,0:T(8,128)S(1)}, f32[4,4,32,256]{3,2,1,0:T(8,128)S(1)}, u32[]{:S(2)}, u32[]{:S(2)}) %collective-permute-start.7) | collective-permute-done | bytes 524320 | tf_op jit(solution)/shard_map/ppermute | solution.py:281
  32.5 1.9 %back.1 = (f32[4,256,256]{2,1,0:T(8,128)S(1)}, f32[608,256]{1,0:T(8,128)S(1)}, f32[608,256]{1,0:T(8,128)S(1)}, f32[608,256]{1,0:T(8,128)S(1)}, f32[608,256]{1,0:T(8,128)S(1)}) custom-call(s32[5]{0:T(128)S(1)} %stack.53.place, bf16[2,1024,256]{2,1,0:T(8,128)(2,1)S(1)} %get-tuple-element.68.high_s, bf16[2,1024,256]{2,1,0:T(8,128)(2,1)S(1)} %get-tuple-element.69.low_s, ...), custom_call_target="tpu_custom_call" | custom-call | tf_op jit(solution)/shard_map/back/pallas_call | solution.py:39
  34.4 2.8 %collective-permute-start.8 = (f32[608,256]{1,0:T(8,128)S(1)}, f32[608,256]{1,0:T(8,128)S(1)}, u32[]{:S(2)}, u32[]{:S(2)}) collective-permute-start(f32[608,256]{1,0:T(8,128)S(1)} %get-tuple-element.77), channel_id=1, source_target_pairs={{0,8},{1,25},{2,10},{3,27},{4,12},{5,29},{6,14},{7,31},{8,0},{9,17... | collective-permute-start | bytes 1867784 | tf_op jit(solution)/shard_map/ppermute | solution.py:290
  37.2 5.6 %collective-permute-start.9 = (f32[608,256]{1,0:T(8,128)S(1)}, f32[608,256]{1,0:T(8,128)S(1)}, u32[]{:S(2)}, u32[]{:S(2)}) collective-permute-start(f32[608,256]{1,0:T(8,128)S(1)} %get-tuple-element.78), channel_id=1, source_target_pairs={{0,32},{1,225},{2,34},{3,227},{4,36},{5,229},{6,38},{7,231},{8,40}... | collective-permute-start | bytes 1867784 | tf_op jit(solution)/shard_map/ppermute | solution.py:290
  42.8 2.1 %collective-permute-done.8.r0 = f32[608,256]{1,0:T(8,128)S(1)} collective-permute-done((f32[608,256]{1,0:T(8,128)S(1)}, f32[608,256]{1,0:T(8,128)S(1)}, u32[]{:S(2)}, u32[]{:S(2)}) %collective-permute-start.8) | collective-permute-done | bytes 622624 | tf_op jit(solution)/shard_map/ppermute | solution.py:290
  44.9 5.7 %collective-permute-done.9.r1 = f32[608,256]{1,0:T(8,128)S(1)} collective-permute-done((f32[608,256]{1,0:T(8,128)S(1)}, f32[608,256]{1,0:T(8,128)S(1)}, u32[]{:S(2)}, u32[]{:S(2)}) %collective-permute-start.9) | collective-permute-done | bytes 622624 | tf_op jit(solution)/shard_map/ppermute | solution.py:290
  50.6 6.4 %collective-permute-done.10.r2 = f32[608,256]{1,0:T(8,128)S(1)} collective-permute-done((f32[608,256]{1,0:T(8,128)S(1)}, f32[608,256]{1,0:T(8,128)S(1)}, u32[]{:S(2)}, u32[]{:S(2)}) %collective-permute-start.10) | collective-permute-done | bytes 622624 | tf_op jit(solution)/shard_map/ppermute | solution.py:290
  56.9 0.7 meet.1
  57.6 1.6 %collective-permute-start.11 = (f32[176,256]{1,0:T(8,128)S(1)}, f32[176,256]{1,0:T(8,128)S(1)}, u32[]{:S(2)}, u32[]{:S(2)}) collective-permute-start(f32[176,256]{1,0:T(8,128)S(1)} %get-tuple-element.81), channel_id=1, source_target_pairs={{0,16},{1,17},{2,18},{3,19},{4,20},{5,21},{6,22},{7,23},{8,24},{9,... | collective-permute-start | bytes 540680 | tf_op jit(solution)/shard_map/ppermute | solution.py:290
  59.2 2.2 %collective-permute-start.12 = (f32[176,256]{1,0:T(8,128)S(1)}, f32[176,256]{1,0:T(8,128)S(1)}, u32[]{:S(2)}, u32[]{:S(2)}) collective-permute-start(f32[176,256]{1,0:T(8,128)S(1)} %get-tuple-element.82), channel_id=1, source_target_pairs={{0,64},{1,193},{2,66},{3,195},{4,68},{5,197},{6,70},{7,199},{8,72}... | collective-permute-start | bytes 540680 | tf_op jit(solution)/shard_map/ppermute | solution.py:290
  61.4 2.5 %collective-permute-start.13 = (f32[176,256]{1,0:T(8,128)S(1)}, f32[176,256]{1,0:T(8,128)S(1)}, u32[]{:S(2)}, u32[]{:S(2)}) collective-permute-start(f32[176,256]{1,0:T(8,128)S(1)} %get-tuple-element.83), channel_id=1, source_target_pairs={{0,80},{1,209},{2,82},{3,211},{4,84},{5,213},{6,86},{7,215},{8,88}... | collective-permute-start | bytes 540680 | tf_op jit(solution)/shard_map/ppermute | solution.py:290
  63.9 1.8 %collective-permute-done.12 = f32[176,256]{1,0:T(8,128)S(1)} collective-permute-done((f32[176,256]{1,0:T(8,128)S(1)}, f32[176,256]{1,0:T(8,128)S(1)}, u32[]{:S(2)}, u32[]{:S(2)}) %collective-permute-start.12) | collective-permute-done | bytes 180256 | tf_op jit(solution)/shard_map/ppermute | solution.py:290
  65.8 5.4 %collective-permute-done.13 = f32[176,256]{1,0:T(8,128)S(1)} collective-permute-done((f32[176,256]{1,0:T(8,128)S(1)}, f32[176,256]{1,0:T(8,128)S(1)}, u32[]{:S(2)}, u32[]{:S(2)}) %collective-permute-start.13) | collective-permute-done | bytes 180256 | tf_op jit(solution)/shard_map/ppermute | solution.py:290
  71.3 5.4 %collective-permute-start.14 = (f32[104,256]{1,0:T(8,128)S(1)}, f32[104,256]{1,0:T(8,128)S(1)}, u32[]{:S(2)}, u32[]{:S(2)}) collective-permute-start(f32[104,256]{1,0:T(8,128)S(1)} %pad_maximum_fusion.1), channel_id=1, source_target_pairs={{0,128},{1,129},{2,130},{3,131},{4,132},{5,133},{6,134},{7,135},{8... | collective-permute-start | bytes 319496 | tf_op jit(solution)/shard_map/ppermute | solution.py:290
  76.7 2.8 %collective-permute-done.14 = f32[104,256]{1,0:T(8,128)S(1)} collective-permute-done((f32[104,256]{1,0:T(8,128)S(1)}, f32[104,256]{1,0:T(8,128)S(1)}, u32[]{:S(2)}, u32[]{:S(2)}) %collective-permute-start.14) | collective-permute-done | bytes 106528 | tf_op jit(solution)/shard_map/ppermute | solution.py:290
  79.5 6.2 %collective-permute-start.18 = (f32[72,256]{1,0:T(8,128)S(1)}, f32[72,256]{1,0:T(8,128)S(1)}, u32[]{:S(2)}, u32[]{:S(2)}) collective-permute-start(f32[72,256]{1,0:T(8,128)S(1)} %get-tuple-element.111), channel_id=1, source_target_pairs={{0,128},{1,129},{2,130},{3,131},{4,132},{5,133},{6,134},{7,135},{8... | collective-permute-start | bytes 221192 | tf_op jit(solution)/shard_map/ppermute | solution.py:290
  85.7 4.5 %collective-permute-start.17 = (f32[32,256]{1,0:T(8,128)S(1)}, f32[32,256]{1,0:T(8,128)S(1)}, u32[]{:S(2)}, u32[]{:S(2)}) collective-permute-start(f32[32,256]{1,0:T(8,128)S(1)} %slice.14.a0), channel_id=1, source_target_pairs={{0,40},{1,249},{2,42},{3,251},{4,44},{5,253},{6,46},{7,255},{8,32}... | collective-permute-start | bytes 98312 | tf_op jit(solution)/shard_map/ppermute | solution.py:290
  90.2 0.4 collective-permute-start.16
  90.6 0.2 collective-permute-start.15
  90.8 1.0 collective-permute-done.17.a3
  91.8 2.4 %collective-permute-done.16.a2 = f32[32,256]{1,0:T(8,128)S(1)} collective-permute-done((f32[32,256]{1,0:T(8,128)S(1)}, f32[32,256]{1,0:T(8,128)S(1)}, u32[]{:S(2)}, u32[]{:S(2)}) %collective-permute-start.16) | collective-permute-done | bytes 32800 | tf_op jit(solution)/shard_map/ppermute | solution.py:290
  94.2 0.4 collective-permute-done.15.a1
  94.6 0.5 stack.63.own_half
  95.2 0.1 collective-permute-start.22
  95.3 1.7 %collective-permute-start.21 = (f32[2,72,256]{2,1,0:T(8,128)S(1)}, f32[2,72,256]{2,1,0:T(8,128)S(1)}, u32[]{:S(2)}, u32[]{:S(2)}) collective-permute-start(f32[2,72,256]{2,1,0:T(8,128)S(1)} %maximum_select_fusion.w0), channel_id=1, source_target_pairs={{0,64},{1,193},{2,66},{3,195},{4,68},{5,197},{6,70},{7,199},{8,72}... | collective-permute-start | bytes 442376 | tf_op jit(solution)/shard_map/ppermute | solution.py:290
  97.0 4.6 %collective-permute-start.20 = (f32[2,72,256]{2,1,0:T(8,128)S(1)}, f32[2,72,256]{2,1,0:T(8,128)S(1)}, u32[]{:S(2)}, u32[]{:S(2)}) collective-permute-start(f32[2,72,256]{2,1,0:T(8,128)S(1)} %maximum_select_fusion.w0), channel_id=1, source_target_pairs={{0,16},{1,17},{2,18},{3,19},{4,20},{5,21},{6,22},{7,23},{8,24},{9,... | collective-permute-start | bytes 442376 | tf_op jit(solution)/shard_map/ppermute | solution.py:290
  101.6 1.3 collective-permute-done.19.other_half
  102.9 9.0 %factor.1.l0 = f32[3,128,128]{2,1,0:T(8,128)S(1)} custom-call(s32[5]{0:T(128)S(1)} %stack.53.place, f32[4,32,256]{2,1,0:T(8,128)S(1)} %stack.63.own_half, f32[4,32,256]{2,1,0:T(8,128)S(1)} %collective-permute-done.19.other_half), custom_call_target="tpu_custom_call" | custom-call | tf_op jit(solution)/shard_map/factor/pallas_call | solution.py:39
  111.9 0.0 copy-start.1
  112.0 0.6 arrange.1.w0
  112.6 2.6 %collective-permute-start.28 = (f32[8,72,256]{2,1,0:T(8,128)S(1)}, f32[8,72,256]{2,1,0:T(8,128)S(1)}, u32[]{:S(2)}, u32[]{:S(2)}) collective-permute-start(f32[8,72,256]{2,1,0:T(8,128)S(1)} %arrange.1.w0), channel_id=1, source_target_pairs={{0,40},{1,249},{2,42},{3,251},{4,44},{5,253},{6,46},{7,255},{8,32}... | collective-permute-start | bytes 1769480 | tf_op jit(solution)/shard_map/ppermute | solution.py:290
  115.2 0.2 collective-permute-start.27
  115.5 2.5 %collective-permute-start.26 = (f32[8,72,256]{2,1,0:T(8,128)S(1)}, f32[8,72,256]{2,1,0:T(8,128)S(1)}, u32[]{:S(2)}, u32[]{:S(2)}) collective-permute-start(f32[8,72,256]{2,1,0:T(8,128)S(1)} %arrange.1.w0), channel_id=1, source_target_pairs={{0,8},{1,25},{2,10},{3,27},{4,12},{5,29},{6,14},{7,31},{8,0},{9,17... | collective-permute-start | bytes 1769480 | tf_op jit(solution)/shard_map/ppermute | solution.py:290
  118.0 0.3 collective-permute-start.25
  118.3 1.1 collective-permute-start.24
  119.3 5.6 %collective-permute-done.25.l3 = f32[3,128,128]{2,1,0:T(8,128)S(1)} collective-permute-done((f32[3,128,128]{2,1,0:T(8,128)S(1)}, f32[3,128,128]{2,1,0:T(8,128)S(1)}, u32[]{:S(2)}, u32[]{:S(2)}) %collective-permute-start.25) | collective-permute-done | bytes 196640 | tf_op jit(solution)/shard_map/ppermute | solution.py:270
  124.9 0.8 collective-permute-done.24.l2
  125.7 5.9 %collective-permute-done.23.l1 = f32[3,128,128]{2,1,0:T(8,128)S(1)} collective-permute-done((f32[3,128,128]{2,1,0:T(8,128)S(1)}, f32[3,128,128]{2,1,0:T(8,128)S(1)}, u32[]{:S(2)}, u32[]{:S(2)}) %collective-permute-start.23) | collective-permute-done | bytes 196640 | tf_op jit(solution)/shard_map/ppermute | solution.py:270
  131.7 2.4 %right.1 = (f32[2,1024,256]{2,1,0:T(8,128)S(1)}, f32[2,128,256]{2,1,0:T(8,128)S(1)}, f32[8,256]{1,0:T(8,128)S(1)}) custom-call(s32[5]{0:T(128)S(1)} %stack.53.place, f32[8,72,256]{2,1,0:T(8,128)S(1)} %arrange.1.w0, f32[8,72,256]{2,1,0:T(8,128)S(1)} %collective-permute-done.26.w1, f32[8,72,256]{2,1,0:T(8,128)S(1)} %collective-permute-done.27.w2, ...), custom_call_target="tpu_custom_call" | custom-call | tf_op jit(solution)/shard_map/right/pallas_call | solution.py:39
  134.1 0.1 collective-permute-start.29
  134.2 1.2 collective-permute-done.29
  135.4 0.4 collective-permute-start.32
  135.8 0.5 collective-permute-start.31
  136.4 0.6 collective-permute-start.30
  136.9 3.2 %momentum.1 = (f32[4,256,256]{2,1,0:T(8,128)S(1)}, f32[2,256,1024]{2,1,0:T(8,128)}, f32[2,256,128]{2,1,0:T(8,128)}) custom-call(s32[5]{0:T(128)S(1)} %stack.53.place, f32[3,128,128]{2,1,0:T(8,128)S(1)} %factor.1.l0, f32[3,128,128]{2,1,0:T(8,128)S(1)} %collective-permute-done.23.l1, f32[3,128,128]{2,1,0:T(8,128)S(1)} %collective-permute-done.24.l2, ...), custom_call_target="tpu_custom_call" | custom-call | tf_op jit(solution)/shard_map/momentum/pallas_call | solution.py:39
  140.2 0.1 collective-permute-done.30.q1
  140.3 3.0 %update.1 = (bf16[2,256,1024]{2,1,0:T(8,128)(2,1)}, f32[2,1024,256]{2,1,0:T(8,128)}, bf16[2,256,128]{2,1,0:T(8,128)(2,1)}, f32[2,128,256]{2,1,0:T(8,128)}) custom-call(s32[5]{0:T(128)S(1)} %stack.53.place, f32[8,256]{1,0:T(8,128)S(1)} %add.98.q0, f32[8,256]{1,0:T(8,128)S(1)} %collective-permute-done.30.q1, f32[8,256]{1,0:T(8,128)S(1)} %collective-permute-done.31.q2, ...), custom_call_target="tpu_custom_call" | custom-call | tf_op jit(solution)/shard_map/update/pallas_call | solution.py:39
  (34 shorter events, 0.3 us)
Async XLA Ops:
  5.4 4.9 %collective-permute-start = (f32[4,4,32,256]{3,2,1,0:T(8,128)S(1)}, f32[4,4,32,256]{3,2,1,0:T(8,128)S(1)}, u32[]{:S(2)}, u32[]{:S(2)}) collective-permute-start(f32[4,4,32,256]{3,2,1,0:T(8,128)S(1)} %get-tuple-element.56), channel_id=1, source_target_pairs={{0,1},{1,0},{2,3},{3,2},{4,5},{5,4},{6,7},{7,6},{8,9},{9,8},{10,11... | collective-permute-start | bytes 1572872 | tf_op jit(solution)/shard_map/ppermute | solution.py:281
  10.4 7.0 %collective-permute-start.1 = (f32[4,32,256]{2,1,0:T(8,128)S(1)}, f32[4,32,256]{2,1,0:T(8,128)S(1)}, u32[]{:S(2)}, u32[]{:S(2)}) collective-permute-start(f32[4,32,256]{2,1,0:T(8,128)S(1)} %get-tuple-element.57), channel_id=1, source_target_pairs={{0,4},{2,6},{4,0},{6,2},{1,5},{3,7},{5,1},{7,3},{8,12},{10,14},{12... | collective-permute-start | bytes 393224 | tf_op jit(solution)/shard_map/ppermute | solution.py:270
  11.5 8.7 %collective-permute-start.2 = (f32[4,32,256]{2,1,0:T(8,128)S(1)}, f32[4,32,256]{2,1,0:T(8,128)S(1)}, u32[]{:S(2)}, u32[]{:S(2)}) collective-permute-start(f32[4,32,256]{2,1,0:T(8,128)S(1)} %get-tuple-element.58), channel_id=1, source_target_pairs={{0,2},{2,4},{4,6},{6,0},{1,3},{3,5},{5,7},{7,1},{8,10},{10,12},{12... | collective-permute-start | bytes 393224 | tf_op jit(solution)/shard_map/ppermute | solution.py:270
  11.8 8.4 %collective-permute-start.3 = (f32[4,32,256]{2,1,0:T(8,128)S(1)}, f32[4,32,256]{2,1,0:T(8,128)S(1)}, u32[]{:S(2)}, u32[]{:S(2)}) collective-permute-start(f32[4,32,256]{2,1,0:T(8,128)S(1)} %get-tuple-element.59), channel_id=1, source_target_pairs={{0,6},{2,0},{4,2},{6,4},{1,7},{3,1},{5,3},{7,5},{8,14},{10,8},{12,... | collective-permute-start | bytes 393224 | tf_op jit(solution)/shard_map/ppermute | solution.py:270
  20.3 4.7 %collective-permute-start.6 = (f32[4,32,256]{2,1,0:T(8,128)S(1)}, f32[4,32,256]{2,1,0:T(8,128)S(1)}, u32[]{:S(2)}, u32[]{:S(2)}) collective-permute-start(f32[4,32,256]{2,1,0:T(8,128)S(1)} %add_add_fusion.1), channel_id=1, source_target_pairs={{0,6},{2,0},{4,2},{6,4},{1,7},{3,1},{5,3},{7,5},{8,14},{10,8},{12,... | collective-permute-start | bytes 393224 | tf_op jit(solution)/shard_map/ppermute | solution.py:270
  20.6 5.4 %collective-permute-start.5 = (f32[4,32,256]{2,1,0:T(8,128)S(1)}, f32[4,32,256]{2,1,0:T(8,128)S(1)}, u32[]{:S(2)}, u32[]{:S(2)}) collective-permute-start(f32[4,32,256]{2,1,0:T(8,128)S(1)} %add_add_fusion.1), channel_id=1, source_target_pairs={{0,4},{2,6},{4,0},{6,2},{1,5},{3,7},{5,1},{7,3},{8,12},{10,14},{12... | collective-permute-start | bytes 393224 | tf_op jit(solution)/shard_map/ppermute | solution.py:270
  21.5 8.0 %collective-permute-start.4 = (f32[4,32,256]{2,1,0:T(8,128)S(1)}, f32[4,32,256]{2,1,0:T(8,128)S(1)}, u32[]{:S(2)}, u32[]{:S(2)}) collective-permute-start(f32[4,32,256]{2,1,0:T(8,128)S(1)} %add_add_fusion.1), channel_id=1, source_target_pairs={{0,2},{2,4},{4,6},{6,0},{1,3},{3,5},{5,7},{7,1},{8,10},{10,12},{12... | collective-permute-start | bytes 393224 | tf_op jit(solution)/shard_map/ppermute | solution.py:270
  29.6 2.9 %collective-permute-start.7 = (f32[4,4,32,256]{3,2,1,0:T(8,128)S(1)}, f32[4,4,32,256]{3,2,1,0:T(8,128)S(1)}, u32[]{:S(2)}, u32[]{:S(2)}) collective-permute-start(f32[4,4,32,256]{3,2,1,0:T(8,128)S(1)} %pad_maximum_fusion.own_half), channel_id=1, source_target_pairs={{0,1},{1,0},{2,3},{3,2},{4,5},{5,4},{6,7},{7,6},{8,9},{9,8},{10,11... | collective-permute-start | bytes 1572872 | tf_op jit(solution)/shard_map/ppermute | solution.py:281
  34.4 10.5 %collective-permute-start.8 = (f32[608,256]{1,0:T(8,128)S(1)}, f32[608,256]{1,0:T(8,128)S(1)}, u32[]{:S(2)}, u32[]{:S(2)}) collective-permute-start(f32[608,256]{1,0:T(8,128)S(1)} %get-tuple-element.77), channel_id=1, source_target_pairs={{0,8},{1,25},{2,10},{3,27},{4,12},{5,29},{6,14},{7,31},{8,0},{9,17... | collective-permute-start | bytes 1867784 | tf_op jit(solution)/shard_map/ppermute | solution.py:290
  37.2 13.3 %collective-permute-start.9 = (f32[608,256]{1,0:T(8,128)S(1)}, f32[608,256]{1,0:T(8,128)S(1)}, u32[]{:S(2)}, u32[]{:S(2)}) collective-permute-start(f32[608,256]{1,0:T(8,128)S(1)} %get-tuple-element.78), channel_id=1, source_target_pairs={{0,32},{1,225},{2,34},{3,227},{4,36},{5,229},{6,38},{7,231},{8,40}... | collective-permute-start | bytes 1867784 | tf_op jit(solution)/shard_map/ppermute | solution.py:290
  42.8 14.1 %collective-permute-start.10 = (f32[608,256]{1,0:T(8,128)S(1)}, f32[608,256]{1,0:T(8,128)S(1)}, u32[]{:S(2)}, u32[]{:S(2)}) collective-permute-start(f32[608,256]{1,0:T(8,128)S(1)} %get-tuple-element.79), channel_id=1, source_target_pairs={{0,40},{1,249},{2,42},{3,251},{4,44},{5,253},{6,46},{7,255},{8,32}... | collective-permute-start | bytes 1867784 | tf_op jit(solution)/shard_map/ppermute | solution.py:290
  57.6 6.4 %collective-permute-start.11 = (f32[176,256]{1,0:T(8,128)S(1)}, f32[176,256]{1,0:T(8,128)S(1)}, u32[]{:S(2)}, u32[]{:S(2)}) collective-permute-start(f32[176,256]{1,0:T(8,128)S(1)} %get-tuple-element.81), channel_id=1, source_target_pairs={{0,16},{1,17},{2,18},{3,19},{4,20},{5,21},{6,22},{7,23},{8,24},{9,... | collective-permute-start | bytes 540680 | tf_op jit(solution)/shard_map/ppermute | solution.py:290
  59.2 6.6 %collective-permute-start.12 = (f32[176,256]{1,0:T(8,128)S(1)}, f32[176,256]{1,0:T(8,128)S(1)}, u32[]{:S(2)}, u32[]{:S(2)}) collective-permute-start(f32[176,256]{1,0:T(8,128)S(1)} %get-tuple-element.82), channel_id=1, source_target_pairs={{0,64},{1,193},{2,66},{3,195},{4,68},{5,197},{6,70},{7,199},{8,72}... | collective-permute-start | bytes 540680 | tf_op jit(solution)/shard_map/ppermute | solution.py:290
  61.4 9.8 %collective-permute-start.13 = (f32[176,256]{1,0:T(8,128)S(1)}, f32[176,256]{1,0:T(8,128)S(1)}, u32[]{:S(2)}, u32[]{:S(2)}) collective-permute-start(f32[176,256]{1,0:T(8,128)S(1)} %get-tuple-element.83), channel_id=1, source_target_pairs={{0,80},{1,209},{2,82},{3,211},{4,84},{5,213},{6,86},{7,215},{8,88}... | collective-permute-start | bytes 540680 | tf_op jit(solution)/shard_map/ppermute | solution.py:290
  71.3 8.2 %collective-permute-start.14 = (f32[104,256]{1,0:T(8,128)S(1)}, f32[104,256]{1,0:T(8,128)S(1)}, u32[]{:S(2)}, u32[]{:S(2)}) collective-permute-start(f32[104,256]{1,0:T(8,128)S(1)} %pad_maximum_fusion.1), channel_id=1, source_target_pairs={{0,128},{1,129},{2,130},{3,131},{4,132},{5,133},{6,134},{7,135},{8... | collective-permute-start | bytes 319496 | tf_op jit(solution)/shard_map/ppermute | solution.py:290
  79.5 15.6 %collective-permute-start.18 = (f32[72,256]{1,0:T(8,128)S(1)}, f32[72,256]{1,0:T(8,128)S(1)}, u32[]{:S(2)}, u32[]{:S(2)}) collective-permute-start(f32[72,256]{1,0:T(8,128)S(1)} %get-tuple-element.111), channel_id=1, source_target_pairs={{0,128},{1,129},{2,130},{3,131},{4,132},{5,133},{6,134},{7,135},{8... | collective-permute-start | bytes 221192 | tf_op jit(solution)/shard_map/ppermute | solution.py:290
  85.7 6.1 %collective-permute-start.17 = (f32[32,256]{1,0:T(8,128)S(1)}, f32[32,256]{1,0:T(8,128)S(1)}, u32[]{:S(2)}, u32[]{:S(2)}) collective-permute-start(f32[32,256]{1,0:T(8,128)S(1)} %slice.14.a0), channel_id=1, source_target_pairs={{0,40},{1,249},{2,42},{3,251},{4,44},{5,253},{6,46},{7,255},{8,32}... | collective-permute-start | bytes 98312 | tf_op jit(solution)/shard_map/ppermute | solution.py:290
  90.2 4.0 %collective-permute-start.16 = (f32[32,256]{1,0:T(8,128)S(1)}, f32[32,256]{1,0:T(8,128)S(1)}, u32[]{:S(2)}, u32[]{:S(2)}) collective-permute-start(f32[32,256]{1,0:T(8,128)S(1)} %slice.14.a0), channel_id=1, source_target_pairs={{0,32},{1,225},{2,34},{3,227},{4,36},{5,229},{6,38},{7,231},{8,40}... | collective-permute-start | bytes 98312 | tf_op jit(solution)/shard_map/ppermute | solution.py:290
  90.6 4.0 %collective-permute-start.15 = (f32[32,256]{1,0:T(8,128)S(1)}, f32[32,256]{1,0:T(8,128)S(1)}, u32[]{:S(2)}, u32[]{:S(2)}) collective-permute-start(f32[32,256]{1,0:T(8,128)S(1)} %slice.14.a0), channel_id=1, source_target_pairs={{0,8},{1,25},{2,10},{3,27},{4,12},{5,29},{6,14},{7,31},{8,0},{9,17... | collective-permute-start | bytes 98312 | tf_op jit(solution)/shard_map/ppermute | solution.py:290
  95.2 16.8 %collective-permute-start.22 = (f32[2,72,256]{2,1,0:T(8,128)S(1)}, f32[2,72,256]{2,1,0:T(8,128)S(1)}, u32[]{:S(2)}, u32[]{:S(2)}) collective-permute-start(f32[2,72,256]{2,1,0:T(8,128)S(1)} %maximum_select_fusion.w0), channel_id=1, source_target_pairs={{0,80},{1,209},{2,82},{3,211},{4,84},{5,213},{6,86},{7,215},{8,88}... | collective-permute-start | bytes 442376 | tf_op jit(solution)/shard_map/ppermute | solution.py:290
  95.3 16.7 %collective-permute-start.21 = (f32[2,72,256]{2,1,0:T(8,128)S(1)}, f32[2,72,256]{2,1,0:T(8,128)S(1)}, u32[]{:S(2)}, u32[]{:S(2)}) collective-permute-start(f32[2,72,256]{2,1,0:T(8,128)S(1)} %maximum_select_fusion.w0), channel_id=1, source_target_pairs={{0,64},{1,193},{2,66},{3,195},{4,68},{5,197},{6,70},{7,199},{8,72}... | collective-permute-start | bytes 442376 | tf_op jit(solution)/shard_map/ppermute | solution.py:290
  97.0 15.0 %collective-permute-start.20 = (f32[2,72,256]{2,1,0:T(8,128)S(1)}, f32[2,72,256]{2,1,0:T(8,128)S(1)}, u32[]{:S(2)}, u32[]{:S(2)}) collective-permute-start(f32[2,72,256]{2,1,0:T(8,128)S(1)} %maximum_select_fusion.w0), channel_id=1, source_target_pairs={{0,16},{1,17},{2,18},{3,19},{4,20},{5,21},{6,22},{7,23},{8,24},{9,... | collective-permute-start | bytes 442376 | tf_op jit(solution)/shard_map/ppermute | solution.py:290
  101.6 1.3 collective-permute-start.19
  111.9 25.0 %copy-start = (f32[2,256,1024]{2,1,0:T(8,128)S(1)}, f32[2,256,1024]{2,1,0:T(8,128)}, u32[]{:S(2)}) copy-start(f32[2,256,1024]{2,1,0:T(8,128)} %ms.4) | copy-start | bytes 6291460
  111.9 25.0 %copy-start.1 = (bf16[2,256,1024]{2,1,0:T(8,128)(2,1)S(1)}, bf16[2,256,1024]{2,1,0:T(8,128)(2,1)}, u32[]{:S(2)}) copy-start(bf16[2,256,1024]{2,1,0:T(8,128)(2,1)} %gs.4) | copy-start | bytes 3145732
  112.0 25.0 %copy-start.2 = (f32[2,256,128]{2,1,0:T(8,128)S(1)}, f32[2,256,128]{2,1,0:T(8,128)}, u32[]{:S(2)}) copy-start(f32[2,256,128]{2,1,0:T(8,128)} %mn.4) | copy-start | bytes 786436
  112.0 25.0 %copy-start.3 = (bf16[2,256,128]{2,1,0:T(8,128)(2,1)S(1)}, bf16[2,256,128]{2,1,0:T(8,128)(2,1)}, u32[]{:S(2)}) copy-start(bf16[2,256,128]{2,1,0:T(8,128)(2,1)} %gn.4) | copy-start | bytes 393220
  112.6 19.1 %collective-permute-start.28 = (f32[8,72,256]{2,1,0:T(8,128)S(1)}, f32[8,72,256]{2,1,0:T(8,128)S(1)}, u32[]{:S(2)}, u32[]{:S(2)}) collective-permute-start(f32[8,72,256]{2,1,0:T(8,128)S(1)} %arrange.1.w0), channel_id=1, source_target_pairs={{0,40},{1,249},{2,42},{3,251},{4,44},{5,253},{6,46},{7,255},{8,32}... | collective-permute-start | bytes 1769480 | tf_op jit(solution)/shard_map/ppermute | solution.py:290
  115.2 16.4 %collective-permute-start.27 = (f32[8,72,256]{2,1,0:T(8,128)S(1)}, f32[8,72,256]{2,1,0:T(8,128)S(1)}, u32[]{:S(2)}, u32[]{:S(2)}) collective-permute-start(f32[8,72,256]{2,1,0:T(8,128)S(1)} %arrange.1.w0), channel_id=1, source_target_pairs={{0,32},{1,225},{2,34},{3,227},{4,36},{5,229},{6,38},{7,231},{8,40}... | collective-permute-start | bytes 1769480 | tf_op jit(solution)/shard_map/ppermute | solution.py:290
  115.5 16.2 %collective-permute-start.26 = (f32[8,72,256]{2,1,0:T(8,128)S(1)}, f32[8,72,256]{2,1,0:T(8,128)S(1)}, u32[]{:S(2)}, u32[]{:S(2)}) collective-permute-start(f32[8,72,256]{2,1,0:T(8,128)S(1)} %arrange.1.w0), channel_id=1, source_target_pairs={{0,8},{1,25},{2,10},{3,27},{4,12},{5,29},{6,14},{7,31},{8,0},{9,17... | collective-permute-start | bytes 1769480 | tf_op jit(solution)/shard_map/ppermute | solution.py:290
  118.0 6.9 %collective-permute-start.25 = (f32[3,128,128]{2,1,0:T(8,128)S(1)}, f32[3,128,128]{2,1,0:T(8,128)S(1)}, u32[]{:S(2)}, u32[]{:S(2)}) collective-permute-start(f32[3,128,128]{2,1,0:T(8,128)S(1)} %factor.1.l0), channel_id=1, source_target_pairs={{0,6},{2,0},{4,2},{6,4},{1,7},{3,1},{5,3},{7,5},{8,14},{10,8},{12,... | collective-permute-start | bytes 589832 | tf_op jit(solution)/shard_map/ppermute | solution.py:270
  118.3 7.4 %collective-permute-start.24 = (f32[3,128,128]{2,1,0:T(8,128)S(1)}, f32[3,128,128]{2,1,0:T(8,128)S(1)}, u32[]{:S(2)}, u32[]{:S(2)}) collective-permute-start(f32[3,128,128]{2,1,0:T(8,128)S(1)} %factor.1.l0), channel_id=1, source_target_pairs={{0,4},{2,6},{4,0},{6,2},{1,5},{3,7},{5,1},{7,3},{8,12},{10,14},{12... | collective-permute-start | bytes 589832 | tf_op jit(solution)/shard_map/ppermute | solution.py:270
  124.9 6.8 %collective-permute-start.23 = (f32[3,128,128]{2,1,0:T(8,128)S(1)}, f32[3,128,128]{2,1,0:T(8,128)S(1)}, u32[]{:S(2)}, u32[]{:S(2)}) collective-permute-start(f32[3,128,128]{2,1,0:T(8,128)S(1)} %factor.1.l0), channel_id=1, source_target_pairs={{0,2},{2,4},{4,6},{6,0},{1,3},{3,5},{5,7},{7,1},{8,10},{10,12},{12... | collective-permute-start | bytes 589832 | tf_op jit(solution)/shard_map/ppermute | solution.py:270
  134.1 1.3 collective-permute-start.29
  135.4 4.8 %collective-permute-start.32 = (f32[8,256]{1,0:T(8,128)S(1)}, f32[8,256]{1,0:T(8,128)S(1)}, u32[]{:S(2)}, u32[]{:S(2)}) collective-permute-start(f32[8,256]{1,0:T(8,128)S(1)} %add.98.q0), channel_id=1, source_target_pairs={{0,6},{2,0},{4,2},{6,4},{1,7},{3,1},{5,3},{7,5},{8,14},{10,8},{12,... | collective-permute-start | bytes 24584 | tf_op jit(solution)/shard_map/ppermute | solution.py:270
  135.8 4.3 %collective-permute-start.31 = (f32[8,256]{1,0:T(8,128)S(1)}, f32[8,256]{1,0:T(8,128)S(1)}, u32[]{:S(2)}, u32[]{:S(2)}) collective-permute-start(f32[8,256]{1,0:T(8,128)S(1)} %add.98.q0), channel_id=1, source_target_pairs={{0,4},{2,6},{4,0},{6,2},{1,5},{3,7},{5,1},{7,3},{8,12},{10,14},{12... | collective-permute-start | bytes 24584 | tf_op jit(solution)/shard_map/ppermute | solution.py:270
  136.4 3.9 %collective-permute-start.30 = (f32[8,256]{1,0:T(8,128)S(1)}, f32[8,256]{1,0:T(8,128)S(1)}, u32[]{:S(2)}, u32[]{:S(2)}) collective-permute-start(f32[8,256]{1,0:T(8,128)S(1)} %add.98.q0), channel_id=1, source_target_pairs={{0,2},{2,4},{4,6},{6,0},{1,3},{3,5},{5,7},{7,1},{8,10},{10,12},{12... | collective-permute-start | bytes 24584 | tf_op jit(solution)/shard_map/ppermute | solution.py:270

commit v6 on v5

--- a/solution.py
+++ b/solution.py
@@ -128,19 +128,12 @@
     return call(stack_kernel, [((4,) + arrays[0].shape, F32)], (place, *arrays), name="stack")
 
 
-def factor_kernel(place, own_half, other_half, out, w):
+def eliminate(w, base, start, stop, write):
     n, nb, step = RANK, 64, 8
-    core, q = place[0], place[2]
-    for j in range(4):
-        w[pl.ds(pl.multiple_of(core * 128 + (q ^ j) * 32, 32), 32), :n] = own_half[j]
-        w[pl.ds(pl.multiple_of((1 - core) * 128 + (q ^ j) * 32, 32), 32), :n] = other_half[j]
-    row = lax.broadcasted_iota(jnp.int32, (n, n), 0)
-    col = lax.broadcasted_iota(jnp.int32, (n, n), 1)
-    w[:, n:] = jnp.where(row == col, 1.0, 0.0)
     sub = lax.broadcasted_iota(jnp.int32, (nb, 128), 0)
-    for o in range(0, n, nb):
+    for o in range(start, stop, nb):
         lo, hi = o // 128 * 128, n + (o + nb + 127) // 128 * 128
-        r = [w[o:o + nb, t:t + 128] for t in range(lo, hi, 128)]
+        r = [w[o - base:o - base + nb, t:t + 128] for t in range(lo, hi, 128)]
         d = jnp.ones((nb, 128), F32)
         for i in range(0, nb, step):
             c = o - lo + i
@@ -158,24 +151,55 @@
                 r = [a - f * b for a, b in zip(r, rows[j])]
         scale = lax.rsqrt(d)
         s = jnp.concatenate([a * scale for a in r], axis=1)
-        half, at = o // 128, o % 128
-        out[half, at:at + nb, :] = s[:, n - lo:n - lo + 128]
-        if half:
-            out[2, at:at + nb, :] = s[:, n - lo + 128:n - lo + 256]
+        write(o % 128, s[:, n - lo:])
         if o + nb < n:
             change = lax.dot_general(
                 s[:, :n - lo], s, TN, precision=lax.Precision.HIGHEST, preferred_element_type=F32
             )
-            w[o + nb:, lo:hi] = w[o + nb:, lo:hi] - change[o + nb - lo:]
+            w[o + nb - base:, lo:hi] = w[o + nb - base:, lo:hi] - change[o + nb - lo:]
+
+
+def factor_first_kernel(place, own_half, other_half, top, w):
+    n, core, q = RANK, place[0], place[2]
+    for j in range(4):
+        w[pl.ds(pl.multiple_of(core * 128 + (q ^ j) * 32, 32), 32), :n] = own_half[j]
+        w[pl.ds(pl.multiple_of((1 - core) * 128 + (q ^ j) * 32, 32), 32), :n] = other_half[j]
+    row = lax.broadcasted_iota(jnp.int32, (n, n), 0)
+    col = lax.broadcasted_iota(jnp.int32, (n, n), 1)
+    w[:, n:] = jnp.where(row == col, 1.0, 0.0)
+
+    def write(at, s):
+        top[at:at + s.shape[0], :] = s
+
+    eliminate(w, 0, 0, 128, write)
+
+
+def factor_second_kernel(place, top, rest, out, out_half, w):
+    w[...] = rest[128:, :]
+    out[0] = top[...]
+
+    def write(at, s):
+        out[1, at:at + s.shape[0], :] = s[:, :128]
+        out[2, at:at + s.shape[0], :] = s[:, 128:]
+
+    eliminate(w, 128, 128, 256, write)
+    out_half[...] = out[:, pl.ds(pl.multiple_of(place[0] * 64, 64), 64), :]
 
 
 def fill_inverse(inv, place, around):
-    for d, blocks in enumerate(around):
-        k = (place[1] - d) & 3
-        inv[k, :128, :128] = blocks[0]
-        inv[k, :128, 128:] = jnp.zeros((128, 128), F32)
-        inv[k, 128:, :128] = blocks[1]
-        inv[k, 128:, 128:] = blocks[2]
+    core, x = place[0], place[1]
+    inv[:, :128, 128:] = jnp.zeros((4, 128, 128), F32)
+
+    def fill(k, blocks, at, size):
+        for i, (row, col) in enumerate(((0, 0), (128, 0), (128, 128))):
+            inv[k, pl.ds(pl.multiple_of(row + at, 64), size), col:col + 128] = blocks[i]
+
+    own, near, other_near, far, other_far = around
+    fill(x, own, 0, 128)
+    fill((x + 2 * core - 1) & 3, near, 0, 128)
+    fill((x - 2 * core + 1) & 3, other_near, 0, 128)
+    fill((x + 2) & 3, far, core * 64, 64)
+    fill((x + 2) & 3, other_far, (1 - core) * 64, 64)
 
 
 def arrange_kernel(place, w0, w1, w2, w3, out):
@@ -184,9 +208,9 @@
             out[a * 4 + (place[3] ^ (j >> 1)) * 2 + (place[4] ^ (j & 1))] = pair[a]
 
 
-def right_kernel(place, w0, w1, w2, w3, l0, l1, l2, l3, right_s, right_n, squares, inv):
+def right_kernel(place, w0, w1, w2, w3, l0, l1, l2, l3, l4, right_s, right_n, squares, inv):
     q = place[2]
-    fill_inverse(inv, place, (l0, l1, l2, l3))
+    fill_inverse(inv, place, (l0, l1, l2, l3, l4))
     for j, w in enumerate((w0, w1, w2, w3)):
         p = q ^ j
         for k in range(2):
@@ -202,8 +226,8 @@
         squares[k:k + 1, :] = jnp.sum(r * r, axis=0, keepdims=True)
 
 
-def momentum_kernel(place, l0, l1, l2, l3, right_s, right_n, left, ms, gs, mn, gn, ortho, mom_s, mom_n, inv, s_out, n_out, sem):
-    fill_inverse(inv, place, (l0, l1, l2, l3))
+def momentum_kernel(place, l0, l1, l2, l3, l4, right_s, right_n, left, ms, gs, mn, gn, ortho, mom_s, mom_n, inv, s_out, n_out, sem):
+    fill_inverse(inv, place, (l0, l1, l2, l3, l4))
     copies = []
     for k in range(4):
         m, g, right, mom, new = (ms, gs, right_s, mom_s, s_out) if k < 2 else (mn, gn, right_n, mom_n, n_out)
@@ -263,7 +287,8 @@
         perm(lambda z, y, c: (far_z(z, c), y)),
         perm(lambda z, y, c: (far_z(z, c), y + 2)),
     ]
-    return near, far, perm(lambda z, y, c: (z + 4, y))
+    sides = [(i, i // 8 * 8 + (i % 8 + (2 if i % 2 == 0 else 6)) % 8) for i in range(256)]
+    return near, far, perm(lambda z, y, c: (z + 4, y)), sides
 
 
 def shift_x(value, d):
@@ -286,7 +311,7 @@
     a, b = zh // 2, zh % 2
     q = lax.axis_index("zl") * 2 + lax.axis_index("yl")
     place = jnp.stack([lax.axis_index("core"), lax.axis_index("x"), q, b, yh]).astype(jnp.int32)
-    near, far, across = partners()
+    near, far, across, sides = partners()
     send = lambda value, pairs: lax.ppermute(value, AXES, pairs)
     inputs = (mom_square, grad_square, basis_square, mom_narrow, grad_narrow, basis_narrow)
 
@@ -326,7 +351,7 @@
         [pltpu.VMEM((32, CHUNK, RANK), F32), pltpu.VMEM((128, RANK), F32)],
         name="back",
     )
-    got = [send(value, pairs) for value, pairs in zip(others[::-1], near[::-1])][::-1]
+    got = [send(value, pairs) for value, pairs in zip(others[::-1], near[::-1])]
     mine, *others = call(meet_kernel, [((2 * CHUNK + 32, RANK), F32)] * 4, (place, own, *got), name="meet")
     got = [send(value, pairs) for value, pairs in zip(others[::-1], far[::-1])][::-1]
     own = mine + got[0] + got[1] + got[2]
@@ -337,19 +362,26 @@
     (gram,) = stack(place, [gram] + [send(gram, pairs) for pairs in near])
     gram, got = lax.optimization_barrier((gram, got))
     other_gram = swap_core(gram)
-    (blocks,) = call(
-        factor_kernel,
-        [((3, 128, 128), F32)],
+    top, rest = call(
+        factor_first_kernel,
+        [((128, 128), F32), ((RANK, 2 * RANK), F32)],
         (place, gram, other_gram),
-        [pltpu.VMEM((RANK, 2 * RANK), F32)],
-        name="factor",
+        name="factor_first",
     )
     pair = jnp.where(a == 0, jnp.stack([own, got]), jnp.stack([got, own]))
     pairs = [pair] + [send(pair, p) for p in far]
-    blocks, pairs = lax.optimization_barrier((blocks, pairs))
+    top, rest, pairs = lax.optimization_barrier((top, rest, pairs))
     (quarter,) = call(arrange_kernel, [((8, CHUNK, RANK), F32)], (place, *pairs), name="arrange")
     quarters = [quarter] + [send(quarter, p) for p in near]
-    around = around_x(blocks)
+    blocks, half_blocks = call(
+        factor_second_kernel,
+        [((3, 128, 128), F32), ((3, 64, 128), F32)],
+        (place, top, rest),
+        [pltpu.VMEM((128, 2 * RANK), F32)],
+        name="factor_second",
+    )
+    beside, apart = send(blocks, sides), shift_x(half_blocks, 2)
+    around = blocks, beside, swap_core(beside), apart, swap_core(apart)
     inverse = pltpu.VMEM((4, RANK, RANK), F32)
     right_s, right_n, squares = call(
         right_kernel,

time: 144 us -> 140 us (0.972)
  waiting for transfers between devices: 56.1 us -> 49.5 us
  starting transfers between devices: 56.5 us -> 59.3 us
    ppermute x12 -> x10, waiting for transfers between devices: 22.5 us -> 10.3 us  [shift_x(): return lax.ppermute(value, 'x', [(i, (i + d) % 4) for i in range(4)])]
    ppermute x17 -> x18, waiting for transfers between devices: 28 us -> 32.6 us  [local(): send = lambda value, pairs: lax.ppermute(value, AXES, pairs)]
    ppermute x4 -> x6, starting transfers between devices: 4.78 us -> 7.33 us  [swap_core(): return lax.ppermute(value, 'core', [(0, 1), (1, 0)])]
    ppermute x4 -> x6, waiting for transfers between devices: 5.58 us -> 6.62 us  [swap_core(): return lax.ppermute(value, 'core', [(0, 1), (1, 0)])]
    pallas_call x10 -> x11, Pallas kernels: 29.3 us -> 29.8 us  [call(): pl.pallas_call(kernel, out_shape=[jax.ShapeDtypeStruct(s, d) for s, d in...]
    ppermute x17 -> x18, starting transfers between devices: 43.1 us -> 43.4 us  [local(): send = lambda value, pairs: lax.ppermute(value, AXES, pairs)]
    ppermute x12 -> x10, starting transfers between devices: 8.63 us -> 8.55 us  [shift_x(): return lax.ppermute(value, 'x', [(i, (i + d) % 4) for i in range(4)])]
  transfers between devices with their start and end apart: 33 -> 34, of which waited for: 21 -> 20; matrix products, arithmetic and copies ran while one was open for 0% -> 0% of each run, Pallas kernels for 11% -> 12%
where the time goes in v6:
time: 140 us
  starting transfers between devices  59.3 us (42%)
  waiting for transfers between devices  49.5 us (35%)
  Pallas kernels  29.8 us (21%)
    ppermute x18, starting transfers between devices, local(): send = lambda value, pairs: lax.ppermute(value, AXES, pairs)  43.4 us
    ppermute x18, waiting for transfers between devices, local(): send = lambda value, pairs: lax.ppermute(value, AXES, pairs)  32.6 us
    pallas_call x11, Pallas kernels, call(): pl.pallas_call(kernel, out_shape=[jax.ShapeDtypeStruct(s, d) for s, d in...  29.8 us
    ppermute x10, waiting for transfers between devices, shift_x(): return lax.ppermute(value, 'x', [(i, (i + d) % 4) for i in range(4)])  10.3 us
    ppermute x10, starting transfers between devices, shift_x(): return lax.ppermute(value, 'x', [(i, (i + d) % 4) for i in range(4)])  8.55 us
    ppermute x6, starting transfers between devices, swap_core(): return lax.ppermute(value, 'core', [(0, 1), (1, 0)])  7.33 us
    ppermute x6, waiting for transfers between devices, swap_core(): return lax.ppermute(value, 'core', [(0, 1), (1, 0)])  6.62 us
  transfers between devices with their start and end apart: 34, of which 20 were waited for; matrix products, arithmetic and copies ran while one was open for 0% of the time, Pallas kernels for 12%

profile of v6, /device:TPU:1, one launch (start us, length us, event | category | flops | bytes accessed | tf_op | source)
XLA Modules:
  0.0 140.2 jit_solution(16128105867564740677)
XLA Ops:
  0.7 0.1 stack.53.place
  0.7 4.7 %project.1 = (f32[4,4,32,256]{3,2,1,0:T(8,128)S(1)}, f32[4,4,32,256]{3,2,1,0:T(8,128)S(1)}) custom-call(s32[5]{0:T(128)S(1)} %stack.53.place, f32[2,256,1024]{2,1,0:T(8,128)} %ms.4, bf16[2,256,1024]{2,1,0:T(8,128)(2,1)} %gs.4, f32[2,1024,256]{2,1,0:T(8,128)} %qs.1, f32[2,256,128]{2,1,0:T(8,128)} %mn.4, bf16[2,256,128]{2,1,0:T(8,128)(2,1)} %gn.4, ...), custom_call_target="tpu_custom_call" | custom-call | tf_op jit(solution)/shard_map/project/pallas_call | solution.py:39
  5.4 3.3 %collective-permute-start = (f32[4,4,32,256]{3,2,1,0:T(8,128)S(1)}, f32[4,4,32,256]{3,2,1,0:T(8,128)S(1)}, u32[]{:S(2)}, u32[]{:S(2)}) collective-permute-start(f32[4,4,32,256]{3,2,1,0:T(8,128)S(1)} %get-tuple-element.61), channel_id=1, source_target_pairs={{0,1},{1,0},{2,3},{3,2},{4,5},{5,4},{6,7},{7,6},{8,9},{9,8},{10,11... | collective-permute-start | bytes 1572872 | tf_op jit(solution)/shard_map/ppermute | solution.py:306
  8.8 1.5 %collective-permute-done = f32[4,4,32,256]{3,2,1,0:T(8,128)S(1)} collective-permute-done((f32[4,4,32,256]{3,2,1,0:T(8,128)S(1)}, f32[4,4,32,256]{3,2,1,0:T(8,128)S(1)}, u32[]{:S(2)}, u32[]{:S(2)}) %collective-permute-start) | collective-permute-done | bytes 524320 | tf_op jit(solution)/shard_map/ppermute | solution.py:306
  10.3 0.1 add.77
  10.4 1.1 collective-permute-start.1
  11.5 0.3 collective-permute-start.2
  11.8 2.4 %collective-permute-start.3 = (f32[4,32,256]{2,1,0:T(8,128)S(1)}, f32[4,32,256]{2,1,0:T(8,128)S(1)}, u32[]{:S(2)}, u32[]{:S(2)}) collective-permute-start(f32[4,32,256]{2,1,0:T(8,128)S(1)} %get-tuple-element.64), channel_id=1, source_target_pairs={{0,6},{2,0},{4,2},{6,4},{1,7},{3,1},{5,3},{7,5},{8,14},{10,8},{12,... | collective-permute-start | bytes 393224 | tf_op jit(solution)/shard_map/ppermute | solution.py:295
  14.2 3.2 %prepare.1 = (bf16[2,1024,256]{2,1,0:T(8,128)(2,1)S(1)}, bf16[2,1024,256]{2,1,0:T(8,128)(2,1)S(1)}, bf16[2,128,256]{2,1,0:T(8,128)(2,1)S(1)}, bf16[2,128,256]{2,1,0:T(8,128)(2,1)S(1)}) custom-call(s32[5]{0:T(128)S(1)} %stack.53.place, f32[2,256,1024]{2,1,0:T(8,128)} %ms.4, bf16[2,256,1024]{2,1,0:T(8,128)(2,1)} %gs.4, f32[2,256,128]{2,1,0:T(8,128)} %mn.4, ...), custom_call_target="tpu_custom_call" | custom-call | tf_op jit(solution)/shard_map/prepare/pallas_call | solution.py:39
  17.4 2.8 %collective-permute-done.2 = f32[4,32,256]{2,1,0:T(8,128)S(1)} collective-permute-done((f32[4,32,256]{2,1,0:T(8,128)S(1)}, f32[4,32,256]{2,1,0:T(8,128)S(1)}, u32[]{:S(2)}, u32[]{:S(2)}) %collective-permute-start.2) | collective-permute-done | bytes 131104 | tf_op jit(solution)/shard_map/ppermute | solution.py:295
  20.3 0.3 collective-permute-start.6
  20.6 0.9 collective-permute-start.5
  21.5 0.8 collective-permute-start.4
  22.2 2.7 %collective-permute-done.6 = f32[4,32,256]{2,1,0:T(8,128)S(1)} collective-permute-done((f32[4,32,256]{2,1,0:T(8,128)S(1)}, f32[4,32,256]{2,1,0:T(8,128)S(1)}, u32[]{:S(2)}, u32[]{:S(2)}) %collective-permute-start.6) | collective-permute-done | bytes 131104 | tf_op jit(solution)/shard_map/ppermute | solution.py:295
  25.0 1.0 collective-permute-done.5
  26.0 3.6 %collective-permute-done.4 = f32[4,32,256]{2,1,0:T(8,128)S(1)} collective-permute-done((f32[4,32,256]{2,1,0:T(8,128)S(1)}, f32[4,32,256]{2,1,0:T(8,128)S(1)}, u32[]{:S(2)}, u32[]{:S(2)}) %collective-permute-start.4) | collective-permute-done | bytes 131104 | tf_op jit(solution)/shard_map/ppermute | solution.py:295
  29.6 1.4 collective-permute-start.7
  30.9 1.5 %collective-permute-done.7.other_half = f32[4,4,32,256]{3,2,1,0:T(8,128)S(1)} collective-permute-done((f32[4,4,32,256]{3,2,1,0:T(8,128)S(1)}, f32[4,4,32,256]{3,2,1,0:T(8,128)S(1)}, u32[]{:S(2)}, u32[]{:S(2)}) %collective-permute-start.7) | collective-permute-done | bytes 524320 | tf_op jit(solution)/shard_map/ppermute | solution.py:306
  32.5 1.9 %back.1 = (f32[4,256,256]{2,1,0:T(8,128)S(1)}, f32[608,256]{1,0:T(8,128)S(1)}, f32[608,256]{1,0:T(8,128)S(1)}, f32[608,256]{1,0:T(8,128)S(1)}, f32[608,256]{1,0:T(8,128)S(1)}) custom-call(s32[5]{0:T(128)S(1)} %stack.53.place, bf16[2,1024,256]{2,1,0:T(8,128)(2,1)S(1)} %get-tuple-element.73.high_s, bf16[2,1024,256]{2,1,0:T(8,128)(2,1)S(1)} %get-tuple-element.74.low_s, ...), custom_call_target="tpu_custom_call" | custom-call | tf_op jit(solution)/shard_map/back/pallas_call | solution.py:39
  34.4 8.1 %collective-permute-start.8 = (f32[608,256]{1,0:T(8,128)S(1)}, f32[608,256]{1,0:T(8,128)S(1)}, u32[]{:S(2)}, u32[]{:S(2)}) collective-permute-start(f32[608,256]{1,0:T(8,128)S(1)} %get-tuple-element.82), channel_id=1, source_target_pairs={{0,40},{1,249},{2,42},{3,251},{4,44},{5,253},{6,46},{7,255},{8,32}... | collective-permute-start | bytes 1867784 | tf_op jit(solution)/shard_map/ppermute | solution.py:315
  42.5 0.4 collective-permute-start.10
  42.9 7.3 %collective-permute-done.8.r0 = f32[608,256]{1,0:T(8,128)S(1)} collective-permute-done((f32[608,256]{1,0:T(8,128)S(1)}, f32[608,256]{1,0:T(8,128)S(1)}, u32[]{:S(2)}, u32[]{:S(2)}) %collective-permute-start.8) | collective-permute-done | bytes 622624 | tf_op jit(solution)/shard_map/ppermute | solution.py:315
  50.3 6.2 %collective-permute-done.9.r1 = f32[608,256]{1,0:T(8,128)S(1)} collective-permute-done((f32[608,256]{1,0:T(8,128)S(1)}, f32[608,256]{1,0:T(8,128)S(1)}, u32[]{:S(2)}, u32[]{:S(2)}) %collective-permute-start.9) | collective-permute-done | bytes 622624 | tf_op jit(solution)/shard_map/ppermute | solution.py:315
  56.4 0.4 collective-permute-done.10.r2
  56.8 0.7 meet.1
  57.5 0.6 collective-permute-start.11
  58.1 3.1 %collective-permute-start.12 = (f32[176,256]{1,0:T(8,128)S(1)}, f32[176,256]{1,0:T(8,128)S(1)}, u32[]{:S(2)}, u32[]{:S(2)}) collective-permute-start(f32[176,256]{1,0:T(8,128)S(1)} %get-tuple-element.87), channel_id=1, source_target_pairs={{0,64},{1,193},{2,66},{3,195},{4,68},{5,197},{6,70},{7,199},{8,72}... | collective-permute-start | bytes 540680 | tf_op jit(solution)/shard_map/ppermute | solution.py:315
  61.2 2.7 %collective-permute-start.13 = (f32[176,256]{1,0:T(8,128)S(1)}, f32[176,256]{1,0:T(8,128)S(1)}, u32[]{:S(2)}, u32[]{:S(2)}) collective-permute-start(f32[176,256]{1,0:T(8,128)S(1)} %get-tuple-element.88), channel_id=1, source_target_pairs={{0,80},{1,209},{2,82},{3,211},{4,84},{5,213},{6,86},{7,215},{8,88}... | collective-permute-start | bytes 540680 | tf_op jit(solution)/shard_map/ppermute | solution.py:315
  63.8 0.8 collective-permute-done.12
  64.6 6.4 %collective-permute-done.13 = f32[176,256]{1,0:T(8,128)S(1)} collective-permute-done((f32[176,256]{1,0:T(8,128)S(1)}, f32[176,256]{1,0:T(8,128)S(1)}, u32[]{:S(2)}, u32[]{:S(2)}) %collective-permute-start.13) | collective-permute-done | bytes 180256 | tf_op jit(solution)/shard_map/ppermute | solution.py:315
  71.1 5.1 %collective-permute-start.14 = (f32[104,256]{1,0:T(8,128)S(1)}, f32[104,256]{1,0:T(8,128)S(1)}, u32[]{:S(2)}, u32[]{:S(2)}) collective-permute-start(f32[104,256]{1,0:T(8,128)S(1)} %pad_maximum_fusion.1), channel_id=1, source_target_pairs={{0,128},{1,129},{2,130},{3,131},{4,132},{5,133},{6,134},{7,135},{8... | collective-permute-start | bytes 319496 | tf_op jit(solution)/shard_map/ppermute | solution.py:315
  76.2 3.2 %collective-permute-done.14 = f32[104,256]{1,0:T(8,128)S(1)} collective-permute-done((f32[104,256]{1,0:T(8,128)S(1)}, f32[104,256]{1,0:T(8,128)S(1)}, u32[]{:S(2)}, u32[]{:S(2)}) %collective-permute-start.14) | collective-permute-done | bytes 106528 | tf_op jit(solution)/shard_map/ppermute | solution.py:315
  79.5 5.4 %collective-permute-start.18 = (f32[72,256]{1,0:T(8,128)S(1)}, f32[72,256]{1,0:T(8,128)S(1)}, u32[]{:S(2)}, u32[]{:S(2)}) collective-permute-start(f32[72,256]{1,0:T(8,128)S(1)} %get-tuple-element.121), channel_id=1, source_target_pairs={{0,128},{1,129},{2,130},{3,131},{4,132},{5,133},{6,134},{7,135},{8... | collective-permute-start | bytes 221192 | tf_op jit(solution)/shard_map/ppermute | solution.py:315
  84.9 4.9 %collective-permute-start.17 = (f32[32,256]{1,0:T(8,128)S(1)}, f32[32,256]{1,0:T(8,128)S(1)}, u32[]{:S(2)}, u32[]{:S(2)}) collective-permute-start(f32[32,256]{1,0:T(8,128)S(1)} %slice.14.a0), channel_id=1, source_target_pairs={{0,40},{1,249},{2,42},{3,251},{4,44},{5,253},{6,46},{7,255},{8,32}... | collective-permute-start | bytes 98312 | tf_op jit(solution)/shard_map/ppermute | solution.py:315
  89.8 1.3 collective-permute-start.16
  91.1 0.5 collective-permute-done.17.a3
  91.7 2.1 %collective-permute-done.16.a2 = f32[32,256]{1,0:T(8,128)S(1)} collective-permute-done((f32[32,256]{1,0:T(8,128)S(1)}, f32[32,256]{1,0:T(8,128)S(1)}, u32[]{:S(2)}, u32[]{:S(2)}) %collective-permute-start.16) | collective-permute-done | bytes 32800 | tf_op jit(solution)/shard_map/ppermute | solution.py:315
  93.8 1.3 collective-permute-done.15.a1
  95.1 0.5 stack.63.own_half
  95.7 0.1 collective-permute-start.22
  95.8 2.1 %collective-permute-start.21 = (f32[2,72,256]{2,1,0:T(8,128)S(1)}, f32[2,72,256]{2,1,0:T(8,128)S(1)}, u32[]{:S(2)}, u32[]{:S(2)}) collective-permute-start(f32[2,72,256]{2,1,0:T(8,128)S(1)} %maximum_select_fusion.w0), channel_id=1, source_target_pairs={{0,64},{1,193},{2,66},{3,195},{4,68},{5,197},{6,70},{7,199},{8,72}... | collective-permute-start | bytes 442376 | tf_op jit(solution)/shard_map/ppermute | solution.py:315
  97.9 4.1 %collective-permute-start.20 = (f32[2,72,256]{2,1,0:T(8,128)S(1)}, f32[2,72,256]{2,1,0:T(8,128)S(1)}, u32[]{:S(2)}, u32[]{:S(2)}) collective-permute-start(f32[2,72,256]{2,1,0:T(8,128)S(1)} %maximum_select_fusion.w0), channel_id=1, source_target_pairs={{0,16},{1,17},{2,18},{3,19},{4,20},{5,21},{6,22},{7,23},{8,24},{9,... | collective-permute-start | bytes 442376 | tf_op jit(solution)/shard_map/ppermute | solution.py:315
  102.0 1.3 collective-permute-done.19.other_half
  103.4 5.2 %factor_first.1 = (f32[128,128]{1,0:T(8,128)S(1)}, f32[256,512]{1,0:T(8,128)S(1)}) custom-call(s32[5]{0:T(128)S(1)} %stack.53.place, f32[4,32,256]{2,1,0:T(8,128)S(1)} %stack.63.own_half, f32[4,32,256]{2,1,0:T(8,128)S(1)} %collective-permute-done.19.other_half), custom_call_target="tpu_custom_call" | custom-call | tf_op jit(solution)/shard_map/factor_first/pallas_call | solution.py:39
  108.6 0.0 collective-permute-done.20.w1
  108.7 0.6 arrange.1.w0
  109.3 0.0 copy-start.1
  109.3 1.2 collective-permute-start.29
  110.6 1.3 collective-permute-start.28
  111.8 2.6 %collective-permute-start.27 = (f32[8,72,256]{2,1,0:T(8,128)S(1)}, f32[8,72,256]{2,1,0:T(8,128)S(1)}, u32[]{:S(2)}, u32[]{:S(2)}) collective-permute-start(f32[8,72,256]{2,1,0:T(8,128)S(1)} %arrange.1.w0), channel_id=1, source_target_pairs={{0,8},{1,25},{2,10},{3,27},{4,12},{5,29},{6,14},{7,31},{8,0},{9,17... | collective-permute-start | bytes 1769480 | tf_op jit(solution)/shard_map/ppermute | solution.py:315
  114.5 4.4 %factor_second.1 = (f32[3,128,128]{2,1,0:T(8,128)S(1)}, f32[3,64,128]{2,1,0:T(8,128)S(1)}) custom-call(s32[5]{0:T(128)S(1)} %stack.53.place, f32[128,128]{1,0:T(8,128)S(1)} %get-tuple-element.93.top, f32[256,512]{1,0:T(8,128)S(1)} %get-tuple-element.94.rest), custom_call_target="tpu_custom_call" | custom-call | tf_op jit(solution)/shard_map/factor_second/pallas_call | solution.py:39
  118.9 0.4 collective-permute-start.23
  119.2 1.0 collective-permute-start.25
  120.3 4.2 %collective-permute-done.23.l1 = f32[3,128,128]{2,1,0:T(8,128)S(1)} collective-permute-done((f32[3,128,128]{2,1,0:T(8,128)S(1)}, f32[3,128,128]{2,1,0:T(8,128)S(1)}, u32[]{:S(2)}, u32[]{:S(2)}) %collective-permute-start.23) | collective-permute-done | bytes 196640 | tf_op jit(solution)/shard_map/ppermute | solution.py:315
  124.5 2.3 %collective-permute-start.24 = (f32[3,128,128]{2,1,0:T(8,128)S(1)}, f32[3,128,128]{2,1,0:T(8,128)S(1)}, u32[]{:S(2)}, u32[]{:S(2)}) collective-permute-start(f32[3,128,128]{2,1,0:T(8,128)S(1)} %collective-permute-done.23.l1), channel_id=1, source_target_pairs={{0,1},{1,0},{2,3},{3,2},{4,5},{5,4},{6,7},{7,6},{8,9},{9,8},{10,11... | collective-permute-start | bytes 589832 | tf_op jit(solution)/shard_map/ppermute | solution.py:306
  126.8 1.3 collective-permute-done.26.l4
  128.1 2.4 %right.1 = (f32[2,1024,256]{2,1,0:T(8,128)S(1)}, f32[2,128,256]{2,1,0:T(8,128)S(1)}, f32[8,256]{1,0:T(8,128)S(1)}) custom-call(s32[5]{0:T(128)S(1)} %stack.53.place, f32[8,72,256]{2,1,0:T(8,128)S(1)} %arrange.1.w0, f32[8,72,256]{2,1,0:T(8,128)S(1)} %collective-permute-done.27.w1, f32[8,72,256]{2,1,0:T(8,128)S(1)} %collective-permute-done.28.w2, ...), custom_call_target="tpu_custom_call" | custom-call | tf_op jit(solution)/shard_map/right/pallas_call | solution.py:39
  130.5 0.4 collective-permute-start.30
  130.8 0.9 collective-permute-done.30
  131.7 1.2 collective-permute-start.33
  132.9 0.6 collective-permute-start.31
  133.5 3.2 %momentum.1 = (f32[4,256,256]{2,1,0:T(8,128)S(1)}, f32[2,256,1024]{2,1,0:T(8,128)}, f32[2,256,128]{2,1,0:T(8,128)}) custom-call(s32[5]{0:T(128)S(1)} %stack.53.place, f32[3,128,128]{2,1,0:T(8,128)S(1)} %get-tuple-element.95.l0, f32[3,128,128]{2,1,0:T(8,128)S(1)} %collective-permute-done.23.l1, f32[3,128,128]{2,1,0:T(8,128)S(1)} %collective-permute-done.24.l2, ...), custom_call_target="tpu_custom_call" | custom-call | tf_op jit(solution)/shard_map/momentum/pallas_call | solution.py:39
  136.7 0.2 collective-permute-done.32.q2
  137.0 3.0 %update.1 = (bf16[2,256,1024]{2,1,0:T(8,128)(2,1)}, f32[2,1024,256]{2,1,0:T(8,128)}, bf16[2,256,128]{2,1,0:T(8,128)(2,1)}, f32[2,128,256]{2,1,0:T(8,128)}) custom-call(s32[5]{0:T(128)S(1)} %stack.53.place, f32[8,256]{1,0:T(8,128)S(1)} %add.98.q0, f32[8,256]{1,0:T(8,128)S(1)} %collective-permute-done.31.q1, f32[8,256]{1,0:T(8,128)S(1)} %collective-permute-done.32.q2, ...), custom_call_target="tpu_custom_call" | custom-call | tf_op jit(solution)/shard_map/update/pallas_call | solution.py:39
  (37 shorter events, 0.3 us)
Async XLA Ops:
  5.4 4.9 %collective-permute-start = (f32[4,4,32,256]{3,2,1,0:T(8,128)S(1)}, f32[4,4,32,256]{3,2,1,0:T(8,128)S(1)}, u32[]{:S(2)}, u32[]{:S(2)}) collective-permute-start(f32[4,4,32,256]{3,2,1,0:T(8,128)S(1)} %get-tuple-element.61), channel_id=1, source_target_pairs={{0,1},{1,0},{2,3},{3,2},{4,5},{5,4},{6,7},{7,6},{8,9},{9,8},{10,11... | collective-permute-start | bytes 1572872 | tf_op jit(solution)/shard_map/ppermute | solution.py:306
  10.4 7.0 %collective-permute-start.1 = (f32[4,32,256]{2,1,0:T(8,128)S(1)}, f32[4,32,256]{2,1,0:T(8,128)S(1)}, u32[]{:S(2)}, u32[]{:S(2)}) collective-permute-start(f32[4,32,256]{2,1,0:T(8,128)S(1)} %get-tuple-element.62), channel_id=1, source_target_pairs={{0,4},{2,6},{4,0},{6,2},{1,5},{3,7},{5,1},{7,3},{8,12},{10,14},{12... | collective-permute-start | bytes 393224 | tf_op jit(solution)/shard_map/ppermute | solution.py:295
  11.5 8.7 %collective-permute-start.2 = (f32[4,32,256]{2,1,0:T(8,128)S(1)}, f32[4,32,256]{2,1,0:T(8,128)S(1)}, u32[]{:S(2)}, u32[]{:S(2)}) collective-permute-start(f32[4,32,256]{2,1,0:T(8,128)S(1)} %get-tuple-element.63), channel_id=1, source_target_pairs={{0,2},{2,4},{4,6},{6,0},{1,3},{3,5},{5,7},{7,1},{8,10},{10,12},{12... | collective-permute-start | bytes 393224 | tf_op jit(solution)/shard_map/ppermute | solution.py:295
  11.8 8.4 %collective-permute-start.3 = (f32[4,32,256]{2,1,0:T(8,128)S(1)}, f32[4,32,256]{2,1,0:T(8,128)S(1)}, u32[]{:S(2)}, u32[]{:S(2)}) collective-permute-start(f32[4,32,256]{2,1,0:T(8,128)S(1)} %get-tuple-element.64), channel_id=1, source_target_pairs={{0,6},{2,0},{4,2},{6,4},{1,7},{3,1},{5,3},{7,5},{8,14},{10,8},{12,... | collective-permute-start | bytes 393224 | tf_op jit(solution)/shard_map/ppermute | solution.py:295
  20.3 4.7 %collective-permute-start.6 = (f32[4,32,256]{2,1,0:T(8,128)S(1)}, f32[4,32,256]{2,1,0:T(8,128)S(1)}, u32[]{:S(2)}, u32[]{:S(2)}) collective-permute-start(f32[4,32,256]{2,1,0:T(8,128)S(1)} %add_add_fusion.1), channel_id=1, source_target_pairs={{0,6},{2,0},{4,2},{6,4},{1,7},{3,1},{5,3},{7,5},{8,14},{10,8},{12,... | collective-permute-start | bytes 393224 | tf_op jit(solution)/shard_map/ppermute | solution.py:295
  20.6 5.4 %collective-permute-start.5 = (f32[4,32,256]{2,1,0:T(8,128)S(1)}, f32[4,32,256]{2,1,0:T(8,128)S(1)}, u32[]{:S(2)}, u32[]{:S(2)}) collective-permute-start(f32[4,32,256]{2,1,0:T(8,128)S(1)} %add_add_fusion.1), channel_id=1, source_target_pairs={{0,4},{2,6},{4,0},{6,2},{1,5},{3,7},{5,1},{7,3},{8,12},{10,14},{12... | collective-permute-start | bytes 393224 | tf_op jit(solution)/shard_map/ppermute | solution.py:295
  21.5 8.0 %collective-permute-start.4 = (f32[4,32,256]{2,1,0:T(8,128)S(1)}, f32[4,32,256]{2,1,0:T(8,128)S(1)}, u32[]{:S(2)}, u32[]{:S(2)}) collective-permute-start(f32[4,32,256]{2,1,0:T(8,128)S(1)} %add_add_fusion.1), channel_id=1, source_target_pairs={{0,2},{2,4},{4,6},{6,0},{1,3},{3,5},{5,7},{7,1},{8,10},{10,12},{12... | collective-permute-start | bytes 393224 | tf_op jit(solution)/shard_map/ppermute | solution.py:295
  29.6 2.9 %collective-permute-start.7 = (f32[4,4,32,256]{3,2,1,0:T(8,128)S(1)}, f32[4,4,32,256]{3,2,1,0:T(8,128)S(1)}, u32[]{:S(2)}, u32[]{:S(2)}) collective-permute-start(f32[4,4,32,256]{3,2,1,0:T(8,128)S(1)} %pad_maximum_fusion.own_half), channel_id=1, source_target_pairs={{0,1},{1,0},{2,3},{3,2},{4,5},{5,4},{6,7},{7,6},{8,9},{9,8},{10,11... | collective-permute-start | bytes 1572872 | tf_op jit(solution)/shard_map/ppermute | solution.py:306
  34.4 15.8 %collective-permute-start.8 = (f32[608,256]{1,0:T(8,128)S(1)}, f32[608,256]{1,0:T(8,128)S(1)}, u32[]{:S(2)}, u32[]{:S(2)}) collective-permute-start(f32[608,256]{1,0:T(8,128)S(1)} %get-tuple-element.82), channel_id=1, source_target_pairs={{0,40},{1,249},{2,42},{3,251},{4,44},{5,253},{6,46},{7,255},{8,32}... | collective-permute-start | bytes 1867784 | tf_op jit(solution)/shard_map/ppermute | solution.py:315
  42.5 13.9 %collective-permute-start.9 = (f32[608,256]{1,0:T(8,128)S(1)}, f32[608,256]{1,0:T(8,128)S(1)}, u32[]{:S(2)}, u32[]{:S(2)}) collective-permute-start(f32[608,256]{1,0:T(8,128)S(1)} %get-tuple-element.83), channel_id=1, source_target_pairs={{0,32},{1,225},{2,34},{3,227},{4,36},{5,229},{6,38},{7,231},{8,40}... | collective-permute-start | bytes 1867784 | tf_op jit(solution)/shard_map/ppermute | solution.py:315
  42.5 14.3 %collective-permute-start.10 = (f32[608,256]{1,0:T(8,128)S(1)}, f32[608,256]{1,0:T(8,128)S(1)}, u32[]{:S(2)}, u32[]{:S(2)}) collective-permute-start(f32[608,256]{1,0:T(8,128)S(1)} %get-tuple-element.84), channel_id=1, source_target_pairs={{0,8},{1,25},{2,10},{3,27},{4,12},{5,29},{6,14},{7,31},{8,0},{9,17... | collective-permute-start | bytes 1867784 | tf_op jit(solution)/shard_map/ppermute | solution.py:315
  57.5 6.4 %collective-permute-start.11 = (f32[176,256]{1,0:T(8,128)S(1)}, f32[176,256]{1,0:T(8,128)S(1)}, u32[]{:S(2)}, u32[]{:S(2)}) collective-permute-start(f32[176,256]{1,0:T(8,128)S(1)} %get-tuple-element.86), channel_id=1, source_target_pairs={{0,16},{1,17},{2,18},{3,19},{4,20},{5,21},{6,22},{7,23},{8,24},{9,... | collective-permute-start | bytes 540680 | tf_op jit(solution)/shard_map/ppermute | solution.py:315
  58.1 6.6 %collective-permute-start.12 = (f32[176,256]{1,0:T(8,128)S(1)}, f32[176,256]{1,0:T(8,128)S(1)}, u32[]{:S(2)}, u32[]{:S(2)}) collective-permute-start(f32[176,256]{1,0:T(8,128)S(1)} %get-tuple-element.87), channel_id=1, source_target_pairs={{0,64},{1,193},{2,66},{3,195},{4,68},{5,197},{6,70},{7,199},{8,72}... | collective-permute-start | bytes 540680 | tf_op jit(solution)/shard_map/ppermute | solution.py:315
  61.2 9.8 %collective-permute-start.13 = (f32[176,256]{1,0:T(8,128)S(1)}, f32[176,256]{1,0:T(8,128)S(1)}, u32[]{:S(2)}, u32[]{:S(2)}) collective-permute-start(f32[176,256]{1,0:T(8,128)S(1)} %get-tuple-element.88), channel_id=1, source_target_pairs={{0,80},{1,209},{2,82},{3,211},{4,84},{5,213},{6,86},{7,215},{8,88}... | collective-permute-start | bytes 540680 | tf_op jit(solution)/shard_map/ppermute | solution.py:315
  71.1 8.4 %collective-permute-start.14 = (f32[104,256]{1,0:T(8,128)S(1)}, f32[104,256]{1,0:T(8,128)S(1)}, u32[]{:S(2)}, u32[]{:S(2)}) collective-permute-start(f32[104,256]{1,0:T(8,128)S(1)} %pad_maximum_fusion.1), channel_id=1, source_target_pairs={{0,128},{1,129},{2,130},{3,131},{4,132},{5,133},{6,134},{7,135},{8... | collective-permute-start | bytes 319496 | tf_op jit(solution)/shard_map/ppermute | solution.py:315
  79.5 16.1 %collective-permute-start.18 = (f32[72,256]{1,0:T(8,128)S(1)}, f32[72,256]{1,0:T(8,128)S(1)}, u32[]{:S(2)}, u32[]{:S(2)}) collective-permute-start(f32[72,256]{1,0:T(8,128)S(1)} %get-tuple-element.121), channel_id=1, source_target_pairs={{0,128},{1,129},{2,130},{3,131},{4,132},{5,133},{6,134},{7,135},{8... | collective-permute-start | bytes 221192 | tf_op jit(solution)/shard_map/ppermute | solution.py:315
  84.9 6.8 %collective-permute-start.17 = (f32[32,256]{1,0:T(8,128)S(1)}, f32[32,256]{1,0:T(8,128)S(1)}, u32[]{:S(2)}, u32[]{:S(2)}) collective-permute-start(f32[32,256]{1,0:T(8,128)S(1)} %slice.14.a0), channel_id=1, source_target_pairs={{0,40},{1,249},{2,42},{3,251},{4,44},{5,253},{6,46},{7,255},{8,32}... | collective-permute-start | bytes 98312 | tf_op jit(solution)/shard_map/ppermute | solution.py:315
  89.8 4.0 %collective-permute-start.16 = (f32[32,256]{1,0:T(8,128)S(1)}, f32[32,256]{1,0:T(8,128)S(1)}, u32[]{:S(2)}, u32[]{:S(2)}) collective-permute-start(f32[32,256]{1,0:T(8,128)S(1)} %slice.14.a0), channel_id=1, source_target_pairs={{0,32},{1,225},{2,34},{3,227},{4,36},{5,229},{6,38},{7,231},{8,40}... | collective-permute-start | bytes 98312 | tf_op jit(solution)/shard_map/ppermute | solution.py:315
  91.1 4.0 %collective-permute-start.15 = (f32[32,256]{1,0:T(8,128)S(1)}, f32[32,256]{1,0:T(8,128)S(1)}, u32[]{:S(2)}, u32[]{:S(2)}) collective-permute-start(f32[32,256]{1,0:T(8,128)S(1)} %slice.14.a0), channel_id=1, source_target_pairs={{0,8},{1,25},{2,10},{3,27},{4,12},{5,29},{6,14},{7,31},{8,0},{9,17... | collective-permute-start | bytes 98312 | tf_op jit(solution)/shard_map/ppermute | solution.py:315
  95.7 12.9 %collective-permute-start.22 = (f32[2,72,256]{2,1,0:T(8,128)S(1)}, f32[2,72,256]{2,1,0:T(8,128)S(1)}, u32[]{:S(2)}, u32[]{:S(2)}) collective-permute-start(f32[2,72,256]{2,1,0:T(8,128)S(1)} %maximum_select_fusion.w0), channel_id=1, source_target_pairs={{0,80},{1,209},{2,82},{3,211},{4,84},{5,213},{6,86},{7,215},{8,88}... | collective-permute-start | bytes 442376 | tf_op jit(solution)/shard_map/ppermute | solution.py:315
  95.8 12.8 %collective-permute-start.21 = (f32[2,72,256]{2,1,0:T(8,128)S(1)}, f32[2,72,256]{2,1,0:T(8,128)S(1)}, u32[]{:S(2)}, u32[]{:S(2)}) collective-permute-start(f32[2,72,256]{2,1,0:T(8,128)S(1)} %maximum_select_fusion.w0), channel_id=1, source_target_pairs={{0,64},{1,193},{2,66},{3,195},{4,68},{5,197},{6,70},{7,199},{8,72}... | collective-permute-start | bytes 442376 | tf_op jit(solution)/shard_map/ppermute | solution.py:315
  97.9 10.8 %collective-permute-start.20 = (f32[2,72,256]{2,1,0:T(8,128)S(1)}, f32[2,72,256]{2,1,0:T(8,128)S(1)}, u32[]{:S(2)}, u32[]{:S(2)}) collective-permute-start(f32[2,72,256]{2,1,0:T(8,128)S(1)} %maximum_select_fusion.w0), channel_id=1, source_target_pairs={{0,16},{1,17},{2,18},{3,19},{4,20},{5,21},{6,22},{7,23},{8,24},{9,... | collective-permute-start | bytes 442376 | tf_op jit(solution)/shard_map/ppermute | solution.py:315
  102.0 1.3 collective-permute-start.19
  109.3 24.3 %copy-start = (f32[2,256,1024]{2,1,0:T(8,128)S(1)}, f32[2,256,1024]{2,1,0:T(8,128)}, u32[]{:S(2)}) copy-start(f32[2,256,1024]{2,1,0:T(8,128)} %ms.4) | copy-start | bytes 6291460
  109.3 24.3 %copy-start.1 = (bf16[2,256,1024]{2,1,0:T(8,128)(2,1)S(1)}, bf16[2,256,1024]{2,1,0:T(8,128)(2,1)}, u32[]{:S(2)}) copy-start(bf16[2,256,1024]{2,1,0:T(8,128)(2,1)} %gs.4) | copy-start | bytes 3145732
  109.3 24.3 %copy-start.2 = (f32[2,256,128]{2,1,0:T(8,128)S(1)}, f32[2,256,128]{2,1,0:T(8,128)}, u32[]{:S(2)}) copy-start(f32[2,256,128]{2,1,0:T(8,128)} %mn.4) | copy-start | bytes 786436
  109.3 24.2 %copy-start.3 = (bf16[2,256,128]{2,1,0:T(8,128)(2,1)S(1)}, bf16[2,256,128]{2,1,0:T(8,128)(2,1)}, u32[]{:S(2)}) copy-start(bf16[2,256,128]{2,1,0:T(8,128)(2,1)} %gn.4) | copy-start | bytes 393220
  109.3 18.8 %collective-permute-start.29 = (f32[8,72,256]{2,1,0:T(8,128)S(1)}, f32[8,72,256]{2,1,0:T(8,128)S(1)}, u32[]{:S(2)}, u32[]{:S(2)}) collective-permute-start(f32[8,72,256]{2,1,0:T(8,128)S(1)} %arrange.1.w0), channel_id=1, source_target_pairs={{0,40},{1,249},{2,42},{3,251},{4,44},{5,253},{6,46},{7,255},{8,32}... | collective-permute-start | bytes 1769480 | tf_op jit(solution)/shard_map/ppermute | solution.py:315
  110.6 17.5 %collective-permute-start.28 = (f32[8,72,256]{2,1,0:T(8,128)S(1)}, f32[8,72,256]{2,1,0:T(8,128)S(1)}, u32[]{:S(2)}, u32[]{:S(2)}) collective-permute-start(f32[8,72,256]{2,1,0:T(8,128)S(1)} %arrange.1.w0), channel_id=1, source_target_pairs={{0,32},{1,225},{2,34},{3,227},{4,36},{5,229},{6,38},{7,231},{8,40}... | collective-permute-start | bytes 1769480 | tf_op jit(solution)/shard_map/ppermute | solution.py:315
  111.8 16.2 %collective-permute-start.27 = (f32[8,72,256]{2,1,0:T(8,128)S(1)}, f32[8,72,256]{2,1,0:T(8,128)S(1)}, u32[]{:S(2)}, u32[]{:S(2)}) collective-permute-start(f32[8,72,256]{2,1,0:T(8,128)S(1)} %arrange.1.w0), channel_id=1, source_target_pairs={{0,8},{1,25},{2,10},{3,27},{4,12},{5,29},{6,14},{7,31},{8,0},{9,17... | collective-permute-start | bytes 1769480 | tf_op jit(solution)/shard_map/ppermute | solution.py:315
  118.9 5.6 %collective-permute-start.23 = (f32[3,128,128]{2,1,0:T(8,128)S(1)}, f32[3,128,128]{2,1,0:T(8,128)S(1)}, u32[]{:S(2)}, u32[]{:S(2)}) collective-permute-start(f32[3,128,128]{2,1,0:T(8,128)S(1)} %get-tuple-element.95.l0), channel_id=1, source_target_pairs={{0,2},{1,7},{2,4},{3,1},{4,6},{5,3},{6,0},{7,5},{8,10},{9,15},{10,... | collective-permute-start | bytes 589832 | tf_op jit(solution)/shard_map/ppermute | solution.py:315
  119.2 7.5 %collective-permute-start.25 = (f32[3,64,128]{2,1,0:T(8,128)S(1)}, f32[3,64,128]{2,1,0:T(8,128)S(1)}, u32[]{:S(2)}, u32[]{:S(2)}) collective-permute-start(f32[3,64,128]{2,1,0:T(8,128)S(1)} %get-tuple-element.96), channel_id=1, source_target_pairs={{0,4},{2,6},{4,0},{6,2},{1,5},{3,7},{5,1},{7,3},{8,12},{10,14},{12... | collective-permute-start | bytes 294920 | tf_op jit(solution)/shard_map/ppermute | solution.py:295
  124.5 3.6 %collective-permute-start.24 = (f32[3,128,128]{2,1,0:T(8,128)S(1)}, f32[3,128,128]{2,1,0:T(8,128)S(1)}, u32[]{:S(2)}, u32[]{:S(2)}) collective-permute-start(f32[3,128,128]{2,1,0:T(8,128)S(1)} %collective-permute-done.23.l1), channel_id=1, source_target_pairs={{0,1},{1,0},{2,3},{3,2},{4,5},{5,4},{6,7},{7,6},{8,9},{9,8},{10,11... | collective-permute-start | bytes 589832 | tf_op jit(solution)/shard_map/ppermute | solution.py:306
  126.8 1.3 collective-permute-start.26
  130.5 1.3 collective-permute-start.30
  131.7 5.0 %collective-permute-start.33 = (f32[8,256]{1,0:T(8,128)S(1)}, f32[8,256]{1,0:T(8,128)S(1)}, u32[]{:S(2)}, u32[]{:S(2)}) collective-permute-start(f32[8,256]{1,0:T(8,128)S(1)} %add.98.q0), channel_id=1, source_target_pairs={{0,6},{2,0},{4,2},{6,4},{1,7},{3,1},{5,3},{7,5},{8,14},{10,8},{12,... | collective-permute-start | bytes 24584 | tf_op jit(solution)/shard_map/ppermute | solution.py:295
  132.9 4.0 %collective-permute-start.32 = (f32[8,256]{1,0:T(8,128)S(1)}, f32[8,256]{1,0:T(8,128)S(1)}, u32[]{:S(2)}, u32[]{:S(2)}) collective-permute-start(f32[8,256]{1,0:T(8,128)S(1)} %add.98.q0), channel_id=1, source_target_pairs={{0,4},{2,6},{4,0},{6,2},{1,5},{3,7},{5,1},{7,3},{8,12},{10,14},{12... | collective-permute-start | bytes 24584 | tf_op jit(solution)/shard_map/ppermute | solution.py:295
  132.9 4.0 %collective-permute-start.31 = (f32[8,256]{1,0:T(8,128)S(1)}, f32[8,256]{1,0:T(8,128)S(1)}, u32[]{:S(2)}, u32[]{:S(2)}) collective-permute-start(f32[8,256]{1,0:T(8,128)S(1)} %add.98.q0), channel_id=1, source_target_pairs={{0,2},{2,4},{4,6},{6,0},{1,3},{3,5},{5,7},{7,1},{8,10},{10,12},{12... | collective-permute-start | bytes 24584 | tf_op jit(solution)/shard_map/ppermute | solution.py:295
